TPU v7x, 512 devices: a whole 4x4x16 slice. The times are simulated.
512 devices in a mesh: gy: 16 (over x, y), gx: 32 (over z, core).
Axes of the slice: x: 4, y: 4, z: 16, core: 2. Of those that a mesh axis runs over, the one named last changes fastest.
Arguments:
- cost_volume: int32 [256, 512, 256], P('gy', 'gx'), may hold values from 0 to 64
- left_image: float32 [256, 512], P('gy', 'gx'), may hold values from -6 to 6
- p_small: int32 [4], replicated, may hold values from 4 to 16
- p_large: int32 [4], replicated, may hold values from 32 to 128
Outputs:
- aggregated: float32 [256, 512, 256], P('gy', 'gx')
Inputs may be any that keep to these rules, and one draw needn't show every extreme that they name: `p_small`: every small penalty is below every large penalty.
All inputs are finite; a program needn't handle non-finite values.
Results may differ from a plain program's by a relative error of at most 0.00002.
Values sent between devices are 32-bit elements; how exact they have to be, the bound alone decides.
No kernel may reach another device: no remote copies, remote signals or barrier semaphores. Data moves between devices by JAX's collectives and lax.ppermute only.
A program may use at most 64 MiB of HBM per device.

v0:
```python
from functools import partial

import jax
import jax.numpy as jnp
from jax import lax
from jax.sharding import PartitionSpec as P

FAR = 1e30
GRADIENT_GAIN = 4.0
OUT_SCALE = 1.0 / 256.0


def shifted(shard, axis, by):
    length = lax.axis_size(axis)
    pairs = [(i, i + by) for i in range(length) if 0 <= i + by < length]
    return lax.ppermute(shard, axis, pairs)


def padded_2(shard, sides, width):
    edges = {}
    for axis, dim in sides:
        size, length = (lax.axis_size(axis), shard.shape[dim])
        up = [(i, (i + 1) % size) for i in range(size - 1)]
        last = lax.slice_in_dim(shard, length - width, length, axis=dim)
        first = lax.slice_in_dim(shard, 0, width, axis=dim)
        edges[dim] = (
            lax.ppermute(last, axis, up),
            lax.ppermute(first, axis, [(b, a) for a, b in up]),
        )
    done = []
    for _, dim in sides:
        low, high = edges[dim]
        around = [(width, width) if d in done else (0, 0) for d in range(shard.ndim)]
        shard = jnp.concatenate([jnp.pad(low, around), shard, jnp.pad(high, around)], axis=dim)
        done.append(dim)
    return shard


def advance(previous, inputs, penalty_one):
    cost_line, large_line = inputs
    lowest = jnp.min(previous, axis=-1, keepdims=True)
    padded = jnp.pad(previous, ((0, 0), (1, 1)), constant_values=FAR)
    neighbour = jnp.minimum(padded[:, :-2], padded[:, 2:]) + penalty_one
    chosen = jnp.minimum(jnp.minimum(previous, neighbour), lowest + large_line[:, None])
    updated = cost_line.astype(jnp.float32) + chosen - lowest
    return (updated, updated)


def sweep(cost_lines, large_lines, penalty_one, start, backward):
    boundary, path_part = lax.scan(
        partial(advance, penalty_one=penalty_one),
        start,
        (cost_lines, large_lines),
        reverse=backward,
    )
    return (path_part, boundary)


def adaptive(penalty_one, penalty_two, step_diff):
    return penalty_one + (penalty_two - penalty_one) / (1.0 + GRADIENT_GAIN * jnp.abs(step_diff))


def send_right(message):
    return shifted(message, "gx", 1)


def send_left(message):
    return shifted(message, "gx", -1)


def send_down(message):
    return shifted(message, "gy", 1)


def send_up(message):
    return shifted(message, "gy", -1)


def run_lane(
    step_index, running, incoming, cost_lines, large_lines, penalty_one, position, pieces, backward
):
    span_width = cost_lines.shape[1] // pieces
    block_id = step_index - position
    active = jnp.logical_and(block_id >= 0, block_id < pieces)
    offset = jnp.clip(block_id, 0, pieces - 1) * span_width

    def process(running):
        cost_part = lax.dynamic_slice_in_dim(cost_lines, offset, span_width, 1)
        large_part = lax.dynamic_slice_in_dim(large_lines, offset, span_width, 1)
        path_part, boundary = sweep(cost_part, large_part, penalty_one, incoming, backward)
        current = lax.dynamic_slice_in_dim(running, offset, span_width, 1)
        return (lax.dynamic_update_slice_in_dim(running, current + path_part, offset, 1), boundary)

    def passing(running):
        return (running, jnp.zeros_like(incoming))

    return lax.cond(active, process, passing, running)


def on_device(cost_volume, left_image, p_small, p_large):
    tile_rows, tile_cols, disparities = cost_volume.shape
    pieces = 2
    padded = padded_2(left_image, (("gy", 0), ("gx", 1)), 1)
    middle = padded[1:-1, 1:-1]
    small_pens = p_small.astype(jnp.float32)
    large_pens = p_large.astype(jnp.float32)
    plain_right = adaptive(small_pens[0], large_pens[0], middle - padded[1:-1, :-2])
    plain_left = adaptive(small_pens[1], large_pens[1], middle - padded[1:-1, 2:])
    penalty_down = adaptive(small_pens[2], large_pens[2], middle - padded[:-2, 1:-1])
    penalty_up = adaptive(small_pens[3], large_pens[3], middle - padded[2:, 1:-1])
    count_x = lax.axis_size("gx")
    count_y = lax.axis_size("gy")
    penalty_right = plain_right.T
    penalty_left = plain_left.T
    crossed = jnp.transpose(cost_volume, (1, 0, 2))
    index_x = lax.axis_index("gx")
    index_y = lax.axis_index("gy")
    start_rows = jnp.zeros((tile_rows // pieces, disparities), jnp.float32)
    start_cols = jnp.zeros((tile_cols // pieces, disparities), jnp.float32)
    across = jnp.zeros((tile_cols, tile_rows, disparities), jnp.float32)
    down_total = jnp.zeros((tile_rows, tile_cols, disparities), jnp.float32)

    def horizontal(step_index, across, from_left, from_right):
        across, out_right = run_lane(
            step_index,
            across,
            from_left,
            crossed,
            penalty_right,
            small_pens[0],
            index_x,
            pieces,
            False,
        )
        across, out_left = run_lane(
            step_index,
            across,
            from_right,
            crossed,
            penalty_left,
            small_pens[1],
            count_x - 1 - index_x,
            pieces,
            True,
        )
        return (across, send_right(out_right), send_left(out_left))

    def vertical(step_index, down_total, from_above, from_below):
        down_total, out_down = run_lane(
            step_index,
            down_total,
            from_above,
            cost_volume,
            penalty_down,
            small_pens[2],
            index_y,
            pieces,
            False,
        )
        down_total, out_up = run_lane(
            step_index,
            down_total,
            from_below,
            cost_volume,
            penalty_up,
            small_pens[3],
            count_y - 1 - index_y,
            pieces,
            True,
        )
        return (down_total, send_down(out_down), send_up(out_up))

    def row_paths(step_index, carried):
        return horizontal(step_index, carried[0], carried[1], carried[2])

    def column_paths(step_index, carried):
        return vertical(step_index, carried[0], carried[1], carried[2])

    across = lax.fori_loop(0, count_x + pieces - 1, row_paths, (across, start_rows, start_rows))[0]
    down_total = lax.fori_loop(
        0, count_y + pieces - 1, column_paths, (down_total, start_cols, start_cols)
    )[0]
    return (down_total + jnp.transpose(across, (1, 0, 2))) * OUT_SCALE


def solution(mesh):
    in_specs = (P("gy", "gx", None), P("gy", "gx"), P(), P())
    out_specs = P("gy", "gx", None)
    return jax.shard_map(
        on_device, mesh=mesh, in_specs=in_specs, out_specs=out_specs, check_vma=False
    )
```

profile of v0, /device:TPU:62, one launch (start us, length us, event | category | flops | bytes accessed | tf_op | source)
XLA Modules:
  0.0 1107.9 jit_solution(2497831201230078459)
XLA Ops:
  23.3 659.9 %while.99 = (s32[]{:T(128)}, f32[16,16,256]{2,1,0:T(8,128)S(1)}, f32[8,256]{1,0:T(8,128)S(1)}, f32[8,256]{1,0:T(8,128)S(1)}, s32[]{:T(128)}, /*index=5*/s32[]{:T...) while((s32[]{:T(128)}, f32[16,16,256]{2,1,0:T(8,128)S(1)}, ...), condition=%wide.region_23.24_spmd, body=%wide.region_12.23_spmd.sunk | while | flops 98333 | bytes 1660603 | solution.py:179
  30.4 5.6 collective-permute-start.1
  79.3 8.0 collective-permute-start
  111.3 8.0 collective-permute-start
  145.1 9.6 collective-permute-start
  157.4 5.4 collective-permute-start
  165.5 5.4 collective-permute-start
  173.6 5.4 collective-permute-start
  181.7 5.4 collective-permute-start
  189.8 5.4 collective-permute-start
  197.9 5.4 collective-permute-start
  206.0 5.4 collective-permute-start
  214.1 5.4 collective-permute-start
  222.2 5.4 collective-permute-start
  262.7 337.4 %collective-permute-start = (f32[8,256]{1,0:T(8,128)S(1)}, f32[8,256]{1,0:T(8,128)S(1)}, u32[]{:S(2)}, u32[]{:S(2)}) collective-permute-start(f32[8,256]{1,0:T(8,128)S(1)} %get-tuple-element.1220), channel_id=1, source_target_pairs={{0,1},{1,2},{2,3},{3,4},{4,5},{5,6},{6,7},{7,8},{8,9},{9,10},{10,1... | collective-permute-start | bytes 24584 | tf_op jit(solution)/shard_map/while/body/eval_jaxpr/ppermute | solution.py:16
  601.0 14.3 %conditional.11 = (f32[16,16,256]{2,1,0:T(8,128)S(1)}, f32[8,256]{1,0:T(8,128)S(1)}) conditional(s32[]{:T(128)} %convert_element_type.93, f32[16,16,256]{2,1,0:T(8,128)S(1)} %get-tuple-element.1218, (s32[]{:T(128)}, f32[16,16,256]{2,1,0:T(8,128)S(1)}, s32[16,16,256]{2,1,0:T(8,128)S(1)}, f32[16,16]{1,0:T(8,128)S(1)}, f32[4]{0:T(128)S(1)}, ...), branch_computations={%region_18.18_spmd, %region_19.22_spmd} | conditional | flops 49161 | bytes 862647 | solution.py:97
  601.7 13.6 %while.97 = (s32[]{:T(128)}, f32[8,256]{1,0:T(8,128)S(1)}, f32[16,8,256]{2,1,0:T(8,128)S(1)}, s32[16,8,256]{2,1,0:T(8,128)S(1)}, f32[]{:T(128)}, /*index=5*/f32[16,8]{1,0:T(8,128)S(1)}, s32[]{:T(128)}, s32[]{:T(128)}, f32[]{:T(128)}) while((s32[]{:T(128)}, f32[8,256]{1,0:T(8,128)S(1)}, f32[16,8,256]{2,1,0:T(8,128)S(1)}, ...), condition=%wide.region_22.21_spmd, body=%wide.region_20.20_spmd.sunk | while | flops 16387 | bytes 58617 | solution.py:50
  617.3 5.4 collective-permute-start
  623.5 14.3 %conditional.11 = (f32[16,16,256]{2,1,0:T(8,128)S(1)}, f32[8,256]{1,0:T(8,128)S(1)}) conditional(s32[]{:T(128)} %convert_element_type.93, f32[16,16,256]{2,1,0:T(8,128)S(1)} %get-tuple-element.1218, (s32[]{:T(128)}, f32[16,16,256]{2,1,0:T(8,128)S(1)}, s32[16,16,256]{2,1,0:T(8,128)S(1)}, f32[16,16]{1,0:T(8,128)S(1)}, f32[4]{0:T(128)S(1)}, ...), branch_computations={%region_18.18_spmd, %region_19.22_spmd} | conditional | flops 49161 | bytes 862647 | solution.py:97
  624.2 13.6 %while.97 = (s32[]{:T(128)}, f32[8,256]{1,0:T(8,128)S(1)}, f32[16,8,256]{2,1,0:T(8,128)S(1)}, s32[16,8,256]{2,1,0:T(8,128)S(1)}, f32[]{:T(128)}, /*index=5*/f32[16,8]{1,0:T(8,128)S(1)}, s32[]{:T(128)}, s32[]{:T(128)}, f32[]{:T(128)}) while((s32[]{:T(128)}, f32[8,256]{1,0:T(8,128)S(1)}, f32[16,8,256]{2,1,0:T(8,128)S(1)}, ...), condition=%wide.region_22.21_spmd, body=%wide.region_20.20_spmd.sunk | while | flops 16387 | bytes 58617 | solution.py:50
  644.7 15.7 %collective-permute-start.1 = (f32[8,256]{1,0:T(8,128)S(1)}, f32[8,256]{1,0:T(8,128)S(1)}, u32[]{:S(2)}, u32[]{:S(2)}) collective-permute-start(f32[8,256]{1,0:T(8,128)S(1)} %get-tuple-element.1221), channel_id=1, source_target_pairs={{1,0},{2,1},{3,2},{4,3},{5,4},{6,5},{7,6},{8,7},{9,8},{10,9},{11,1... | collective-permute-start | bytes 24584 | tf_op jit(solution)/shard_map/while/body/eval_jaxpr/ppermute | solution.py:16
  669.8 13.4 %collective-permute-done = f32[8,256]{1,0:T(8,128)S(1)} collective-permute-done((f32[8,256]{1,0:T(8,128)S(1)}, f32[8,256]{1,0:T(8,128)S(1)}, u32[]{:S(2)}, u32[]{:S(2)}) %collective-permute-start) | collective-permute-done | bytes 8224 | tf_op jit(solution)/shard_map/while/body/eval_jaxpr/ppermute | solution.py:16
  684.2 422.8 %while.98 = (s32[]{:T(128)}, f32[16,16,256]{2,1,0:T(8,128)S(1)}, f32[8,256]{1,0:T(8,128)S(1)}, f32[8,256]{1,0:T(8,128)S(1)}, s32[]{:T(128)}, /*index=5*/s32[]{:T...) while((s32[]{:T(128)}, f32[16,16,256]{2,1,0:T(8,128)S(1)}, ...), condition=%wide.region_11.12_spmd, body=%wide.region_0.11_spmd.sunk | while | flops 98333 | bytes 1660103 | solution.py:180
  684.2 13.3 %conditional.9 = (f32[16,16,256]{2,1,0:T(8,128)S(1)}, f32[8,256]{1,0:T(8,128)S(1)}) conditional(s32[]{:T(128)} %convert_element_type.91, f32[16,16,256]{2,1,0:T(8,128)S(1)} %get-tuple-element.1204, (s32[]{:T(128)}, f32[16,16,256]{2,1,0:T(8,128)S(1)}, s32[16,16,256]{2,1,0:T(8,128)S(1)}, f32[16,16]{1,0:T(8,128)S(1)}, f32[4]{0:T(128)S(1)}, ...), branch_computations={%region_6.6_spmd, %region_7.10_spmd} | conditional | flops 49161 | bytes 862647 | solution.py:97
  684.9 12.6 %while.95 = (s32[]{:T(128)}, f32[8,256]{1,0:T(8,128)S(1)}, f32[16,8,256]{2,1,0:T(8,128)S(1)}, s32[16,8,256]{2,1,0:T(8,128)S(1)}, f32[]{:T(128)}, /*index=5*/f32[16,8]{1,0:T(8,128)S(1)}, s32[]{:T(128)}, s32[]{:T(128)}, f32[]{:T(128)}) while((s32[]{:T(128)}, f32[8,256]{1,0:T(8,128)S(1)}, f32[16,8,256]{2,1,0:T(8,128)S(1)}, ...), condition=%wide.region_10.9_spmd, body=%wide.region_8.8_spmd.sunk | while | flops 16387 | bytes 58617 | solution.py:50
  704.4 13.3 %conditional.9 = (f32[16,16,256]{2,1,0:T(8,128)S(1)}, f32[8,256]{1,0:T(8,128)S(1)}) conditional(s32[]{:T(128)} %convert_element_type.91, f32[16,16,256]{2,1,0:T(8,128)S(1)} %get-tuple-element.1204, (s32[]{:T(128)}, f32[16,16,256]{2,1,0:T(8,128)S(1)}, s32[16,16,256]{2,1,0:T(8,128)S(1)}, f32[16,16]{1,0:T(8,128)S(1)}, f32[4]{0:T(128)S(1)}, ...), branch_computations={%region_6.6_spmd, %region_7.10_spmd} | conditional | flops 49161 | bytes 862647 | solution.py:97
  705.0 12.6 %while.95 = (s32[]{:T(128)}, f32[8,256]{1,0:T(8,128)S(1)}, f32[16,8,256]{2,1,0:T(8,128)S(1)}, s32[16,8,256]{2,1,0:T(8,128)S(1)}, f32[]{:T(128)}, /*index=5*/f32[16,8]{1,0:T(8,128)S(1)}, s32[]{:T(128)}, s32[]{:T(128)}, f32[]{:T(128)}) while((s32[]{:T(128)}, f32[8,256]{1,0:T(8,128)S(1)}, f32[16,8,256]{2,1,0:T(8,128)S(1)}, ...), condition=%wide.region_10.9_spmd, body=%wide.region_8.8_spmd.sunk | while | flops 16387 | bytes 58617 | solution.py:50
  724.9 15.3 %collective-permute-start.3 = (f32[8,256]{1,0:T(8,128)S(1)}, f32[8,256]{1,0:T(8,128)S(1)}, u32[]{:S(2)}, u32[]{:S(2)}) collective-permute-start(f32[8,256]{1,0:T(8,128)S(1)} %get-tuple-element.1207), channel_id=1, source_target_pairs={{32,0},{64,32},{96,64},{128,96},{160,128},{192,160},{224,192},{256... | collective-permute-start | bytes 24584 | tf_op jit(solution)/shard_map/while/body/eval_jaxpr/ppermute | solution.py:16
  749.0 15.3 %collective-permute-done.2 = f32[8,256]{1,0:T(8,128)S(1)} collective-permute-done((f32[8,256]{1,0:T(8,128)S(1)}, f32[8,256]{1,0:T(8,128)S(1)}, u32[]{:S(2)}, u32[]{:S(2)}) %collective-permute-start.2) | collective-permute-done | bytes 8224 | tf_op jit(solution)/shard_map/while/body/eval_jaxpr/ppermute | solution.py:16
  773.7 15.1 %collective-permute-start.3 = (f32[8,256]{1,0:T(8,128)S(1)}, f32[8,256]{1,0:T(8,128)S(1)}, u32[]{:S(2)}, u32[]{:S(2)}) collective-permute-start(f32[8,256]{1,0:T(8,128)S(1)} %get-tuple-element.1207), channel_id=1, source_target_pairs={{32,0},{64,32},{96,64},{128,96},{160,128},{192,160},{224,192},{256... | collective-permute-start | bytes 24584 | tf_op jit(solution)/shard_map/while/body/eval_jaxpr/ppermute | solution.py:16
  799.8 15.3 %collective-permute-done.2 = f32[8,256]{1,0:T(8,128)S(1)} collective-permute-done((f32[8,256]{1,0:T(8,128)S(1)}, f32[8,256]{1,0:T(8,128)S(1)}, u32[]{:S(2)}, u32[]{:S(2)}) %collective-permute-start.2) | collective-permute-done | bytes 8224 | tf_op jit(solution)/shard_map/while/body/eval_jaxpr/ppermute | solution.py:16
  815.1 6.0 collective-permute-start.3
  826.6 10.9 collective-permute-start.3
  843.1 6.0 collective-permute-start.3
  850.4 20.2 %collective-permute-done.2 = f32[8,256]{1,0:T(8,128)S(1)} collective-permute-done((f32[8,256]{1,0:T(8,128)S(1)}, f32[8,256]{1,0:T(8,128)S(1)}, u32[]{:S(2)}, u32[]{:S(2)}) %collective-permute-start.2) | collective-permute-done | bytes 8224 | tf_op jit(solution)/shard_map/while/body/eval_jaxpr/ppermute | solution.py:16
  870.6 19.3 %collective-permute-start.3 = (f32[8,256]{1,0:T(8,128)S(1)}, f32[8,256]{1,0:T(8,128)S(1)}, u32[]{:S(2)}, u32[]{:S(2)}) collective-permute-start(f32[8,256]{1,0:T(8,128)S(1)} %get-tuple-element.1207), channel_id=1, source_target_pairs={{32,0},{64,32},{96,64},{128,96},{160,128},{192,160},{224,192},{256... | collective-permute-start | bytes 24584 | tf_op jit(solution)/shard_map/while/body/eval_jaxpr/ppermute | solution.py:16
  891.3 6.1 collective-permute-done.2
  897.4 34.7 %collective-permute-start.3 = (f32[8,256]{1,0:T(8,128)S(1)}, f32[8,256]{1,0:T(8,128)S(1)}, u32[]{:S(2)}, u32[]{:S(2)}) collective-permute-start(f32[8,256]{1,0:T(8,128)S(1)} %get-tuple-element.1207), channel_id=1, source_target_pairs={{32,0},{64,32},{96,64},{128,96},{160,128},{192,160},{224,192},{256... | collective-permute-start | bytes 24584 | tf_op jit(solution)/shard_map/while/body/eval_jaxpr/ppermute | solution.py:16
  933.4 19.5 %collective-permute-done.2 = f32[8,256]{1,0:T(8,128)S(1)} collective-permute-done((f32[8,256]{1,0:T(8,128)S(1)}, f32[8,256]{1,0:T(8,128)S(1)}, u32[]{:S(2)}, u32[]{:S(2)}) %collective-permute-start.2) | collective-permute-done | bytes 8224 | tf_op jit(solution)/shard_map/while/body/eval_jaxpr/ppermute | solution.py:16
  952.9 19.3 %collective-permute-start.3 = (f32[8,256]{1,0:T(8,128)S(1)}, f32[8,256]{1,0:T(8,128)S(1)}, u32[]{:S(2)}, u32[]{:S(2)}) collective-permute-start(f32[8,256]{1,0:T(8,128)S(1)} %get-tuple-element.1207), channel_id=1, source_target_pairs={{32,0},{64,32},{96,64},{128,96},{160,128},{192,160},{224,192},{256... | collective-permute-start | bytes 24584 | tf_op jit(solution)/shard_map/while/body/eval_jaxpr/ppermute | solution.py:16
  973.6 19.5 %collective-permute-done.2 = f32[8,256]{1,0:T(8,128)S(1)} collective-permute-done((f32[8,256]{1,0:T(8,128)S(1)}, f32[8,256]{1,0:T(8,128)S(1)}, u32[]{:S(2)}, u32[]{:S(2)}) %collective-permute-start.2) | collective-permute-done | bytes 8224 | tf_op jit(solution)/shard_map/while/body/eval_jaxpr/ppermute | solution.py:16
  993.1 21.3 %collective-permute-start.3 = (f32[8,256]{1,0:T(8,128)S(1)}, f32[8,256]{1,0:T(8,128)S(1)}, u32[]{:S(2)}, u32[]{:S(2)}) collective-permute-start(f32[8,256]{1,0:T(8,128)S(1)} %get-tuple-element.1207), channel_id=1, source_target_pairs={{32,0},{64,32},{96,64},{128,96},{160,128},{192,160},{224,192},{256... | collective-permute-start | bytes 24584 | tf_op jit(solution)/shard_map/while/body/eval_jaxpr/ppermute | solution.py:16
  1015.8 19.5 %collective-permute-done.2 = f32[8,256]{1,0:T(8,128)S(1)} collective-permute-done((f32[8,256]{1,0:T(8,128)S(1)}, f32[8,256]{1,0:T(8,128)S(1)}, u32[]{:S(2)}, u32[]{:S(2)}) %collective-permute-start.2) | collective-permute-done | bytes 8224 | tf_op jit(solution)/shard_map/while/body/eval_jaxpr/ppermute | solution.py:16
  1035.3 19.3 %collective-permute-start.3 = (f32[8,256]{1,0:T(8,128)S(1)}, f32[8,256]{1,0:T(8,128)S(1)}, u32[]{:S(2)}, u32[]{:S(2)}) collective-permute-start(f32[8,256]{1,0:T(8,128)S(1)} %get-tuple-element.1207), channel_id=1, source_target_pairs={{32,0},{64,32},{96,64},{128,96},{160,128},{192,160},{224,192},{256... | collective-permute-start | bytes 24584 | tf_op jit(solution)/shard_map/while/body/eval_jaxpr/ppermute | solution.py:16
  1060.1 15.2 %conditional.8 = (f32[16,16,256]{2,1,0:T(8,128)S(1)}, f32[8,256]{1,0:T(8,128)S(1)}) conditional(s32[]{:T(128)} %convert_element_type.92, f32[16,16,256]{2,1,0:T(8,128)S(1)} %get-tuple-element.1386, (s32[]{:T(128)}, f32[16,16,256]{2,1,0:T(8,128)S(1)}, s32[16,16,256]{2,1,0:T(8,128)S(1)}, f32[16,16]{1,0:T(8,128)S(1)}, f32[4]{0:T(128)S(1)}, ...), branch_computations={%region_1.1_spmd, %region_2.5_spmd} | conditional | flops 49160 | bytes 731543 | solution.py:97
  1060.9 14.4 %while.94 = (s32[]{:T(128)}, f32[8,256]{1,0:T(8,128)S(1)}, f32[16,8,256]{2,1,0:T(8,128)S(1)}, s32[16,8,256]{2,1,0:T(8,128)S(1)}, f32[]{:T(128)}, /*index=5*/f32[16,8]{1,0:T(8,128)S(1)}, s32[]{:T(128)}, f32[]{:T(128)}) while((s32[]{:T(128)}, f32[8,256]{1,0:T(8,128)S(1)}, f32[16,8,256]{2,1,0:T(8,128)S(1)}, s32[16,8,256]{2,1,0:T(8,128)S(1)}, ...), condition=%wide.region_5.4_spmd, body=%wide.region_3.3_spmd.sunk | while | flops 16386 | bytes 58597 | solution.py:50
  1084.9 15.2 %conditional.8 = (f32[16,16,256]{2,1,0:T(8,128)S(1)}, f32[8,256]{1,0:T(8,128)S(1)}) conditional(s32[]{:T(128)} %convert_element_type.92, f32[16,16,256]{2,1,0:T(8,128)S(1)} %get-tuple-element.1386, (s32[]{:T(128)}, f32[16,16,256]{2,1,0:T(8,128)S(1)}, s32[16,16,256]{2,1,0:T(8,128)S(1)}, f32[16,16]{1,0:T(8,128)S(1)}, f32[4]{0:T(128)S(1)}, ...), branch_computations={%region_1.1_spmd, %region_2.5_spmd} | conditional | flops 49160 | bytes 731543 | solution.py:97
  1085.6 14.4 %while.94 = (s32[]{:T(128)}, f32[8,256]{1,0:T(8,128)S(1)}, f32[16,8,256]{2,1,0:T(8,128)S(1)}, s32[16,8,256]{2,1,0:T(8,128)S(1)}, f32[]{:T(128)}, /*index=5*/f32[16,8]{1,0:T(8,128)S(1)}, s32[]{:T(128)}, f32[]{:T(128)}) while((s32[]{:T(128)}, f32[8,256]{1,0:T(8,128)S(1)}, f32[16,8,256]{2,1,0:T(8,128)S(1)}, s32[16,8,256]{2,1,0:T(8,128)S(1)}, ...), condition=%wide.region_5.4_spmd, body=%wide.region_3.3_spmd.sunk | while | flops 16386 | bytes 58597 | solution.py:50
  (945 shorter events, 382.9 us)
Async XLA Ops:
  0.8 19.6 %collective-permute-start.4 = (f32[1,16]{0,1:T(8,128)S(1)}, f32[1,16]{0,1:T(8,128)S(1)}, u32[]{:S(2)}, u32[]{:S(2)}) collective-permute-start(f32[1,16]{0,1:T(8,128)S(1)} %get-tuple-element.943), channel_id=1, source_target_pairs={{0,32},{32,64},{64,96},{96,128},{128,160},{160,192},{192,224},{224... | collective-permute-start | bytes 200 | tf_op jit(solution)/shard_map/ppermute | solution.py:27
  2.1 18.3 %collective-permute-start.5 = (f32[1,16]{0,1:T(8,128)S(1)}, f32[1,16]{0,1:T(8,128)S(1)}, u32[]{:S(2)}, u32[]{:S(2)}) collective-permute-start(f32[1,16]{0,1:T(8,128)S(1)} %get-tuple-element.942), channel_id=1, source_target_pairs={{32,0},{64,32},{96,64},{128,96},{160,128},{192,160},{224,192},{256... | collective-permute-start | bytes 200 | tf_op jit(solution)/shard_map/ppermute | solution.py:28
  6.7 13.8 %collective-permute-start.6 = (f32[16,1]{0,1:T(1,128)S(1)}, f32[16,1]{0,1:T(1,128)S(1)}, u32[]{:S(2)}, u32[]{:S(2)}) collective-permute-start(f32[16,1]{0,1:T(1,128)S(1)} %get-tuple-element.941), channel_id=1, source_target_pairs={{0,1},{1,2},{2,3},{3,4},{4,5},{5,6},{6,7},{7,8},{8,9},{9,10},{10,1... | collective-permute-start | bytes 200 | tf_op jit(solution)/shard_map/ppermute | solution.py:27
  8.6 11.8 %collective-permute-start.7 = (f32[16,1]{0,1:T(1,128)S(1)}, f32[16,1]{0,1:T(1,128)S(1)}, u32[]{:S(2)}, u32[]{:S(2)}) collective-permute-start(f32[16,1]{0,1:T(1,128)S(1)} %get-tuple-element.940), channel_id=1, source_target_pairs={{1,0},{2,1},{3,2},{4,3},{5,4},{6,5},{7,6},{8,7},{9,8},{10,9},{11,1... | collective-permute-start | bytes 200 | tf_op jit(solution)/shard_map/ppermute | solution.py:28
  30.4 7.5 collective-permute-start.1
  77.4 9.9 collective-permute-start.1
  79.3 8.8 collective-permute-start
  109.3 9.9 collective-permute-start.1
  111.3 8.8 collective-permute-start
  126.9 7.3 collective-permute-start.1
  135.0 7.3 collective-permute-start.1
  143.1 11.5 %collective-permute-start.1 = (f32[8,256]{1,0:T(8,128)S(1)}, f32[8,256]{1,0:T(8,128)S(1)}, u32[]{:S(2)}, u32[]{:S(2)}) collective-permute-start(f32[8,256]{1,0:T(8,128)S(1)} %get-tuple-element.1221), channel_id=1, source_target_pairs={{1,0},{2,1},{3,2},{4,3},{5,4},{6,5},{7,6},{8,7},{9,8},{10,9},{11,1... | collective-permute-start | bytes 24584 | tf_op jit(solution)/shard_map/while/body/eval_jaxpr/ppermute | solution.py:16
  145.1 10.4 collective-permute-start
  155.4 7.3 collective-permute-start.1
  163.5 7.3 collective-permute-start.1
  171.6 7.3 collective-permute-start.1
  179.8 7.3 collective-permute-start.1
  187.9 7.3 collective-permute-start.1
  196.0 7.3 collective-permute-start.1
  204.1 7.3 collective-permute-start.1
  212.2 7.3 collective-permute-start.1
  220.3 7.3 collective-permute-start.1
  228.4 7.3 collective-permute-start.1
  236.5 7.3 collective-permute-start.1
  244.6 7.3 collective-permute-start.1
  252.7 7.3 collective-permute-start.1
  260.8 339.4 %collective-permute-start.1 = (f32[8,256]{1,0:T(8,128)S(1)}, f32[8,256]{1,0:T(8,128)S(1)}, u32[]{:S(2)}, u32[]{:S(2)}) collective-permute-start(f32[8,256]{1,0:T(8,128)S(1)} %get-tuple-element.1221), channel_id=1, source_target_pairs={{1,0},{2,1},{3,2},{4,3},{5,4},{6,5},{7,6},{8,7},{9,8},{10,9},{11,1... | collective-permute-start | bytes 24584 | tf_op jit(solution)/shard_map/while/body/eval_jaxpr/ppermute | solution.py:16
  262.7 338.3 %collective-permute-start = (f32[8,256]{1,0:T(8,128)S(1)}, f32[8,256]{1,0:T(8,128)S(1)}, u32[]{:S(2)}, u32[]{:S(2)}) collective-permute-start(f32[8,256]{1,0:T(8,128)S(1)} %get-tuple-element.1220), channel_id=1, source_target_pairs={{0,1},{1,2},{2,3},{3,4},{4,5},{5,6},{6,7},{7,8},{8,9},{9,10},{10,1... | collective-permute-start | bytes 24584 | tf_op jit(solution)/shard_map/while/body/eval_jaxpr/ppermute | solution.py:16
  615.3 7.4 collective-permute-start.1
  644.7 17.7 %collective-permute-start.1 = (f32[8,256]{1,0:T(8,128)S(1)}, f32[8,256]{1,0:T(8,128)S(1)}, u32[]{:S(2)}, u32[]{:S(2)}) collective-permute-start(f32[8,256]{1,0:T(8,128)S(1)} %get-tuple-element.1221), channel_id=1, source_target_pairs={{1,0},{2,1},{3,2},{4,3},{5,4},{6,5},{7,6},{8,7},{9,8},{10,9},{11,1... | collective-permute-start | bytes 24584 | tf_op jit(solution)/shard_map/while/body/eval_jaxpr/ppermute | solution.py:16
  667.4 15.9 %collective-permute-start = (f32[8,256]{1,0:T(8,128)S(1)}, f32[8,256]{1,0:T(8,128)S(1)}, u32[]{:S(2)}, u32[]{:S(2)}) collective-permute-start(f32[8,256]{1,0:T(8,128)S(1)} %get-tuple-element.1220), channel_id=1, source_target_pairs={{0,1},{1,2},{2,3},{3,4},{4,5},{5,6},{6,7},{7,8},{8,9},{9,10},{10,1... | collective-permute-start | bytes 24584 | tf_op jit(solution)/shard_map/while/body/eval_jaxpr/ppermute | solution.py:16
  724.9 16.6 %collective-permute-start.3 = (f32[8,256]{1,0:T(8,128)S(1)}, f32[8,256]{1,0:T(8,128)S(1)}, u32[]{:S(2)}, u32[]{:S(2)}) collective-permute-start(f32[8,256]{1,0:T(8,128)S(1)} %get-tuple-element.1207), channel_id=1, source_target_pairs={{32,0},{64,32},{96,64},{128,96},{160,128},{192,160},{224,192},{256... | collective-permute-start | bytes 24584 | tf_op jit(solution)/shard_map/while/body/eval_jaxpr/ppermute | solution.py:16
  747.6 16.6 %collective-permute-start.2 = (f32[8,256]{1,0:T(8,128)S(1)}, f32[8,256]{1,0:T(8,128)S(1)}, u32[]{:S(2)}, u32[]{:S(2)}) collective-permute-start(f32[8,256]{1,0:T(8,128)S(1)} %get-tuple-element.1206), channel_id=1, source_target_pairs={{0,32},{32,64},{64,96},{96,128},{128,160},{160,192},{192,224},{224... | collective-permute-start | bytes 24584 | tf_op jit(solution)/shard_map/while/body/eval_jaxpr/ppermute | solution.py:16
  773.7 16.5 %collective-permute-start.3 = (f32[8,256]{1,0:T(8,128)S(1)}, f32[8,256]{1,0:T(8,128)S(1)}, u32[]{:S(2)}, u32[]{:S(2)}) collective-permute-start(f32[8,256]{1,0:T(8,128)S(1)} %get-tuple-element.1207), channel_id=1, source_target_pairs={{32,0},{64,32},{96,64},{128,96},{160,128},{192,160},{224,192},{256... | collective-permute-start | bytes 24584 | tf_op jit(solution)/shard_map/while/body/eval_jaxpr/ppermute | solution.py:16
  798.4 16.6 %collective-permute-start.2 = (f32[8,256]{1,0:T(8,128)S(1)}, f32[8,256]{1,0:T(8,128)S(1)}, u32[]{:S(2)}, u32[]{:S(2)}) collective-permute-start(f32[8,256]{1,0:T(8,128)S(1)} %get-tuple-element.1206), channel_id=1, source_target_pairs={{0,32},{32,64},{64,96},{96,128},{128,160},{160,192},{192,224},{224... | collective-permute-start | bytes 24584 | tf_op jit(solution)/shard_map/while/body/eval_jaxpr/ppermute | solution.py:16
  815.1 7.4 collective-permute-start.3
  826.6 12.2 %collective-permute-start.3 = (f32[8,256]{1,0:T(8,128)S(1)}, f32[8,256]{1,0:T(8,128)S(1)}, u32[]{:S(2)}, u32[]{:S(2)}) collective-permute-start(f32[8,256]{1,0:T(8,128)S(1)} %get-tuple-element.1207), channel_id=1, source_target_pairs={{32,0},{64,32},{96,64},{128,96},{160,128},{192,160},{224,192},{256... | collective-permute-start | bytes 24584 | tf_op jit(solution)/shard_map/while/body/eval_jaxpr/ppermute | solution.py:16
  843.1 7.4 collective-permute-start.3
  849.1 21.5 %collective-permute-start.2 = (f32[8,256]{1,0:T(8,128)S(1)}, f32[8,256]{1,0:T(8,128)S(1)}, u32[]{:S(2)}, u32[]{:S(2)}) collective-permute-start(f32[8,256]{1,0:T(8,128)S(1)} %get-tuple-element.1206), channel_id=1, source_target_pairs={{0,32},{32,64},{64,96},{96,128},{128,160},{160,192},{192,224},{224... | collective-permute-start | bytes 24584 | tf_op jit(solution)/shard_map/while/body/eval_jaxpr/ppermute | solution.py:16
  870.6 20.7 %collective-permute-start.3 = (f32[8,256]{1,0:T(8,128)S(1)}, f32[8,256]{1,0:T(8,128)S(1)}, u32[]{:S(2)}, u32[]{:S(2)}) collective-permute-start(f32[8,256]{1,0:T(8,128)S(1)} %get-tuple-element.1207), channel_id=1, source_target_pairs={{32,0},{64,32},{96,64},{128,96},{160,128},{192,160},{224,192},{256... | collective-permute-start | bytes 24584 | tf_op jit(solution)/shard_map/while/body/eval_jaxpr/ppermute | solution.py:16
  889.9 7.5 collective-permute-start.2
  897.4 36.0 %collective-permute-start.3 = (f32[8,256]{1,0:T(8,128)S(1)}, f32[8,256]{1,0:T(8,128)S(1)}, u32[]{:S(2)}, u32[]{:S(2)}) collective-permute-start(f32[8,256]{1,0:T(8,128)S(1)} %get-tuple-element.1207), channel_id=1, source_target_pairs={{32,0},{64,32},{96,64},{128,96},{160,128},{192,160},{224,192},{256... | collective-permute-start | bytes 24584 | tf_op jit(solution)/shard_map/while/body/eval_jaxpr/ppermute | solution.py:16
  932.1 20.8 %collective-permute-start.2 = (f32[8,256]{1,0:T(8,128)S(1)}, f32[8,256]{1,0:T(8,128)S(1)}, u32[]{:S(2)}, u32[]{:S(2)}) collective-permute-start(f32[8,256]{1,0:T(8,128)S(1)} %get-tuple-element.1206), channel_id=1, source_target_pairs={{0,32},{32,64},{64,96},{96,128},{128,160},{160,192},{192,224},{224... | collective-permute-start | bytes 24584 | tf_op jit(solution)/shard_map/while/body/eval_jaxpr/ppermute | solution.py:16
  952.9 20.7 %collective-permute-start.3 = (f32[8,256]{1,0:T(8,128)S(1)}, f32[8,256]{1,0:T(8,128)S(1)}, u32[]{:S(2)}, u32[]{:S(2)}) collective-permute-start(f32[8,256]{1,0:T(8,128)S(1)} %get-tuple-element.1207), channel_id=1, source_target_pairs={{32,0},{64,32},{96,64},{128,96},{160,128},{192,160},{224,192},{256... | collective-permute-start | bytes 24584 | tf_op jit(solution)/shard_map/while/body/eval_jaxpr/ppermute | solution.py:16
  972.3 20.8 %collective-permute-start.2 = (f32[8,256]{1,0:T(8,128)S(1)}, f32[8,256]{1,0:T(8,128)S(1)}, u32[]{:S(2)}, u32[]{:S(2)}) collective-permute-start(f32[8,256]{1,0:T(8,128)S(1)} %get-tuple-element.1206), channel_id=1, source_target_pairs={{0,32},{32,64},{64,96},{96,128},{128,160},{160,192},{192,224},{224... | collective-permute-start | bytes 24584 | tf_op jit(solution)/shard_map/while/body/eval_jaxpr/ppermute | solution.py:16
  993.1 22.7 %collective-permute-start.3 = (f32[8,256]{1,0:T(8,128)S(1)}, f32[8,256]{1,0:T(8,128)S(1)}, u32[]{:S(2)}, u32[]{:S(2)}) collective-permute-start(f32[8,256]{1,0:T(8,128)S(1)} %get-tuple-element.1207), channel_id=1, source_target_pairs={{32,0},{64,32},{96,64},{128,96},{160,128},{192,160},{224,192},{256... | collective-permute-start | bytes 24584 | tf_op jit(solution)/shard_map/while/body/eval_jaxpr/ppermute | solution.py:16
  1014.4 20.8 %collective-permute-start.2 = (f32[8,256]{1,0:T(8,128)S(1)}, f32[8,256]{1,0:T(8,128)S(1)}, u32[]{:S(2)}, u32[]{:S(2)}) collective-permute-start(f32[8,256]{1,0:T(8,128)S(1)} %get-tuple-element.1206), channel_id=1, source_target_pairs={{0,32},{32,64},{64,96},{96,128},{128,160},{160,192},{192,224},{224... | collective-permute-start | bytes 24584 | tf_op jit(solution)/shard_map/while/body/eval_jaxpr/ppermute | solution.py:16
  1035.3 20.7 %collective-permute-start.3 = (f32[8,256]{1,0:T(8,128)S(1)}, f32[8,256]{1,0:T(8,128)S(1)}, u32[]{:S(2)}, u32[]{:S(2)}) collective-permute-start(f32[8,256]{1,0:T(8,128)S(1)} %get-tuple-element.1207), channel_id=1, source_target_pairs={{32,0},{64,32},{96,64},{128,96},{160,128},{192,160},{224,192},{256... | collective-permute-start | bytes 24584 | tf_op jit(solution)/shard_map/while/body/eval_jaxpr/ppermute | solution.py:16
  (59 other events, 303.8 us)
where the time goes:
time: 1110 us
  starting transfers between devices  789 us (71%)
  waiting for transfers between devices  209 us (19%)
  other arithmetic  91.7 us (8%)
    ppermute x100, starting transfers between devices, shifted(): return lax.ppermute(shard, axis, pairs)  778 us
    ppermute x100, waiting for transfers between devices, shifted(): return lax.ppermute(shard, axis, pairs)  209 us
    dynamic_update_slice x128, other arithmetic, sweep(): lax.scan(partial(advance, penalty_one=penalty_one), start, (cost_lines, l...  71.4 us
  transfers between devices with their start and end apart: 104, of which 50 were waited for; matrix products, arithmetic and copies ran while one was open for 0% of the time, Pallas kernels for 0%

commit v1 on v0

v1 whole, which is shorter than its diff:
```python
from functools import partial

import jax
import jax.numpy as jnp
from jax import lax
from jax.experimental import pallas as pl
from jax.experimental.pallas import tpu as pltpu
from jax.sharding import PartitionSpec as P

FAR = 1e30
GRADIENT_GAIN = 4.0
OUT_SCALE = 1.0 / 256.0
LANES = 128
TILES = 32
ROWS = 24


def adaptive(penalty_one, penalty_two, step_diff):
    return penalty_one + (penalty_two - penalty_one) / (1.0 + GRADIENT_GAIN * jnp.abs(step_diff))


def gather_costs(blocks, two, core_ref, sources, scr, img):
    for z in range(blocks // len(sources)):
        for which, source in enumerate(sources):
            if two:
                core = core_ref[0]
                place = 2 * z + core if which == 0 else 2 * z + 1 - core
            else:
                place = z
            scr[place] = source[z, 0:16, :].astype(jnp.bfloat16)
            img[pl.ds(place, 1), :] = source[z, 16:17, 0:LANES]


def path_kernel(blocks, first, two, core_ref, small_ref, large_ref, *refs):
    sources, (out_ref, scr, img, ahead, back, costs, starts, states) = refs[:-8], refs[-8:]
    groups = blocks // 4
    lane = lax.broadcasted_iota(jnp.int32, (8, LANES), 1)
    sub = lax.broadcasted_iota(jnp.int32, (8, LANES), 0)
    gather_costs(blocks, two, core_ref, sources, scr, img)

    place, row = lane[:groups] % 64, sub[:groups]
    line = img[pl.ds(0, groups, stride=4), :]
    for k in range(1, 4):
        line = jnp.where(place // 16 == k, img[pl.ds(k, groups, stride=4), :], line)
    before = pltpu.roll(line, 1, 1)
    wrapped = jnp.concatenate([before[groups - 1 :], before[: groups - 1]], 0)
    before = jnp.where(place == 0, jnp.where(row == 0, 0.0, wrapped), before)
    after = pltpu.roll(line, LANES - 1, 1)
    wrapped = jnp.concatenate([after[1:], after[:1]], 0)
    after = jnp.where(place == 63, jnp.where(row == groups - 1, 0.0, wrapped), after)
    small = [small_ref[first + i].astype(jnp.float32) for i in range(2)]
    large = [large_ref[first + i].astype(jnp.float32) for i in range(2)]
    ahead[...] = adaptive(small[0], large[0], line - before)
    back[...] = adaptive(small[1], large[1], line - after)
    forward = lane < 64
    penalty_one = jnp.where(forward, small[0], small[1])

    to = lax.broadcasted_iota(jnp.int32, (256, 256), 0)
    of = lax.broadcasted_iota(jnp.int32, (256, 256), 1)
    order = (of == (to % 8) * TILES + to // 8).astype(jnp.bfloat16)
    for g in range(groups):
        pixels = jnp.concatenate(
            [
                scr[4 * g : 4 * g + 4].reshape(64, 256),
                scr[blocks - 4 * g - 4 : blocks - 4 * g].reshape(64, 256),
            ],
            0,
        )
        turned = lax.dot_general(
            order, pixels, (((1,), (1,)), ((), ())), preferred_element_type=jnp.float32
        )
        costs[g] = turned.reshape(TILES, 8, LANES)

    def lowest_of(level):
        while len(level) > 1:
            level = [jnp.minimum(level[i], level[i + 1]) for i in range(0, len(level), 2)]
        lowest = level[0]
        for shift in (4, 2, 1):
            lowest = jnp.minimum(lowest, pltpu.roll(lowest, shift, 0))
        return lowest

    def segment(k, path):
        lowest = lowest_of(path)
        path = [x - lowest for x in path]
        here = lane % 64 == k
        for v in range(TILES):
            starts[v] = jnp.where(here, path[v], starts[v])
        g = k // 4
        penalty_two = jnp.where(
            forward,
            jnp.broadcast_to(ahead[pl.ds(g, 1), :], (8, LANES)),
            jnp.broadcast_to(back[pl.ds(groups - 1 - g, 1), :], (8, LANES)),
        )
        base = 16 * (k % 4)
        for j in range(16):
            source = jnp.where(forward, base + j, 127 - base - j)
            jump = jnp.take_along_axis(penalty_two, source, axis=1)
            if j == 0:
                highest = jump
            else:
                highest = lowest_of(path) + jump
            raised = [x + penalty_one for x in path]
            below = jnp.where(sub == 0, FAR, pltpu.roll(raised[-1], 1, 0))
            above = jnp.where(sub == 7, FAR, pltpu.roll(raised[0], 7, 0))
            padded = [below, *raised, above]
            path = [
                jnp.minimum(
                    jnp.minimum(path[v], jnp.minimum(padded[v], padded[v + 2])), highest
                )
                + jnp.take_along_axis(costs[g, v], source, axis=1)
                for v in range(TILES)
            ]
        return tuple(path)

    zero = jnp.zeros((8, LANES), jnp.float32)
    lax.fori_loop(0, blocks, segment, (zero,) * TILES)
    states[...] = jnp.concatenate([starts[:, s, :] for s in range(8)], 0).T
    for z in range(16):
        block = 2 * z + core_ref[0] if two else z
        out_ref[z, 0:1, :] = states[pl.ds(block, 1), :]
        out_ref[z, 1:2, :] = states[pl.ds(64 + blocks - 1 - block, 1), :]
        fore, rear = ahead[pl.ds(block // 4, 1), :], back[pl.ds(block // 4, 1), :]
        out_ref[z, 2:3, :] = jnp.concatenate([fore, fore], 1)
        out_ref[z, 3:4, :] = jnp.concatenate([rear, rear], 1)


def path_states(blocks, first, two, core, p_small, p_large, *sources):
    smem = pl.BlockSpec(memory_space=pltpu.SMEM)
    vmem = pl.BlockSpec(memory_space=pltpu.VMEM)
    return pl.pallas_call(
        partial(path_kernel, blocks, first, two),
        out_shape=jax.ShapeDtypeStruct((16, 4, 256), jnp.float32),
        in_specs=[smem] * 3 + [vmem] * len(sources),
        out_specs=vmem,
        scratch_shapes=[
            pltpu.VMEM((blocks, 16, 256), jnp.bfloat16),
            pltpu.VMEM((blocks, LANES), jnp.float32),
            pltpu.VMEM((blocks // 4, LANES), jnp.float32),
            pltpu.VMEM((blocks // 4, LANES), jnp.float32),
            pltpu.VMEM((blocks // 4, TILES, 8, LANES), jnp.float32),
            pltpu.VMEM((TILES, 8, LANES), jnp.float32),
            pltpu.VMEM((LANES, 256), jnp.float32),
        ],
        compiler_params=pltpu.CompilerParams(vmem_limit_bytes=24 * 2**20),
        cost_estimate=pl.CostEstimate(
            flops=blocks * 16 * 256 * 128 * 8, bytes_accessed=blocks * 24 * 1024, transcendentals=0
        ),
        name="line_paths",
    )(core, p_small, p_large, *sources)


def replay_kernel(first, across, quarter_ref, small_ref, entry_ref, cost_ref, *refs):
    *so_far, out_ref = refs
    lane = lax.broadcasted_iota(jnp.int32, (16, 256), 1)
    shift = (LANES - 16 * quarter_ref[0]) % LANES
    paths = [entry_ref[:, i, :] for i in range(2)]
    jumps = [pltpu.roll(entry_ref[:, 2 + i, 0:LANES], shift, 1) for i in range(2)]
    small = [small_ref[first + i].astype(jnp.float32) for i in range(2)]
    for j in range(16):
        for i, at in enumerate((j, 15 - j)):
            path = paths[i]
            lowest = jnp.min(path, axis=1, keepdims=True)
            below = jnp.where(lane == 0, FAR, pltpu.roll(path, 1, 1))
            above = jnp.where(lane == 255, FAR, pltpu.roll(path, 255, 1))
            chosen = jnp.minimum(path, jnp.minimum(below, above) + small[i])
            chosen = jnp.minimum(chosen, lowest + jumps[i][:, at : at + 1])
            cost = cost_ref[:, at, :] if across else cost_ref[at]
            path = cost.astype(jnp.float32) + chosen - lowest
            paths[i] = path
            here = (slice(None), at) if across else (at,)
            seen = j >= 8
            if across:
                value = path if seen else path + so_far[0][here]
                value = value + out_ref[here] if seen else value
                out_ref[here] = value * OUT_SCALE if seen else value
            else:
                out_ref[here] = path + out_ref[here] if seen else path


def replay(first, across, quarter, p_small, entry, cost, *so_far):
    smem = pl.BlockSpec(memory_space=pltpu.SMEM)
    vmem = pl.BlockSpec(memory_space=pltpu.VMEM)
    return pl.pallas_call(
        partial(replay_kernel, first, across),
        out_shape=jax.ShapeDtypeStruct((16, 16, 256), jnp.float32),
        in_specs=[smem] * 2 + [vmem] * (2 + len(so_far)),
        out_specs=vmem,
        cost_estimate=pl.CostEstimate(
            flops=2 * 65536 * 100, bytes_accessed=2**20, transcendentals=0
        ),
        name="block_paths",
    )(quarter, p_small, entry, cost, *so_far)


def message(cost, image):
    wide = jnp.tile(image, (1, 16))[:, None, :]
    empty = jnp.zeros((16, ROWS - 17, 256), jnp.float32)
    return jnp.concatenate([cost.astype(jnp.float32), wide, empty], 1)


def on_device(cost_volume, left_image, p_small, p_large):
    index_x, index_y = lax.axis_index("gx"), lax.axis_index("gy")
    core = (index_x % 2).reshape(1)
    chips = [[2 * z + c for z in range(16)] for c in range(2)]
    swap = [(i, i ^ 1) for i in range(32)]

    lines = message(cost_volume, left_image)
    lines = lax.all_to_all(lines, "gx", 0, 0, axis_index_groups=chips)
    columns = message(jnp.transpose(cost_volume, (1, 0, 2)), left_image.T)
    columns = lax.all_to_all(columns, "gy", 0, 0)
    others = lax.ppermute(lines, "gx", swap)

    entry_y = path_states(16, 2, False, core, p_small, p_large, columns)
    entry_y = lax.all_to_all(entry_y, "gy", 0, 0)
    entry_x = path_states(32, 0, True, core, p_small, p_large, lines, others)
    entry_x = lax.all_to_all(entry_x, "gx", 0, 0, axis_index_groups=chips)

    total = replay(2, False, (index_y % 4).reshape(1), p_small, entry_y, cost_volume)
    return replay(0, True, (index_x % 4).reshape(1), p_small, entry_x, cost_volume, total)


def solution(mesh):
    in_specs = (P("gy", "gx", None), P("gy", "gx"), P(), P())
    out_specs = P("gy", "gx", None)
    return jax.shard_map(
        on_device, mesh=mesh, in_specs=in_specs, out_specs=out_specs, check_vma=False
    )
```

time: 1110 us -> 124 us (0.11)
  the two profiles are of different devices: /device:TPU:62 before, /device:TPU:2 now
where the time goes in v1:
time: 124 us; the launch traced here: 123 us
  Pallas kernels  45.1 us (36%)
  starting transfers between devices  36.7 us (30%)
  waiting for transfers between devices  36.5 us (29%)
  local copies, waits for them, and re-layouts  3.47 us (3%)
    pallas_call x2, Pallas kernels, path_states(): pl.pallas_call(partial(path_kernel, blocks, first, two), out_shape=jax.Sh...  36.5 us
    all_to_all x1, waiting for transfers between devices, on_device(): lines = lax.all_to_all(lines, 'gx', 0, 0, axis_index_groups=chips)  22.7 us
    all_to_all x1, starting transfers between devices, on_device(): lines = lax.all_to_all(lines, 'gx', 0, 0, axis_index_groups=chips)  15.3 us
    pallas_call x2, Pallas kernels, replay(): pl.pallas_call(partial(replay_kernel, first, across), out_shape=jax.Shape...  8.66 us
    all_to_all x1, waiting for transfers between devices, on_device(): entry_x = lax.all_to_all(entry_x, 'gx', 0, 0, axis_index_groups=chips)  8.45 us
    all_to_all x1, starting transfers between devices, on_device(): columns = lax.all_to_all(columns, 'gy', 0, 0)  7.48 us
    all_to_all x1, starting transfers between devices, on_device(): entry_x = lax.all_to_all(entry_x, 'gx', 0, 0, axis_index_groups=chips)  6.41 us
    all_to_all x1, starting transfers between devices, on_device(): entry_y = lax.all_to_all(entry_y, 'gy', 0, 0)  5.61 us
  transfers between devices with their start and end apart: 5, of which 3 were waited for; matrix products, arithmetic and copies ran while one was open for 1% of the time, Pallas kernels for 33%

profile of v1, /device:TPU:2, one launch (start us, length us, event | category | flops | bytes accessed | tf_op | source)
XLA Modules:
  0.0 123.0 jit_solution(6087648605360754619)
XLA Ops:
  0.0 0.0 copy-start.2
  0.0 0.7 tile.16
  0.8 0.1 tile.17
  0.9 0.1 copy-done.2
  1.0 0.2 fusion
  1.1 0.1 pad.5.clone
  1.2 0.1 maximum_maximum_fusion
  1.3 1.0 copy.12
  2.3 0.0 copy-start.5
  2.3 15.3 %all-to-all-start = ((f32[16,24,256]{2,1,0:T(8,128)}), f32[16,24,256]{2,1,0:T(8,128)S(1)}, u32[]{:S(2)}, u32[]{:S(2)}) async-start(f32[16,24,256]{2,1,0:T(8,128)} %copy.12), calls=%async_computation | async-start | bytes 786432 | tf_op jit(solution)/shard_map/all_to_all | solution.py:208
  17.6 0.0 copy-done.5
  17.6 0.1 copy.13
  17.7 0.1 tile.19
  17.9 0.8 maximum_maximum_fusion.1
  18.7 22.7 %all-to-all-done.refs_0_ = f32[16,24,256]{2,1,0:T(8,128)S(1)} async-done(((f32[16,24,256]{2,1,0:T(8,128)}), f32[16,24,256]{2,1,0:T(8,128)S(1)}, u32[]{:S(2)}, u32[]{:S(2)}) %all-to-all-start) | async-done | bytes 393248 | tf_op jit(solution)/shard_map/all_to_all | solution.py:208
  41.4 7.5 %all-to-all-start.2 = ((f32[16,24,256]{2,1,0:T(8,128)}), f32[16,24,256]{2,1,0:T(8,128)S(1)}, u32[]{:S(2)}, u32[]{:S(2)}) async-start(f32[16,24,256]{2,1,0:T(8,128)} %maximum_maximum_fusion.1), calls=%async_computation.2 | async-start | bytes 786432 | tf_op jit(solution)/shard_map/all_to_all | solution.py:210
  48.9 1.9 %collective-permute-start = (f32[16,24,256]{2,1,0:T(8,128)S(1)}, f32[16,24,256]{2,1,0:T(8,128)S(1)}, u32[]{:S(2)}, u32[]{:S(2)}) collective-permute-start(f32[16,24,256]{2,1,0:T(8,128)S(1)} %all-to-all-done.refs_0_), channel_id=1, source_target_pairs={{0,1},{1,0},{2,3},{3,2},{4,5},{5,4},{6,7},{7,6},{8,9},{9,8},{10,11... | collective-permute-start | bytes 1179656 | tf_op jit(solution)/shard_map/ppermute | solution.py:211
  50.8 0.0 copy-start
  50.8 0.0 copy-start.1
  50.8 5.3 %all-to-all-done.2.refs_0_ = f32[16,24,256]{2,1,0:T(8,128)S(1)} async-done(((f32[16,24,256]{2,1,0:T(8,128)}), f32[16,24,256]{2,1,0:T(8,128)S(1)}, u32[]{:S(2)}, u32[]{:S(2)}) %all-to-all-start.2) | async-done | bytes 393248 | tf_op jit(solution)/shard_map/all_to_all | solution.py:210
  56.1 0.0 copy-done
  56.1 0.0 copy-done.1
  56.1 12.6 %line_paths.3 = f32[16,4,256]{2,1,0:T(4,128)} custom-call(s32[1]{0:T(128)} %bitcast.1.core_ref, s32[4]{0:T(128)S(1)} %copy-done, s32[4]{0:T(128)S(1)} %copy-done.1, f32[16,24,256]{2,1,0:T(8,128)S(1)} %all-to-all-done.2.refs_0_), custom_call_target="tpu_custom_call" | custom-call | flops 67108864 | bytes 393216 | tf_op jit(solution)/shard_map/line_paths/pallas_call | solution.py:130
  68.7 5.6 %all-to-all-start.3 = ((f32[16,4,256]{2,1,0:T(4,128)}), f32[16,4,256]{2,1,0:T(4,128)S(1)}, u32[]{:S(2)}, u32[]{:S(2)}) async-start(f32[16,4,256]{2,1,0:T(4,128)} %line_paths.3), calls=%async_computation.3 | async-start | bytes 131072 | tf_op jit(solution)/shard_map/all_to_all | solution.py:214
  74.4 0.0 collective-permute-done.refs_1_
  74.4 23.9 %line_paths.2 = f32[16,4,256]{2,1,0:T(4,128)} custom-call(s32[1]{0:T(128)} %bitcast.1.core_ref, s32[4]{0:T(128)S(1)} %copy-done, s32[4]{0:T(128)S(1)} %copy-done.1, f32[16,24,256]{2,1,0:T(8,128)S(1)} %all-to-all-done.refs_0_, f32[16,24,256]{2,1,0:T(8,128)S(1)} %collective-permute-done.refs_1_), custom_call_target="tpu_custom_call" | custom-call | flops 134217728 | bytes 786432 | tf_op jit(solution)/shard_map/line_paths/pallas_call | solution.py:130
  98.2 0.0 all-to-all-done.3.entry_ref
  98.2 0.0 copy-start.3
  98.2 0.6 copy-done.3
  98.9 6.4 %all-to-all-start.1 = ((f32[16,4,256]{2,1,0:T(4,128)}), f32[16,4,256]{2,1,0:T(4,128)S(1)}, u32[]{:S(2)}, u32[]{:S(2)}) async-start(f32[16,4,256]{2,1,0:T(4,128)} %line_paths.2), calls=%async_computation.1 | async-start | bytes 131072 | tf_op jit(solution)/shard_map/all_to_all | solution.py:216
  105.3 4.3 %block_paths.2.refs_0_ = f32[16,16,256]{2,1,0:T(8,128)} custom-call(s32[1]{0:T(128)} %bitcast.2.quarter_ref, s32[4]{0:T(128)} %small_ref.7, f32[16,4,256]{2,1,0:T(4,128)} %copy-done.3, s32[16,16,256]{2,1,0:T(8,128)} %cost_ref.3), custom_call_target="tpu_custom_call" | custom-call | flops 13107200 | bytes 1048576 | tf_op jit(solution)/shard_map/block_paths/pallas_call | solution.py:183
  109.6 8.4 %all-to-all-done.1.entry_ref = f32[16,4,256]{2,1,0:T(4,128)S(1)} async-done(((f32[16,4,256]{2,1,0:T(4,128)}), f32[16,4,256]{2,1,0:T(4,128)S(1)}, u32[]{:S(2)}, u32[]{:S(2)}) %all-to-all-start.1) | async-done | bytes 65568 | tf_op jit(solution)/shard_map/all_to_all | solution.py:216
  118.0 0.0 copy-start.4
  118.0 0.6 copy-done.4
  118.6 4.4 %block_paths.3 = f32[16,16,256]{2,1,0:T(8,128)} custom-call(s32[1]{0:T(128)} %bitcast.quarter_ref, s32[4]{0:T(128)} %small_ref.7, f32[16,4,256]{2,1,0:T(4,128)} %copy-done.4, s32[16,16,256]{2,1,0:T(8,128)} %cost_ref.3, f32[16,16,256]{2,1,0:T(8,128)} %block_paths.2.refs_0_), custom_call_target="tpu_custom_call" | custom-call | flops 13107200 | bytes 1048576 | tf_op jit(solution)/shard_map/block_paths/pallas_call | solution.py:183
  (2 shorter events, 0.0 us)
Async XLA Ops:
  0.0 1.0 copy-start.2
  2.3 15.3 %copy-start.5 = (f32[16,16]{1,0:T(8,128)S(1)}, f32[16,16]{1,0:T(8,128)}, u32[]{:S(2)}) copy-start(f32[16,16]{1,0:T(8,128)} %param.5) | copy-start | bytes 3076
  2.3 39.1 %all-to-all-start = ((f32[16,24,256]{2,1,0:T(8,128)}), f32[16,24,256]{2,1,0:T(8,128)S(1)}, u32[]{:S(2)}, u32[]{:S(2)}) async-start(f32[16,24,256]{2,1,0:T(8,128)} %copy.12), calls=%async_computation | async-start | bytes 786432 | tf_op jit(solution)/shard_map/all_to_all | solution.py:208
  41.4 14.7 %all-to-all-start.2 = ((f32[16,24,256]{2,1,0:T(8,128)}), f32[16,24,256]{2,1,0:T(8,128)S(1)}, u32[]{:S(2)}, u32[]{:S(2)}) async-start(f32[16,24,256]{2,1,0:T(8,128)} %maximum_maximum_fusion.1), calls=%async_computation.2 | async-start | bytes 786432 | tf_op jit(solution)/shard_map/all_to_all | solution.py:210
  48.9 25.5 %collective-permute-start = (f32[16,24,256]{2,1,0:T(8,128)S(1)}, f32[16,24,256]{2,1,0:T(8,128)S(1)}, u32[]{:S(2)}, u32[]{:S(2)}) collective-permute-start(f32[16,24,256]{2,1,0:T(8,128)S(1)} %all-to-all-done.refs_0_), channel_id=1, source_target_pairs={{0,1},{1,0},{2,3},{3,2},{4,5},{5,4},{6,7},{7,6},{8,9},{9,8},{10,11... | collective-permute-start | bytes 1179656 | tf_op jit(solution)/shard_map/ppermute | solution.py:211
  50.8 5.3 %copy-start = (s32[4]{0:T(128)S(1)}, s32[4]{0:T(128)}, u32[]{:S(2)}) copy-start(s32[4]{0:T(128)} %small_ref.7) | copy-start | bytes 52
  50.8 5.3 %copy-start.1 = (s32[4]{0:T(128)S(1)}, s32[4]{0:T(128)}, u32[]{:S(2)}) copy-start(s32[4]{0:T(128)} %large_ref.3) | copy-start | bytes 52
  68.7 29.5 %all-to-all-start.3 = ((f32[16,4,256]{2,1,0:T(4,128)}), f32[16,4,256]{2,1,0:T(4,128)S(1)}, u32[]{:S(2)}, u32[]{:S(2)}) async-start(f32[16,4,256]{2,1,0:T(4,128)} %line_paths.3), calls=%async_computation.3 | async-start | bytes 131072 | tf_op jit(solution)/shard_map/all_to_all | solution.py:214
  98.2 0.6 copy-start.3
  98.9 19.2 %all-to-all-start.1 = ((f32[16,4,256]{2,1,0:T(4,128)}), f32[16,4,256]{2,1,0:T(4,128)S(1)}, u32[]{:S(2)}, u32[]{:S(2)}) async-start(f32[16,4,256]{2,1,0:T(4,128)} %line_paths.2), calls=%async_computation.1 | async-start | bytes 131072 | tf_op jit(solution)/shard_map/all_to_all | solution.py:216
  118.0 0.6 copy-start.4

commit v2 on v1

--- a/solution.py
+++ b/solution.py
@@ -12,7 +12,7 @@
 OUT_SCALE = 1.0 / 256.0
 LANES = 128
 TILES = 32
-ROWS = 24
+ROWS = 40
 
 
 def adaptive(penalty_one, penalty_two, step_diff):
@@ -27,8 +27,9 @@
                 place = 2 * z + core if which == 0 else 2 * z + 1 - core
             else:
                 place = z
-            scr[place] = source[z, 0:16, :].astype(jnp.bfloat16)
-            img[pl.ds(place, 1), :] = source[z, 16:17, 0:LANES]
+            scr[place, :, 0:LANES] = source[z, 0:16, :].astype(jnp.bfloat16)
+            scr[place, :, LANES:] = source[z, 16:32, :].astype(jnp.bfloat16)
+            img[pl.ds(place, 1), :] = source[z, 32:33, :]
 
 
 def path_kernel(blocks, first, two, core_ref, small_ref, large_ref, *refs):
@@ -193,9 +194,26 @@
 
 
 def message(cost, image):
-    wide = jnp.tile(image, (1, 16))[:, None, :]
-    empty = jnp.zeros((16, ROWS - 17, 256), jnp.float32)
-    return jnp.concatenate([cost.astype(jnp.float32), wide, empty], 1)
+    wide = jnp.tile(image, (1, LANES // 16))[:, None, :]
+    empty = jnp.zeros((16, ROWS - 33, LANES), jnp.float32)
+    cost = cost.astype(jnp.float32)
+    return jnp.concatenate([cost[:, :, :LANES], cost[:, :, LANES:], wide, empty], 1)
+
+
+def after_kernel(value_ref, earlier_ref, out_ref):
+    pass
+
+
+def after(value, earlier):
+    anywhere = pl.BlockSpec(memory_space=pl.ANY)
+    return pl.pallas_call(
+        after_kernel,
+        out_shape=jax.ShapeDtypeStruct(value.shape, value.dtype),
+        in_specs=[anywhere] * 2,
+        out_specs=anywhere,
+        input_output_aliases={0: 0},
+        name="after",
+    )(value, earlier)
 
 
 def on_device(cost_volume, left_image, p_small, p_large):
@@ -204,13 +222,15 @@
     chips = [[2 * z + c for z in range(16)] for c in range(2)]
     swap = [(i, i ^ 1) for i in range(32)]
 
+    columns = message(jnp.transpose(cost_volume, (1, 0, 2)), left_image.T)
     lines = message(cost_volume, left_image)
+    columns = lax.all_to_all(columns, "gy", 0, 0)
+    lines = after(lines, columns[:1, :8])
     lines = lax.all_to_all(lines, "gx", 0, 0, axis_index_groups=chips)
-    columns = message(jnp.transpose(cost_volume, (1, 0, 2)), left_image.T)
-    columns = lax.all_to_all(columns, "gy", 0, 0)
+    entry_y = path_states(16, 2, False, core, p_small, p_large, columns)
+    lines = after(lines, entry_y)
     others = lax.ppermute(lines, "gx", swap)
 
-    entry_y = path_states(16, 2, False, core, p_small, p_large, columns)
     entry_y = lax.all_to_all(entry_y, "gy", 0, 0)
     entry_x = path_states(32, 0, True, core, p_small, p_large, lines, others)
     entry_x = lax.all_to_all(entry_x, "gx", 0, 0, axis_index_groups=chips)

time: 124 us -> 111 us (0.90)
  waiting for transfers between devices: 36.5 us -> 20.8 us
  local copies, waits for them, and re-layouts: 3.47 us -> 6.05 us
    all_to_all x1, waiting for transfers between devices: 22.7 us -> 6.17 us  [on_device(): lines = lax.all_to_all(lines, 'gx', 0, 0, axis_index_groups=chips)]
    unnamed x12 -> x14, local copies, waits for them, and re-layouts: 1.36 us -> 4.26 us
    all_to_all x1, starting transfers between devices: 7.48 us -> 9.26 us  [on_device(): columns = lax.all_to_all(columns, 'gy', 0, 0)]
    all_to_all x1, starting transfers between devices: 15.3 us -> 13.7 us  [on_device(): lines = lax.all_to_all(lines, 'gx', 0, 0, axis_index_groups=chips)]
  transfers between devices with their start and end apart: 5 -> 5, of which waited for: 3 -> 3; matrix products, arithmetic and copies ran while one was open for 1% -> 1% of each run, Pallas kernels for 33% -> 37%
where the time goes in v2:
time: 111 us
  Pallas kernels  45.2 us (41%)
  starting transfers between devices  36.6 us (33%)
  waiting for transfers between devices  20.8 us (19%)
  local copies, waits for them, and re-layouts  6.05 us (5%)
  other arithmetic  2.03 us (2%)
    pallas_call x2, Pallas kernels, path_states(): pl.pallas_call(partial(path_kernel, blocks, first, two), out_shape=jax.Sh...  36.5 us
    all_to_all x1, starting transfers between devices, on_device(): lines = lax.all_to_all(lines, 'gx', 0, 0, axis_index_groups=chips)  13.7 us
    all_to_all x1, starting transfers between devices, on_device(): columns = lax.all_to_all(columns, 'gy', 0, 0)  9.26 us
    pallas_call x2, Pallas kernels, replay(): pl.pallas_call(partial(replay_kernel, first, across), out_shape=jax.Shape...  8.67 us
    all_to_all x1, waiting for transfers between devices, on_device(): entry_x = lax.all_to_all(entry_x, 'gx', 0, 0, axis_index_groups=chips)  8.6 us
    all_to_all x1, waiting for transfers between devices, on_device(): lines = lax.all_to_all(lines, 'gx', 0, 0, axis_index_groups=chips)  6.17 us
    all_to_all x1, starting transfers between devices, on_device(): entry_x = lax.all_to_all(entry_x, 'gx', 0, 0, axis_index_groups=chips)  6.1 us
    all_to_all x1, waiting for transfers between devices, on_device(): columns = lax.all_to_all(columns, 'gy', 0, 0)  6.03 us
  transfers between devices with their start and end apart: 5, of which 3 were waited for; matrix products, arithmetic and copies ran while one was open for 1% of the time, Pallas kernels for 37%

profile of v2, /device:TPU:2, one launch (start us, length us, event | category | flops | bytes accessed | tf_op | source)
XLA Modules:
  0.0 110.8 jit_solution(13104820637894788084)
XLA Ops:
  0.0 1.1 fusion
  1.1 0.0 copy-start.6
  1.1 0.7 copy-done.6
  1.8 0.1 copy.10
  1.9 0.1 tile.19
  2.0 0.1 pad.7.clone
  2.1 0.8 maximum_maximum_fusion.1
  2.9 9.3 %all-to-all-start = ((f32[16,40,128]{2,1,0:T(8,128)}), f32[16,40,128]{2,1,0:T(8,128)S(1)}, u32[]{:S(2)}, u32[]{:S(2)}) async-start(f32[16,40,128]{2,1,0:T(8,128)} %maximum_maximum_fusion.1), calls=%async_computation | async-start | bytes 655360 | tf_op jit(solution)/shard_map/all_to_all | solution.py:227
  12.2 0.1 tile.17
  12.3 0.1 maximum_maximum_fusion
  12.4 0.8 copy.9.value_ref
  13.2 6.0 %all-to-all-done.refs_0_ = f32[16,40,128]{2,1,0:T(8,128)S(1)} async-done(((f32[16,40,128]{2,1,0:T(8,128)}), f32[16,40,128]{2,1,0:T(8,128)S(1)}, u32[]{:S(2)}, u32[]{:S(2)}) %all-to-all-start) | async-done | bytes 327712 | tf_op jit(solution)/shard_map/all_to_all | solution.py:227
  19.2 0.6 slice.24.earlier_ref
  19.8 13.7 %all-to-all-start.1 = ((f32[16,40,128]{2,1,0:T(8,128)}), f32[16,40,128]{2,1,0:T(8,128)S(1)}, u32[]{:S(2)}, u32[]{:S(2)}) async-start(f32[16,40,128]{2,1,0:T(8,128)} %after.2), calls=%async_computation.1 | async-start | bytes 655360 | tf_op jit(solution)/shard_map/all_to_all | solution.py:229
  33.5 0.0 copy-start.2
  33.5 0.0 copy-start.3
  33.6 0.6 copy-done.2
  34.2 0.0 copy-done.3
  34.2 12.6 %line_paths.2.earlier_ref = f32[16,4,256]{2,1,0:T(4,128)} custom-call(s32[1]{0:T(128)} %bitcast.1.core_ref, s32[4]{0:T(128)S(1)} %copy-done.2, s32[4]{0:T(128)S(1)} %copy-done.3, f32[16,40,128]{2,1,0:T(8,128)S(1)} %all-to-all-done.refs_0_), custom_call_target="tpu_custom_call" | custom-call | flops 67108864 | bytes 393216 | tf_op jit(solution)/shard_map/line_paths/pallas_call | solution.py:131
  46.8 6.2 %all-to-all-done.1.value_ref = f32[16,40,128]{2,1,0:T(8,128)S(1)} async-done(((f32[16,40,128]{2,1,0:T(8,128)}), f32[16,40,128]{2,1,0:T(8,128)S(1)}, u32[]{:S(2)}, u32[]{:S(2)}) %all-to-all-start.1) | async-done | bytes 327712 | tf_op jit(solution)/shard_map/all_to_all | solution.py:229
  53.0 0.0 copy-start
  53.0 0.7 copy-done
  53.7 1.9 %collective-permute-start = (f32[16,40,128]{2,1,0:T(8,128)}, f32[16,40,128]{2,1,0:T(8,128)S(1)}, u32[]{:S(2)}, u32[]{:S(2)}) collective-permute-start(f32[16,40,128]{2,1,0:T(8,128)} %after.3.refs_0_), channel_id=1, source_target_pairs={{0,1},{1,0},{2,3},{3,2},{4,5},{5,4},{6,7},{7,6},{8,9},{9,8},{10,11... | collective-permute-start | bytes 983048 | tf_op jit(solution)/shard_map/ppermute | solution.py:232
  55.7 5.7 %all-to-all-start.3 = ((f32[16,4,256]{2,1,0:T(4,128)}), f32[16,4,256]{2,1,0:T(4,128)S(1)}, u32[]{:S(2)}, u32[]{:S(2)}) async-start(f32[16,4,256]{2,1,0:T(4,128)} %line_paths.2.earlier_ref), calls=%async_computation.3 | async-start | bytes 131072 | tf_op jit(solution)/shard_map/all_to_all | solution.py:234
  61.3 0.0 collective-permute-done.refs_1_
  61.3 0.0 copy-start.1
  61.3 1.0 copy-done.1
  62.3 23.9 %line_paths.3 = f32[16,4,256]{2,1,0:T(4,128)} custom-call(s32[1]{0:T(128)} %bitcast.1.core_ref, s32[4]{0:T(128)S(1)} %copy-done.2, s32[4]{0:T(128)S(1)} %copy-done.3, f32[16,40,128]{2,1,0:T(8,128)S(1)} %copy-done.1, f32[16,40,128]{2,1,0:T(8,128)S(1)} %collective-permute-done.refs_1_), custom_call_target="tpu_custom_call" | custom-call | flops 134217728 | bytes 786432 | tf_op jit(solution)/shard_map/line_paths/pallas_call | solution.py:131
  86.2 0.0 all-to-all-done.3.entry_ref
  86.2 0.0 copy-start.4
  86.2 0.6 copy-done.4
  86.8 6.1 %all-to-all-start.2 = ((f32[16,4,256]{2,1,0:T(4,128)}), f32[16,4,256]{2,1,0:T(4,128)S(1)}, u32[]{:S(2)}, u32[]{:S(2)}) async-start(f32[16,4,256]{2,1,0:T(4,128)} %line_paths.3), calls=%async_computation.2 | async-start | bytes 131072 | tf_op jit(solution)/shard_map/all_to_all | solution.py:236
  92.9 4.3 %block_paths.2.refs_0_ = f32[16,16,256]{2,1,0:T(8,128)} custom-call(s32[1]{0:T(128)} %bitcast.4.quarter_ref, s32[4]{0:T(128)} %small_ref.7, f32[16,4,256]{2,1,0:T(4,128)} %copy-done.4, s32[16,16,256]{2,1,0:T(8,128)} %cost_ref.3), custom_call_target="tpu_custom_call" | custom-call | flops 13107200 | bytes 1048576 | tf_op jit(solution)/shard_map/block_paths/pallas_call | solution.py:184
  97.2 8.6 %all-to-all-done.2.entry_ref = f32[16,4,256]{2,1,0:T(4,128)S(1)} async-done(((f32[16,4,256]{2,1,0:T(4,128)}), f32[16,4,256]{2,1,0:T(4,128)S(1)}, u32[]{:S(2)}, u32[]{:S(2)}) %all-to-all-start.2) | async-done | bytes 65568 | tf_op jit(solution)/shard_map/all_to_all | solution.py:236
  105.8 0.0 copy-start.5
  105.8 0.6 copy-done.5
  106.4 4.4 %block_paths.3 = f32[16,16,256]{2,1,0:T(8,128)} custom-call(s32[1]{0:T(128)} %bitcast.quarter_ref, s32[4]{0:T(128)} %small_ref.7, f32[16,4,256]{2,1,0:T(4,128)} %copy-done.5, s32[16,16,256]{2,1,0:T(8,128)} %cost_ref.3, f32[16,16,256]{2,1,0:T(8,128)} %block_paths.2.refs_0_), custom_call_target="tpu_custom_call" | custom-call | flops 13107200 | bytes 1048576 | tf_op jit(solution)/shard_map/block_paths/pallas_call | solution.py:184
  (7 shorter events, 0.1 us)
Async XLA Ops:
  1.1 0.7 copy-start.6
  2.9 16.3 %all-to-all-start = ((f32[16,40,128]{2,1,0:T(8,128)}), f32[16,40,128]{2,1,0:T(8,128)S(1)}, u32[]{:S(2)}, u32[]{:S(2)}) async-start(f32[16,40,128]{2,1,0:T(8,128)} %maximum_maximum_fusion.1), calls=%async_computation | async-start | bytes 655360 | tf_op jit(solution)/shard_map/all_to_all | solution.py:227
  19.8 33.2 %all-to-all-start.1 = ((f32[16,40,128]{2,1,0:T(8,128)}), f32[16,40,128]{2,1,0:T(8,128)S(1)}, u32[]{:S(2)}, u32[]{:S(2)}) async-start(f32[16,40,128]{2,1,0:T(8,128)} %after.2), calls=%async_computation.1 | async-start | bytes 655360 | tf_op jit(solution)/shard_map/all_to_all | solution.py:229
  33.5 0.7 copy-start.2
  33.5 0.7 copy-start.3
  53.0 0.7 copy-start
  53.7 7.6 %collective-permute-start = (f32[16,40,128]{2,1,0:T(8,128)}, f32[16,40,128]{2,1,0:T(8,128)S(1)}, u32[]{:S(2)}, u32[]{:S(2)}) collective-permute-start(f32[16,40,128]{2,1,0:T(8,128)} %after.3.refs_0_), channel_id=1, source_target_pairs={{0,1},{1,0},{2,3},{3,2},{4,5},{5,4},{6,7},{7,6},{8,9},{9,8},{10,11... | collective-permute-start | bytes 983048 | tf_op jit(solution)/shard_map/ppermute | solution.py:232
  55.7 30.5 %all-to-all-start.3 = ((f32[16,4,256]{2,1,0:T(4,128)}), f32[16,4,256]{2,1,0:T(4,128)S(1)}, u32[]{:S(2)}, u32[]{:S(2)}) async-start(f32[16,4,256]{2,1,0:T(4,128)} %line_paths.2.earlier_ref), calls=%async_computation.3 | async-start | bytes 131072 | tf_op jit(solution)/shard_map/all_to_all | solution.py:234
  61.3 1.0 copy-start.1
  86.2 0.6 copy-start.4
  86.8 19.0 %all-to-all-start.2 = ((f32[16,4,256]{2,1,0:T(4,128)}), f32[16,4,256]{2,1,0:T(4,128)S(1)}, u32[]{:S(2)}, u32[]{:S(2)}) async-start(f32[16,4,256]{2,1,0:T(4,128)} %line_paths.3), calls=%async_computation.2 | async-start | bytes 131072 | tf_op jit(solution)/shard_map/all_to_all | solution.py:236
  105.8 0.6 copy-start.5

commit v3 on v2

--- a/solution.py
+++ b/solution.py
@@ -33,7 +33,7 @@
 
 
 def path_kernel(blocks, first, two, core_ref, small_ref, large_ref, *refs):
-    sources, (out_ref, scr, img, ahead, back, costs, starts, states) = refs[:-8], refs[-8:]
+    sources, (out_ref, scr, img, ahead, back, costs, pick, starts, states) = refs[:-9], refs[-9:]
     groups = blocks // 4
     lane = lax.broadcasted_iota(jnp.int32, (8, LANES), 1)
     sub = lax.broadcasted_iota(jnp.int32, (8, LANES), 0)
@@ -70,59 +70,78 @@
         turned = lax.dot_general(
             order, pixels, (((1,), (1,)), ((), ())), preferred_element_type=jnp.float32
         )
-        costs[g] = turned.reshape(TILES, 8, LANES)
-
-    def lowest_of(level):
-        while len(level) > 1:
-            level = [jnp.minimum(level[i], level[i + 1]) for i in range(0, len(level), 2)]
-        lowest = level[0]
+        costs[g] = turned.astype(jnp.bfloat16)
+
+    mirror = jnp.where(lane < 64, 0, LANES - 1)
+    lane_in = lax.broadcasted_iota(jnp.int32, (LANES, LANES), 0)
+    lane_out = lax.broadcasted_iota(jnp.int32, (LANES, LANES), 1)
+
+    def build(i, nothing):
+        pick[i] = (lane_in == jnp.where(lane_out < 64, i, LANES - 1 - i)).astype(jnp.bfloat16)
+        return nothing
+
+    lax.fori_loop(0, 64, build, 0)
+
+    def across_sublanes(lowest):
         for shift in (4, 2, 1):
             lowest = jnp.minimum(lowest, pltpu.roll(lowest, shift, 0))
         return lowest
 
-    def segment(k, path):
-        lowest = lowest_of(path)
-        path = [x - lowest for x in path]
-        here = lane % 64 == k
-        for v in range(TILES):
-            starts[v] = jnp.where(here, path[v], starts[v])
-        g = k // 4
+    def halved(level):
+        return [jnp.minimum(level[i], level[i + 1]) for i in range(0, len(level), 2)]
+
+    def lowest_of(level):
+        while len(level) > 1:
+            level = halved(level)
+        return across_sublanes(level[0])
+
+    def segments(t, path):
+        path = list(path)
+        g = t // 2
+        base = 32 * (t % 2)
         penalty_two = jnp.where(
             forward,
             jnp.broadcast_to(ahead[pl.ds(g, 1), :], (8, LANES)),
             jnp.broadcast_to(back[pl.ds(groups - 1 - g, 1), :], (8, LANES)),
         )
-        base = 16 * (k % 4)
-        for j in range(16):
-            source = jnp.where(forward, base + j, 127 - base - j)
-            jump = jnp.take_along_axis(penalty_two, source, axis=1)
-            if j == 0:
-                highest = jump
-            else:
-                highest = lowest_of(path) + jump
-            raised = [x + penalty_one for x in path]
+        lowest = lowest_of(path)
+        ordered = penalty_one
+        for i in range(32):
+            if i % 16 == 0:
+                path = [x - lowest for x in path]
+                lowest = jnp.zeros_like(lowest)
+                here = lane % 64 == 2 * t + i // 16
+                for v in range(TILES):
+                    starts[v] = jnp.where(here, path[v], starts[v])
+            highest = lowest + jnp.take_along_axis(penalty_two, mirror ^ (base + i), axis=1)
+            cost = jnp.dot(costs[g], pick[base + i], preferred_element_type=jnp.float32)
+            cost = cost.reshape(TILES, 8, LANES)
+            raised = [x + ordered for x in path]
             below = jnp.where(sub == 0, FAR, pltpu.roll(raised[-1], 1, 0))
             above = jnp.where(sub == 7, FAR, pltpu.roll(raised[0], 7, 0))
             padded = [below, *raised, above]
-            path = [
-                jnp.minimum(
-                    jnp.minimum(path[v], jnp.minimum(padded[v], padded[v + 2])), highest
-                )
-                + jnp.take_along_axis(costs[g, v], source, axis=1)
-                for v in range(TILES)
+            near = [
+                jnp.minimum(path[v], jnp.minimum(padded[v], padded[v + 2])) for v in range(TILES)
             ]
+            path = [jnp.minimum(near[v], highest) + cost[v] for v in range(TILES)]
+            pairs = halved(path)
+            ordered = jnp.maximum(penalty_one, jnp.minimum(pairs[-1], -FAR))
+            lowest = lowest_of(pairs)
         return tuple(path)
 
     zero = jnp.zeros((8, LANES), jnp.float32)
-    lax.fori_loop(0, blocks, segment, (zero,) * TILES)
+    lax.fori_loop(0, blocks // 2, segments, (zero,) * TILES)
     states[...] = jnp.concatenate([starts[:, s, :] for s in range(8)], 0).T
     for z in range(16):
         block = 2 * z + core_ref[0] if two else z
-        out_ref[z, 0:1, :] = states[pl.ds(block, 1), :]
-        out_ref[z, 1:2, :] = states[pl.ds(64 + blocks - 1 - block, 1), :]
         fore, rear = ahead[pl.ds(block // 4, 1), :], back[pl.ds(block // 4, 1), :]
-        out_ref[z, 2:3, :] = jnp.concatenate([fore, fore], 1)
-        out_ref[z, 3:4, :] = jnp.concatenate([rear, rear], 1)
+        start, end = states[pl.ds(block, 1), :], states[pl.ds(64 + blocks - 1 - block, 1), :]
+        if two:
+            out_ref[z, 0:1, :] = jnp.concatenate([start, fore], 1)
+            out_ref[z, 1:2, :] = jnp.concatenate([end, rear], 1)
+        else:
+            out_ref[2 * z : 2 * z + 1, :] = jnp.concatenate([start, fore, fore], 1)
+            out_ref[2 * z + 1 : 2 * z + 2, :] = jnp.concatenate([end, rear, rear], 1)
 
 
 def path_states(blocks, first, two, core, p_small, p_large, *sources):
@@ -130,7 +149,7 @@
     vmem = pl.BlockSpec(memory_space=pltpu.VMEM)
     return pl.pallas_call(
         partial(path_kernel, blocks, first, two),
-        out_shape=jax.ShapeDtypeStruct((16, 4, 256), jnp.float32),
+        out_shape=jax.ShapeDtypeStruct((16, 2, 384) if two else (32, 512), jnp.float32),
         in_specs=[smem] * 3 + [vmem] * len(sources),
         out_specs=vmem,
         scratch_shapes=[
@@ -138,7 +157,8 @@
             pltpu.VMEM((blocks, LANES), jnp.float32),
             pltpu.VMEM((blocks // 4, LANES), jnp.float32),
             pltpu.VMEM((blocks // 4, LANES), jnp.float32),
-            pltpu.VMEM((blocks // 4, TILES, 8, LANES), jnp.float32),
+            pltpu.VMEM((blocks // 4, 256, LANES), jnp.bfloat16),
+            pltpu.VMEM((64, LANES, LANES), jnp.bfloat16),
             pltpu.VMEM((TILES, 8, LANES), jnp.float32),
             pltpu.VMEM((LANES, 256), jnp.float32),
         ],
@@ -154,28 +174,32 @@
     *so_far, out_ref = refs
     lane = lax.broadcasted_iota(jnp.int32, (16, 256), 1)
     shift = (LANES - 16 * quarter_ref[0]) % LANES
-    paths = [entry_ref[:, i, :] for i in range(2)]
-    jumps = [pltpu.roll(entry_ref[:, 2 + i, 0:LANES], shift, 1) for i in range(2)]
+    paths = [entry_ref[:, i, 0:256] for i in range(2)]
+    jumps = [pltpu.roll(entry_ref[:, i, 256:], shift, 1) for i in range(2)]
     small = [small_ref[first + i].astype(jnp.float32) for i in range(2)]
+    lowest = [jnp.min(path, axis=1, keepdims=True) for path in paths]
     for j in range(16):
         for i, at in enumerate((j, 15 - j)):
             path = paths[i]
-            lowest = jnp.min(path, axis=1, keepdims=True)
+            cost = (cost_ref[:, at, :] if across else cost_ref[at]).astype(jnp.float32)
             below = jnp.where(lane == 0, FAR, pltpu.roll(path, 1, 1))
             above = jnp.where(lane == 255, FAR, pltpu.roll(path, 255, 1))
-            chosen = jnp.minimum(path, jnp.minimum(below, above) + small[i])
-            chosen = jnp.minimum(chosen, lowest + jumps[i][:, at : at + 1])
-            cost = cost_ref[:, at, :] if across else cost_ref[at]
-            path = cost.astype(jnp.float32) + chosen - lowest
+            near = jnp.minimum(path, jnp.minimum(below, above) + small[i]) + cost
+            highest = lowest[i] + jumps[i][:, at : at + 1]
+            path = jnp.minimum(near, highest + cost)
+            value = path - lowest[i]
+            lowest[i] = jnp.minimum(
+                jnp.min(near, axis=1, keepdims=True),
+                highest + jnp.min(cost, axis=1, keepdims=True),
+            )
             paths[i] = path
             here = (slice(None), at) if across else (at,)
             seen = j >= 8
-            if across:
-                value = path if seen else path + so_far[0][here]
-                value = value + out_ref[here] if seen else value
-                out_ref[here] = value * OUT_SCALE if seen else value
-            else:
-                out_ref[here] = path + out_ref[here] if seen else path
+            if seen:
+                value = value + out_ref[here]
+            elif across:
+                value = value + so_far[0][here]
+            out_ref[here] = value * OUT_SCALE if across and seen else value
 
 
 def replay(first, across, quarter, p_small, entry, cost, *so_far):
@@ -200,20 +224,20 @@
     return jnp.concatenate([cost[:, :, :LANES], cost[:, :, LANES:], wide, empty], 1)
 
 
-def after_kernel(value_ref, earlier_ref, out_ref):
+def together_kernel(*refs):
     pass
 
 
-def after(value, earlier):
+def together(first, second):
     anywhere = pl.BlockSpec(memory_space=pl.ANY)
     return pl.pallas_call(
-        after_kernel,
-        out_shape=jax.ShapeDtypeStruct(value.shape, value.dtype),
+        together_kernel,
+        out_shape=[jax.ShapeDtypeStruct(x.shape, x.dtype) for x in (first, second)],
         in_specs=[anywhere] * 2,
-        out_specs=anywhere,
-        input_output_aliases={0: 0},
-        name="after",
-    )(value, earlier)
+        out_specs=[anywhere] * 2,
+        input_output_aliases={0: 0, 1: 1},
+        name="together",
+    )(first, second)
 
 
 def on_device(cost_volume, left_image, p_small, p_large):
@@ -225,13 +249,14 @@
     columns = message(jnp.transpose(cost_volume, (1, 0, 2)), left_image.T)
     lines = message(cost_volume, left_image)
     columns = lax.all_to_all(columns, "gy", 0, 0)
-    lines = after(lines, columns[:1, :8])
+    lines, columns = together(lines, columns)
     lines = lax.all_to_all(lines, "gx", 0, 0, axis_index_groups=chips)
     entry_y = path_states(16, 2, False, core, p_small, p_large, columns)
-    lines = after(lines, entry_y)
+    lines, entry_y = together(lines, entry_y)
     others = lax.ppermute(lines, "gx", swap)
 
-    entry_y = lax.all_to_all(entry_y, "gy", 0, 0)
+    entry_y = lax.all_gather(entry_y, "gy", axis=0, tiled=True).reshape(16, 32, 512)
+    entry_y = lax.dynamic_slice(entry_y, (0, 2 * index_y, 0), (16, 2, 384))
     entry_x = path_states(32, 0, True, core, p_small, p_large, lines, others)
     entry_x = lax.all_to_all(entry_x, "gx", 0, 0, axis_index_groups=chips)
 

time: 111 us -> 130 us (1.17)
  the two profiles are of different devices: /device:TPU:2 before, /device:TPU:32 now
where the time goes in v3:
time: 130 us; the launch traced here: 129 us
  Pallas kernels  41 us (32%)
  waiting for transfers between devices  34.6 us (27%)
  starting transfers between devices  31.1 us (24%)
  between operations  13.5 us (10%)
  local copies, waits for them, and re-layouts  7.08 us (5%)
  other arithmetic  2.06 us (2%)
    pallas_call x2, Pallas kernels, path_states(): pl.pallas_call(partial(path_kernel, blocks, first, two), out_shape=jax.Sh...  32 us
    all_gather x1, waiting for transfers between devices, on_device(): lax.all_gather(entry_y, 'gy', axis=0, tiled=True).reshape(16, 32, 512)  18.3 us
    all_to_all x1, starting transfers between devices, on_device(): lines = lax.all_to_all(lines, 'gx', 0, 0, axis_index_groups=chips)  15.3 us
    pallas_call x2, Pallas kernels, replay(): pl.pallas_call(partial(replay_kernel, first, across), out_shape=jax.Shape...  9.02 us
    all_to_all x1, waiting for transfers between devices, on_device(): columns = lax.all_to_all(columns, 'gy', 0, 0)  8.11 us
    all_to_all x1, starting transfers between devices, on_device(): columns = lax.all_to_all(columns, 'gy', 0, 0)  7.03 us
    all_to_all x1, starting transfers between devices, on_device(): entry_x = lax.all_to_all(entry_x, 'gx', 0, 0, axis_index_groups=chips)  6.78 us
    all_to_all x1, waiting for transfers between devices, on_device(): lines = lax.all_to_all(lines, 'gx', 0, 0, axis_index_groups=chips)  6.32 us
  transfers between devices with their start and end apart: 5, of which 4 were waited for; matrix products, arithmetic and copies ran while one was open for 2% of the time, Pallas kernels for 28%

profile of v3, /device:TPU:32, one launch (start us, length us, event | category | flops | bytes accessed | tf_op | source)
XLA Modules:
  0.0 129.4 jit_solution(227200282376881223)
XLA Ops:
  6.5 0.0 copy-start.8
  6.5 1.1 fusion
  7.7 0.0 copy-done.8
  7.7 0.1 copy.12
  7.7 0.1 tile.19
  7.9 0.1 pad.7.clone
  8.0 0.8 maximum_maximum_fusion.1
  8.8 7.0 %all-to-all-start = ((f32[16,40,128]{2,1,0:T(8,128)}), f32[16,40,128]{2,1,0:T(8,128)S(1)}, u32[]{:S(2)}, u32[]{:S(2)}) async-start(f32[16,40,128]{2,1,0:T(8,128)} %maximum_maximum_fusion.1), calls=%async_computation | async-start | bytes 655360 | tf_op jit(solution)/shard_map/all_to_all | solution.py:251
  15.9 0.1 tile.17
  16.0 0.1 maximum_maximum_fusion
  16.1 0.8 copy.11.refs_0_
  16.9 8.1 %all-to-all-done.refs_1_ = f32[16,40,128]{2,1,0:T(8,128)S(1)} async-done(((f32[16,40,128]{2,1,0:T(8,128)}), f32[16,40,128]{2,1,0:T(8,128)S(1)}, u32[]{:S(2)}, u32[]{:S(2)}) %all-to-all-start) | async-done | bytes 327712 | tf_op jit(solution)/shard_map/all_to_all | solution.py:251
  25.0 0.0 copy-start.2
  25.0 0.7 copy-done.2
  25.7 0.0 copy-start.3
  25.7 15.3 %all-to-all-start.1 = ((f32[16,40,128]{2,1,0:T(8,128)}), f32[16,40,128]{2,1,0:T(8,128)S(1)}, u32[]{:S(2)}, u32[]{:S(2)}) async-start(f32[16,40,128]{2,1,0:T(8,128)} %get-tuple-element.9), calls=%async_computation.1 | async-start | bytes 655360 | tf_op jit(solution)/shard_map/all_to_all | solution.py:253
  41.1 0.0 all-gather.2.cloned.1.call-start
  41.1 0.0 copy-start.5
  41.1 0.0 copy-start.6
  41.2 0.0 copy-done.3
  41.2 0.6 copy-done.5
  41.8 0.0 copy-done.6
  41.8 10.9 %line_paths.2.refs_1_ = f32[32,512]{1,0:T(8,128)S(1)} custom-call(s32[1]{0:T(128)} %bitcast.1.core_ref, s32[4]{0:T(128)S(1)} %copy-done.5, s32[4]{0:T(128)S(1)} %copy-done.6, f32[16,40,128]{2,1,0:T(8,128)S(1)} %copy-done.3), custom_call_target="tpu_custom_call" | custom-call | flops 67108864 | bytes 393216 | tf_op jit(solution)/shard_map/line_paths/pallas_call | solution.py:150
  52.7 0.0 copy-start.4
  52.7 0.6 copy-done.4
  53.3 6.3 %all-to-all-done.1.refs_0_ = f32[16,40,128]{2,1,0:T(8,128)S(1)} async-done(((f32[16,40,128]{2,1,0:T(8,128)}), f32[16,40,128]{2,1,0:T(8,128)S(1)}, u32[]{:S(2)}, u32[]{:S(2)}) %all-to-all-start.1) | async-done | bytes 327712 | tf_op jit(solution)/shard_map/all_to_all | solution.py:253
  59.6 0.0 copy-start
  59.6 0.7 copy-done
  60.4 0.0 all-gather.2.cloned.1.call-update
  60.4 1.9 %collective-permute-start = (f32[16,40,128]{2,1,0:T(8,128)}, f32[16,40,128]{2,1,0:T(8,128)S(1)}, u32[]{:S(2)}, u32[]{:S(2)}) collective-permute-start(f32[16,40,128]{2,1,0:T(8,128)} %get-tuple-element.11.refs_0_), channel_id=1, source_target_pairs={{0,1},{1,0},{2,3},{3,2},{4,5},{5,4},{6,7},{7,6},{8,9},{9,8},{10,11... | collective-permute-start | bytes 983048 | tf_op jit(solution)/shard_map/ppermute | solution.py:256
  62.3 1.8 %collective-permute-done.refs_1_ = f32[16,40,128]{2,1,0:T(8,128)S(1)} collective-permute-done((f32[16,40,128]{2,1,0:T(8,128)}, f32[16,40,128]{2,1,0:T(8,128)S(1)}, u32[]{:S(2)}, u32[]{:S(2)}) %collective-permute-start) | collective-permute-done | bytes 327712 | tf_op jit(solution)/shard_map/ppermute | solution.py:256
  64.1 0.0 copy-start.1
  64.1 1.0 copy-done.1
  65.1 21.1 %line_paths.3 = f32[16,2,384]{2,1,0:T(2,128)} custom-call(s32[1]{0:T(128)} %bitcast.1.core_ref, s32[4]{0:T(128)S(1)} %copy-done.5, s32[4]{0:T(128)S(1)} %copy-done.6, f32[16,40,128]{2,1,0:T(8,128)S(1)} %copy-done.1, f32[16,40,128]{2,1,0:T(8,128)S(1)} %collective-permute-done.refs_1_), custom_call_target="tpu_custom_call" | custom-call | flops 134217728 | bytes 786432 | tf_op jit(solution)/shard_map/line_paths/pallas_call | solution.py:150
  86.2 6.8 %all-to-all-start.2 = ((f32[16,2,384]{2,1,0:T(2,128)}), f32[16,2,384]{2,1,0:T(2,128)S(1)}, u32[]{:S(2)}, u32[]{:S(2)}) async-start(f32[16,2,384]{2,1,0:T(2,128)} %line_paths.3), calls=%async_computation.2 | async-start | bytes 98304 | tf_op jit(solution)/shard_map/all_to_all | solution.py:261
  93.0 18.3 %all-gather.2.cloned.1.call-done = f32[512,512]{1,0:T(8,128)} async-done(((f32[32,512]{1,0:T(8,128)}), f32[512,512]{1,0:T(8,128)}) %all-gather.2.cloned.1.call-update) | async-done | bytes 1048592 | tf_op jit(solution)/shard_map/all_gather | solution.py:258
  111.3 1.6 %constant_dynamic-slice_fusion.entry_ref = f32[16,2,384]{2,1,0:T(2,128)} fusion(f32[16,32,512]{2,1,0:T(8,128)} %bitcast.8, s32[]{:T(128)S(6)} %select_n.21), kind=kLoop, calls=%fused_computation.3 | loop fusion | bytes 98308 | tf_op jit(solution)/shard_map/dynamic_slice | solution.py:259
  112.9 4.4 %block_paths.2.refs_0_ = f32[16,16,256]{2,1,0:T(8,128)} custom-call(s32[1]{0:T(128)} %bitcast.4.quarter_ref, s32[4]{0:T(128)} %small_ref.7, f32[16,2,384]{2,1,0:T(2,128)} %constant_dynamic-slice_fusion.entry_ref, s32[16,16,256]{2,1,0:T(8,128)} %cost_ref.3), custom_call_target="tpu_custom_call" | custom-call | flops 13107200 | bytes 1048576 | tf_op jit(solution)/shard_map/block_paths/pallas_call | solution.py:208
  117.3 0.0 all-to-all-done.2.entry_ref
  117.3 0.0 copy-start.7
  117.3 0.6 copy-done.7
  117.9 4.6 %block_paths.3 = f32[16,16,256]{2,1,0:T(8,128)} custom-call(s32[1]{0:T(128)} %bitcast.quarter_ref, s32[4]{0:T(128)} %small_ref.7, f32[16,2,384]{2,1,0:T(2,128)} %copy-done.7, s32[16,16,256]{2,1,0:T(8,128)} %cost_ref.3, f32[16,16,256]{2,1,0:T(8,128)} %block_paths.2.refs_0_), custom_call_target="tpu_custom_call" | custom-call | flops 13107200 | bytes 1048576 | tf_op jit(solution)/shard_map/block_paths/pallas_call | solution.py:208
  (7 shorter events, 0.1 us)
Async XLA Ops:
  6.5 1.1 copy-start.8
  8.8 16.2 %all-to-all-start = ((f32[16,40,128]{2,1,0:T(8,128)}), f32[16,40,128]{2,1,0:T(8,128)S(1)}, u32[]{:S(2)}, u32[]{:S(2)}) async-start(f32[16,40,128]{2,1,0:T(8,128)} %maximum_maximum_fusion.1), calls=%async_computation | async-start | bytes 655360 | tf_op jit(solution)/shard_map/all_to_all | solution.py:251
  25.0 0.7 copy-start.2
  25.7 15.4 %copy-start.3 = (f32[16,40,128]{2,1,0:T(8,128)S(1)}, f32[16,40,128]{2,1,0:T(8,128)}, u32[]{:S(2)}) copy-start(f32[16,40,128]{2,1,0:T(8,128)} %get-tuple-element.10.refs_0_) | copy-start | bytes 983044
  25.7 33.9 %all-to-all-start.1 = ((f32[16,40,128]{2,1,0:T(8,128)}), f32[16,40,128]{2,1,0:T(8,128)S(1)}, u32[]{:S(2)}, u32[]{:S(2)}) async-start(f32[16,40,128]{2,1,0:T(8,128)} %get-tuple-element.9), calls=%async_computation.1 | async-start | bytes 655360 | tf_op jit(solution)/shard_map/all_to_all | solution.py:253
  41.1 70.2 %all-gather.2.cloned.1.call-start = ((), (), s32[]{:S(2)}) async-start(), calls=%async_computation.3 | async-start | bytes 1114112 | tf_op jit(solution)/shard_map/all_gather | solution.py:258
  41.1 0.7 copy-start.5
  41.1 0.7 copy-start.6
  52.7 0.6 copy-start.4
  59.6 0.7 copy-start
  60.4 3.7 %collective-permute-start = (f32[16,40,128]{2,1,0:T(8,128)}, f32[16,40,128]{2,1,0:T(8,128)S(1)}, u32[]{:S(2)}, u32[]{:S(2)}) collective-permute-start(f32[16,40,128]{2,1,0:T(8,128)} %get-tuple-element.11.refs_0_), channel_id=1, source_target_pairs={{0,1},{1,0},{2,3},{3,2},{4,5},{5,4},{6,7},{7,6},{8,9},{9,8},{10,11... | collective-permute-start | bytes 983048 | tf_op jit(solution)/shard_map/ppermute | solution.py:256
  64.1 1.0 copy-start.1
  86.2 31.1 %all-to-all-start.2 = ((f32[16,2,384]{2,1,0:T(2,128)}), f32[16,2,384]{2,1,0:T(2,128)S(1)}, u32[]{:S(2)}, u32[]{:S(2)}) async-start(f32[16,2,384]{2,1,0:T(2,128)} %line_paths.3), calls=%async_computation.2 | async-start | bytes 98304 | tf_op jit(solution)/shard_map/all_to_all | solution.py:261
  117.3 0.6 copy-start.7
Sparse Core Ops, SparseCore 0:
  60.5 50.7 all-gather.1

commit v4 on v3

--- a/solution.py
+++ b/solution.py
@@ -19,11 +19,10 @@
     return penalty_one + (penalty_two - penalty_one) / (1.0 + GRADIENT_GAIN * jnp.abs(step_diff))
 
 
-def gather_costs(blocks, two, core_ref, sources, scr, img):
+def gather_costs(blocks, two, core, sources, scr, img):
     for z in range(blocks // len(sources)):
         for which, source in enumerate(sources):
             if two:
-                core = core_ref[0]
                 place = 2 * z + core if which == 0 else 2 * z + 1 - core
             else:
                 place = z
@@ -32,12 +31,12 @@
             img[pl.ds(place, 1), :] = source[z, 32:33, :]
 
 
-def path_kernel(blocks, first, two, core_ref, small_ref, large_ref, *refs):
-    sources, (out_ref, scr, img, ahead, back, costs, pick, starts, states) = refs[:-9], refs[-9:]
+def path_kernel(blocks, first, two, numbers_ref, *refs):
+    sources, (out_ref, scr, img, ahead, back, costs, pick, ready, starts, states) = refs[:-10], refs[-10:]
     groups = blocks // 4
     lane = lax.broadcasted_iota(jnp.int32, (8, LANES), 1)
     sub = lax.broadcasted_iota(jnp.int32, (8, LANES), 0)
-    gather_costs(blocks, two, core_ref, sources, scr, img)
+    gather_costs(blocks, two, numbers_ref[8], sources, scr, img)
 
     place, row = lane[:groups] % 64, sub[:groups]
     line = img[pl.ds(0, groups, stride=4), :]
@@ -49,8 +48,8 @@
     after = pltpu.roll(line, LANES - 1, 1)
     wrapped = jnp.concatenate([after[1:], after[:1]], 0)
     after = jnp.where(place == 63, jnp.where(row == groups - 1, 0.0, wrapped), after)
-    small = [small_ref[first + i].astype(jnp.float32) for i in range(2)]
-    large = [large_ref[first + i].astype(jnp.float32) for i in range(2)]
+    small = [numbers_ref[first + i].astype(jnp.float32) for i in range(2)]
+    large = [numbers_ref[4 + first + i].astype(jnp.float32) for i in range(2)]
     ahead[...] = adaptive(small[0], large[0], line - before)
     back[...] = adaptive(small[1], large[1], line - after)
     forward = lane < 64
@@ -94,6 +93,12 @@
         while len(level) > 1:
             level = halved(level)
         return across_sublanes(level[0])
+
+    def costs_at(g, i):
+        cost = jnp.dot(costs[g], pick[i], preferred_element_type=jnp.float32)
+        return cost.reshape(TILES, 8, LANES)
+
+    ready[...] = costs_at(0, 0)
 
     def segments(t, path):
         path = list(path)
@@ -114,8 +119,7 @@
                 for v in range(TILES):
                     starts[v] = jnp.where(here, path[v], starts[v])
             highest = lowest + jnp.take_along_axis(penalty_two, mirror ^ (base + i), axis=1)
-            cost = jnp.dot(costs[g], pick[base + i], preferred_element_type=jnp.float32)
-            cost = cost.reshape(TILES, 8, LANES)
+            cost = ready if i == 0 else costs_at(g, base + i)
             raised = [x + ordered for x in path]
             below = jnp.where(sub == 0, FAR, pltpu.roll(raised[-1], 1, 0))
             above = jnp.where(sub == 7, FAR, pltpu.roll(raised[0], 7, 0))
@@ -127,30 +131,29 @@
             pairs = halved(path)
             ordered = jnp.maximum(penalty_one, jnp.minimum(pairs[-1], -FAR))
             lowest = lowest_of(pairs)
+            if i == 28:
+                later = jnp.minimum(t + 1, blocks // 2 - 1)
+                ready[...] = costs_at(later // 2, 32 * (later % 2))
         return tuple(path)
 
     zero = jnp.zeros((8, LANES), jnp.float32)
     lax.fori_loop(0, blocks // 2, segments, (zero,) * TILES)
     states[...] = jnp.concatenate([starts[:, s, :] for s in range(8)], 0).T
     for z in range(16):
-        block = 2 * z + core_ref[0] if two else z
+        block = 2 * z + numbers_ref[8] if two else z
         fore, rear = ahead[pl.ds(block // 4, 1), :], back[pl.ds(block // 4, 1), :]
         start, end = states[pl.ds(block, 1), :], states[pl.ds(64 + blocks - 1 - block, 1), :]
-        if two:
-            out_ref[z, 0:1, :] = jnp.concatenate([start, fore], 1)
-            out_ref[z, 1:2, :] = jnp.concatenate([end, rear], 1)
-        else:
-            out_ref[2 * z : 2 * z + 1, :] = jnp.concatenate([start, fore, fore], 1)
-            out_ref[2 * z + 1 : 2 * z + 2, :] = jnp.concatenate([end, rear, rear], 1)
-
-
-def path_states(blocks, first, two, core, p_small, p_large, *sources):
+        out_ref[z, 0:1, :] = jnp.concatenate([start, fore], 1)
+        out_ref[z, 1:2, :] = jnp.concatenate([end, rear], 1)
+
+
+def path_states(blocks, first, two, numbers, *sources):
     smem = pl.BlockSpec(memory_space=pltpu.SMEM)
     vmem = pl.BlockSpec(memory_space=pltpu.VMEM)
     return pl.pallas_call(
         partial(path_kernel, blocks, first, two),
-        out_shape=jax.ShapeDtypeStruct((16, 2, 384) if two else (32, 512), jnp.float32),
-        in_specs=[smem] * 3 + [vmem] * len(sources),
+        out_shape=jax.ShapeDtypeStruct((16, 2, 384), jnp.float32),
+        in_specs=[smem] + [vmem] * len(sources),
         out_specs=vmem,
         scratch_shapes=[
             pltpu.VMEM((blocks, 16, 256), jnp.bfloat16),
@@ -160,23 +163,24 @@
             pltpu.VMEM((blocks // 4, 256, LANES), jnp.bfloat16),
             pltpu.VMEM((64, LANES, LANES), jnp.bfloat16),
             pltpu.VMEM((TILES, 8, LANES), jnp.float32),
+            pltpu.VMEM((TILES, 8, LANES), jnp.float32),
             pltpu.VMEM((LANES, 256), jnp.float32),
         ],
-        compiler_params=pltpu.CompilerParams(vmem_limit_bytes=24 * 2**20),
+        compiler_params=pltpu.CompilerParams(vmem_limit_bytes=12 * 2**20),
         cost_estimate=pl.CostEstimate(
             flops=blocks * 16 * 256 * 128 * 8, bytes_accessed=blocks * 24 * 1024, transcendentals=0
         ),
         name="line_paths",
-    )(core, p_small, p_large, *sources)
-
-
-def replay_kernel(first, across, quarter_ref, small_ref, entry_ref, cost_ref, *refs):
+    )(numbers, *sources)
+
+
+def replay_kernel(first, across, numbers_ref, entry_ref, cost_ref, *refs):
     *so_far, out_ref = refs
     lane = lax.broadcasted_iota(jnp.int32, (16, 256), 1)
-    shift = (LANES - 16 * quarter_ref[0]) % LANES
+    shift = (LANES - 16 * numbers_ref[9 if across else 10]) % LANES
     paths = [entry_ref[:, i, 0:256] for i in range(2)]
     jumps = [pltpu.roll(entry_ref[:, i, 256:], shift, 1) for i in range(2)]
-    small = [small_ref[first + i].astype(jnp.float32) for i in range(2)]
+    small = [numbers_ref[first + i].astype(jnp.float32) for i in range(2)]
     lowest = [jnp.min(path, axis=1, keepdims=True) for path in paths]
     for j in range(16):
         for i, at in enumerate((j, 15 - j)):
@@ -202,19 +206,20 @@
             out_ref[here] = value * OUT_SCALE if across and seen else value
 
 
-def replay(first, across, quarter, p_small, entry, cost, *so_far):
+def replay(first, across, numbers, entry, cost, *so_far):
     smem = pl.BlockSpec(memory_space=pltpu.SMEM)
     vmem = pl.BlockSpec(memory_space=pltpu.VMEM)
     return pl.pallas_call(
         partial(replay_kernel, first, across),
         out_shape=jax.ShapeDtypeStruct((16, 16, 256), jnp.float32),
-        in_specs=[smem] * 2 + [vmem] * (2 + len(so_far)),
+        in_specs=[smem] + [vmem] * (2 + len(so_far)),
         out_specs=vmem,
         cost_estimate=pl.CostEstimate(
             flops=2 * 65536 * 100, bytes_accessed=2**20, transcendentals=0
         ),
+        compiler_params=pltpu.CompilerParams(vmem_limit_bytes=3 * 2**20),
         name="block_paths",
-    )(quarter, p_small, entry, cost, *so_far)
+    )(numbers, entry, cost, *so_far)
 
 
 def message(cost, image):
@@ -224,44 +229,44 @@
     return jnp.concatenate([cost[:, :, :LANES], cost[:, :, LANES:], wide, empty], 1)
 
 
-def together_kernel(*refs):
-    pass
-
-
-def together(first, second):
-    anywhere = pl.BlockSpec(memory_space=pl.ANY)
+def after_kernel(value_ref, earlier_ref, out_ref):
+    out_ref[...] = value_ref[...]
+
+
+def after(value, earlier):
+    vmem = pl.BlockSpec(memory_space=pltpu.VMEM)
     return pl.pallas_call(
-        together_kernel,
-        out_shape=[jax.ShapeDtypeStruct(x.shape, x.dtype) for x in (first, second)],
-        in_specs=[anywhere] * 2,
-        out_specs=[anywhere] * 2,
-        input_output_aliases={0: 0, 1: 1},
-        name="together",
-    )(first, second)
+        after_kernel,
+        out_shape=jax.ShapeDtypeStruct(value.shape, value.dtype),
+        in_specs=[vmem] * 2,
+        out_specs=vmem,
+        compiler_params=pltpu.CompilerParams(vmem_limit_bytes=2 * 2**20),
+        name="after",
+    )(value, earlier)
 
 
 def on_device(cost_volume, left_image, p_small, p_large):
     index_x, index_y = lax.axis_index("gx"), lax.axis_index("gy")
-    core = (index_x % 2).reshape(1)
+    here = jnp.stack([index_x % 2, index_x % 4, index_y % 4]).astype(jnp.int32)
+    numbers = jnp.concatenate([p_small, p_large, here])
     chips = [[2 * z + c for z in range(16)] for c in range(2)]
     swap = [(i, i ^ 1) for i in range(32)]
 
     columns = message(jnp.transpose(cost_volume, (1, 0, 2)), left_image.T)
     lines = message(cost_volume, left_image)
     columns = lax.all_to_all(columns, "gy", 0, 0)
-    lines, columns = together(lines, columns)
+    lines = after(lines, columns)
     lines = lax.all_to_all(lines, "gx", 0, 0, axis_index_groups=chips)
-    entry_y = path_states(16, 2, False, core, p_small, p_large, columns)
-    lines, entry_y = together(lines, entry_y)
+    entry_y = path_states(16, 2, False, numbers, columns)
+    lines = after(lines, entry_y)
     others = lax.ppermute(lines, "gx", swap)
 
-    entry_y = lax.all_gather(entry_y, "gy", axis=0, tiled=True).reshape(16, 32, 512)
-    entry_y = lax.dynamic_slice(entry_y, (0, 2 * index_y, 0), (16, 2, 384))
-    entry_x = path_states(32, 0, True, core, p_small, p_large, lines, others)
+    entry_y = lax.all_to_all(entry_y, "gy", 0, 0)
+    entry_x = path_states(32, 0, True, numbers, lines, others)
     entry_x = lax.all_to_all(entry_x, "gx", 0, 0, axis_index_groups=chips)
 
-    total = replay(2, False, (index_y % 4).reshape(1), p_small, entry_y, cost_volume)
-    return replay(0, True, (index_x % 4).reshape(1), p_small, entry_x, cost_volume, total)
+    total = replay(2, False, numbers, entry_y, cost_volume)
+    return replay(0, True, numbers, entry_x, cost_volume, total)
 
 
 def solution(mesh):

time: 130 us -> 107 us (0.82)
  the two profiles are of different devices: /device:TPU:32 before, /device:TPU:2 now
where the time goes in v4:
time: 107 us; the launch traced here: 106 us
  Pallas kernels  43.7 us (41%)
  starting transfers between devices  36.6 us (34%)
  waiting for transfers between devices  22.5 us (21%)
  other arithmetic  2.04 us (2%)
  local copies, waits for them, and re-layouts  1.23 us (1%)
    pallas_call x2, Pallas kernels, path_states(): pl.pallas_call(partial(path_kernel, blocks, first, two), out_shape=jax.Sh...  34.7 us
    all_to_all x1, starting transfers between devices, on_device(): lines = lax.all_to_all(lines, 'gx', 0, 0, axis_index_groups=chips)  13.7 us
    all_to_all x1, waiting for transfers between devices, on_device(): entry_x = lax.all_to_all(entry_x, 'gx', 0, 0, axis_index_groups=chips)  9.3 us
    all_to_all x1, starting transfers between devices, on_device(): columns = lax.all_to_all(columns, 'gy', 0, 0)  9.26 us
    pallas_call x2, Pallas kernels, replay(): pl.pallas_call(partial(replay_kernel, first, across), out_shape=jax.Shape...  7.42 us
    all_to_all x1, waiting for transfers between devices, on_device(): columns = lax.all_to_all(columns, 'gy', 0, 0)  6.74 us
    all_to_all x1, waiting for transfers between devices, on_device(): lines = lax.all_to_all(lines, 'gx', 0, 0, axis_index_groups=chips)  6.42 us
    all_to_all x1, starting transfers between devices, on_device(): entry_x = lax.all_to_all(entry_x, 'gx', 0, 0, axis_index_groups=chips)  6.1 us
  transfers between devices with their start and end apart: 5, of which 3 were waited for; matrix products, arithmetic and copies ran while one was open for 0% of the time, Pallas kernels for 36%

profile of v4, /device:TPU:2, one launch (start us, length us, event | category | flops | bytes accessed | tf_op | source)
XLA Modules:
  0.0 106.2 jit_solution(2479708087390559208)
XLA Ops:
  0.0 0.0 copy-start.1
  0.0 1.1 %fusion = (f32[16,16,256]{2,1,0:T(8,128)S(1)}, f32[16,16,256]{2,0,1:T(8,128)S(1)}) fusion(s32[16,16,256]{2,1,0:T(8,128)} %cost_ref.3), kind=kLoop, calls=%fused_computation.3 | loop fusion | flops 65536 | bytes 786432 | tf_op jit(solution)/shard_map/convert_element_type | solution.py:228
  1.1 0.0 copy-done.1
  1.1 0.1 copy.7
  1.2 0.1 tile.19
  1.3 0.1 pad.7.clone
  1.4 0.8 maximum_maximum_fusion.1
  2.2 9.3 %all-to-all-start = ((f32[16,40,128]{2,1,0:T(8,128)}), f32[16,40,128]{2,1,0:T(8,128)S(1)}, u32[]{:S(2)}, u32[]{:S(2)}) async-start(f32[16,40,128]{2,1,0:T(8,128)} %maximum_maximum_fusion.1), calls=%async_computation | async-start | bytes 655360 | tf_op jit(solution)/shard_map/all_to_all | solution.py:257
  11.5 0.1 tile.17
  11.6 0.1 maximum_maximum_fusion
  11.7 0.1 copy.8.value_ref
  11.8 6.7 %all-to-all-done.earlier_ref.refs_0_ = f32[16,40,128]{2,1,0:T(8,128)S(1)} async-done(((f32[16,40,128]{2,1,0:T(8,128)}), f32[16,40,128]{2,1,0:T(8,128)S(1)}, u32[]{:S(2)}, u32[]{:S(2)}) %all-to-all-start) | async-done | bytes 327712 | tf_op jit(solution)/shard_map/all_to_all | solution.py:257
  18.6 0.7 after.2
  19.3 13.7 %all-to-all-start.1 = ((f32[16,40,128]{2,1,0:T(8,128)}), f32[16,40,128]{2,1,0:T(8,128)S(1)}, u32[]{:S(2)}, u32[]{:S(2)}) async-start(f32[16,40,128]{2,1,0:T(8,128)} %after.2), calls=%async_computation.1 | async-start | bytes 655360 | tf_op jit(solution)/shard_map/all_to_all | solution.py:259
  33.0 0.0 copy-start.2
  33.1 0.0 copy-start.3
  33.1 0.6 copy-done.2
  33.7 0.0 copy-done.3
  33.7 0.1 concatenate.9.numbers_ref
  33.8 12.3 %line_paths.2.earlier_ref = f32[16,2,384]{2,1,0:T(2,128)} custom-call(s32[11]{0:T(128)S(1)} %concatenate.9.numbers_ref, f32[16,40,128]{2,1,0:T(8,128)S(1)} %all-to-all-done.earlier_ref.refs_0_), custom_call_target="tpu_custom_call" | custom-call | flops 67108864 | bytes 393216 | tf_op jit(solution)/shard_map/line_paths/pallas_call | solution.py:153
  46.1 6.4 %all-to-all-done.1.value_ref = f32[16,40,128]{2,1,0:T(8,128)S(1)} async-done(((f32[16,40,128]{2,1,0:T(8,128)}), f32[16,40,128]{2,1,0:T(8,128)S(1)}, u32[]{:S(2)}, u32[]{:S(2)}) %all-to-all-start.1) | async-done | bytes 327712 | tf_op jit(solution)/shard_map/all_to_all | solution.py:259
  52.5 0.8 after.3.refs_0_
  53.3 1.9 %collective-permute-start = (f32[16,40,128]{2,1,0:T(8,128)S(1)}, f32[16,40,128]{2,1,0:T(8,128)S(1)}, u32[]{:S(2)}, u32[]{:S(2)}) collective-permute-start(f32[16,40,128]{2,1,0:T(8,128)S(1)} %after.3.refs_0_), channel_id=1, source_target_pairs={{0,1},{1,0},{2,3},{3,2},{4,5},{5,4},{6,7},{7,6},{8,9},{9,8},{10,11... | collective-permute-start | bytes 983048 | tf_op jit(solution)/shard_map/ppermute | solution.py:262
  55.3 5.7 %all-to-all-start.3 = ((f32[16,2,384]{2,1,0:T(2,128)}), f32[16,2,384]{2,1,0:T(2,128)S(1)}, u32[]{:S(2)}, u32[]{:S(2)}) async-start(f32[16,2,384]{2,1,0:T(2,128)} %line_paths.2.earlier_ref), calls=%async_computation.3 | async-start | bytes 98304 | tf_op jit(solution)/shard_map/all_to_all | solution.py:264
  60.9 0.0 copy-start
  60.9 0.0 collective-permute-done.refs_1_
  61.0 22.4 %line_paths.3 = f32[16,2,384]{2,1,0:T(2,128)} custom-call(s32[11]{0:T(128)S(1)} %concatenate.9.numbers_ref, f32[16,40,128]{2,1,0:T(8,128)S(1)} %after.3.refs_0_, f32[16,40,128]{2,1,0:T(8,128)S(1)} %collective-permute-done.refs_1_), custom_call_target="tpu_custom_call" | custom-call | flops 134217728 | bytes 786432 | tf_op jit(solution)/shard_map/line_paths/pallas_call | solution.py:153
  83.4 0.0 all-to-all-done.3.entry_ref
  83.4 6.1 %all-to-all-start.2 = ((f32[16,2,384]{2,1,0:T(2,128)}), f32[16,2,384]{2,1,0:T(2,128)S(1)}, u32[]{:S(2)}, u32[]{:S(2)}) async-start(f32[16,2,384]{2,1,0:T(2,128)} %line_paths.3), calls=%async_computation.2 | async-start | bytes 98304 | tf_op jit(solution)/shard_map/all_to_all | solution.py:266
  89.5 0.0 copy-done
  89.5 3.3 %block_paths.2.refs_0_ = f32[16,16,256]{2,1,0:T(8,128)S(1)} custom-call(s32[11]{0:T(128)S(1)} %concatenate.9.numbers_ref, f32[16,2,384]{2,1,0:T(2,128)S(1)} %all-to-all-done.3.entry_ref, s32[16,16,256]{2,1,0:T(8,128)S(1)} %copy-done), custom_call_target="tpu_custom_call" | custom-call | flops 13107200 | bytes 1048576 | tf_op jit(solution)/shard_map/block_paths/pallas_call | solution.py:212
  92.8 9.3 %all-to-all-done.2.entry_ref = f32[16,2,384]{2,1,0:T(2,128)S(1)} async-done(((f32[16,2,384]{2,1,0:T(2,128)}), f32[16,2,384]{2,1,0:T(2,128)S(1)}, u32[]{:S(2)}, u32[]{:S(2)}) %all-to-all-start.2) | async-done | bytes 49184 | tf_op jit(solution)/shard_map/all_to_all | solution.py:266
  102.1 4.1 %block_paths.3 = f32[16,16,256]{2,1,0:T(8,128)} custom-call(s32[11]{0:T(128)S(1)} %concatenate.9.numbers_ref, f32[16,2,384]{2,1,0:T(2,128)S(1)} %all-to-all-done.2.entry_ref, s32[16,16,256]{2,1,0:T(8,128)S(1)} %copy-done, f32[16,16,256]{2,1,0:T(8,128)S(1)} %block_paths.2.refs_0_), custom_call_target="tpu_custom_call" | custom-call | flops 13107200 | bytes 1048576 | tf_op jit(solution)/shard_map/block_paths/pallas_call | solution.py:212
  (5 shorter events, 0.1 us)
Async XLA Ops:
  0.0 1.1 %copy-start.1 = (f32[16,16]{1,0:T(8,128)S(1)}, f32[16,16]{1,0:T(8,128)}, u32[]{:S(2)}) copy-start(f32[16,16]{1,0:T(8,128)} %param.5) | copy-start | bytes 3076
  2.2 16.3 %all-to-all-start = ((f32[16,40,128]{2,1,0:T(8,128)}), f32[16,40,128]{2,1,0:T(8,128)S(1)}, u32[]{:S(2)}, u32[]{:S(2)}) async-start(f32[16,40,128]{2,1,0:T(8,128)} %maximum_maximum_fusion.1), calls=%async_computation | async-start | bytes 655360 | tf_op jit(solution)/shard_map/all_to_all | solution.py:257
  19.3 33.2 %all-to-all-start.1 = ((f32[16,40,128]{2,1,0:T(8,128)}), f32[16,40,128]{2,1,0:T(8,128)S(1)}, u32[]{:S(2)}, u32[]{:S(2)}) async-start(f32[16,40,128]{2,1,0:T(8,128)} %after.2), calls=%async_computation.1 | async-start | bytes 655360 | tf_op jit(solution)/shard_map/all_to_all | solution.py:259
  33.0 0.7 copy-start.2
  33.1 0.7 copy-start.3
  53.3 7.6 %collective-permute-start = (f32[16,40,128]{2,1,0:T(8,128)S(1)}, f32[16,40,128]{2,1,0:T(8,128)S(1)}, u32[]{:S(2)}, u32[]{:S(2)}) collective-permute-start(f32[16,40,128]{2,1,0:T(8,128)S(1)} %after.3.refs_0_), channel_id=1, source_target_pairs={{0,1},{1,0},{2,3},{3,2},{4,5},{5,4},{6,7},{7,6},{8,9},{9,8},{10,11... | collective-permute-start | bytes 983048 | tf_op jit(solution)/shard_map/ppermute | solution.py:262
  55.3 28.1 %all-to-all-start.3 = ((f32[16,2,384]{2,1,0:T(2,128)}), f32[16,2,384]{2,1,0:T(2,128)S(1)}, u32[]{:S(2)}, u32[]{:S(2)}) async-start(f32[16,2,384]{2,1,0:T(2,128)} %line_paths.2.earlier_ref), calls=%async_computation.3 | async-start | bytes 98304 | tf_op jit(solution)/shard_map/all_to_all | solution.py:264
  60.9 28.6 %copy-start = (s32[16,16,256]{2,1,0:T(8,128)S(1)}, s32[16,16,256]{2,1,0:T(8,128)}, u32[]{:S(2)}) copy-start(s32[16,16,256]{2,1,0:T(8,128)} %cost_ref.3) | copy-start | bytes 786436
  83.4 18.8 %all-to-all-start.2 = ((f32[16,2,384]{2,1,0:T(2,128)}), f32[16,2,384]{2,1,0:T(2,128)S(1)}, u32[]{:S(2)}, u32[]{:S(2)}) async-start(f32[16,2,384]{2,1,0:T(2,128)} %line_paths.3), calls=%async_computation.2 | async-start | bytes 98304 | tf_op jit(solution)/shard_map/all_to_all | solution.py:266

commit v5 on v4

--- a/solution.py
+++ b/solution.py
@@ -12,6 +12,8 @@
 OUT_SCALE = 1.0 / 256.0
 LANES = 128
 TILES = 32
+UNROLL = 4
+AHEAD = 3
 ROWS = 40
 
 
@@ -20,7 +22,7 @@
 
 
 def gather_costs(blocks, two, core, sources, scr, img):
-    for z in range(blocks // len(sources)):
+    def fetch(z, nothing):
         for which, source in enumerate(sources):
             if two:
                 place = 2 * z + core if which == 0 else 2 * z + 1 - core
@@ -29,10 +31,13 @@
             scr[place, :, 0:LANES] = source[z, 0:16, :].astype(jnp.bfloat16)
             scr[place, :, LANES:] = source[z, 16:32, :].astype(jnp.bfloat16)
             img[pl.ds(place, 1), :] = source[z, 32:33, :]
-
-
-def path_kernel(blocks, first, two, numbers_ref, *refs):
-    sources, (out_ref, scr, img, ahead, back, costs, pick, ready, starts, states) = refs[:-10], refs[-10:]
+        return nothing
+
+    lax.fori_loop(0, 16, fetch, 0, unroll=4)
+
+
+def path_kernel(blocks, first, two, numbers_ref, pick, *refs):
+    sources, (out_ref, scr, img, ahead, back, costs, ready, starts, states) = refs[:-9], refs[-9:]
     groups = blocks // 4
     lane = lax.broadcasted_iota(jnp.int32, (8, LANES), 1)
     sub = lax.broadcasted_iota(jnp.int32, (8, LANES), 0)
@@ -72,14 +77,6 @@
         costs[g] = turned.astype(jnp.bfloat16)
 
     mirror = jnp.where(lane < 64, 0, LANES - 1)
-    lane_in = lax.broadcasted_iota(jnp.int32, (LANES, LANES), 0)
-    lane_out = lax.broadcasted_iota(jnp.int32, (LANES, LANES), 1)
-
-    def build(i, nothing):
-        pick[i] = (lane_in == jnp.where(lane_out < 64, i, LANES - 1 - i)).astype(jnp.bfloat16)
-        return nothing
-
-    lax.fori_loop(0, 64, build, 0)
 
     def across_sublanes(lowest):
         for shift in (4, 2, 1):
@@ -98,28 +95,35 @@
         cost = jnp.dot(costs[g], pick[i], preferred_element_type=jnp.float32)
         return cost.reshape(TILES, 8, LANES)
 
-    ready[...] = costs_at(0, 0)
-
-    def segments(t, path):
-        path = list(path)
-        g = t // 2
-        base = 32 * (t % 2)
-        penalty_two = jnp.where(
+    def penalties(g):
+        return jnp.where(
             forward,
             jnp.broadcast_to(ahead[pl.ds(g, 1), :], (8, LANES)),
             jnp.broadcast_to(back[pl.ds(groups - 1 - g, 1), :], (8, LANES)),
         )
+
+    def jump_at(g, i):
+        return jnp.take_along_axis(penalties(g), mirror ^ i, axis=1)
+
+    for i in range(AHEAD):
+        ready[i] = costs_at(0, i)
+
+    def segments(t, carried):
+        *path, jump = carried
+        g = t >> 1
+        base = (t & 1) << 5
+        later = jnp.minimum(t + 1, blocks // 2 - 1)
         lowest = lowest_of(path)
         ordered = penalty_one
         for i in range(32):
             if i % 16 == 0:
                 path = [x - lowest for x in path]
                 lowest = jnp.zeros_like(lowest)
-                here = lane % 64 == 2 * t + i // 16
+                here = (lane & 63) == 2 * t + i // 16
                 for v in range(TILES):
                     starts[v] = jnp.where(here, path[v], starts[v])
-            highest = lowest + jnp.take_along_axis(penalty_two, mirror ^ (base + i), axis=1)
-            cost = ready if i == 0 else costs_at(g, base + i)
+            highest = lowest + (jump if i == 0 else jump_at(g, base + i))
+            cost = ready[i] if i < AHEAD else costs_at(g, base + i)
             raised = [x + ordered for x in path]
             below = jnp.where(sub == 0, FAR, pltpu.roll(raised[-1], 1, 0))
             above = jnp.where(sub == 7, FAR, pltpu.roll(raised[0], 7, 0))
@@ -131,13 +135,14 @@
             pairs = halved(path)
             ordered = jnp.maximum(penalty_one, jnp.minimum(pairs[-1], -FAR))
             lowest = lowest_of(pairs)
-            if i == 28:
-                later = jnp.minimum(t + 1, blocks // 2 - 1)
-                ready[...] = costs_at(later // 2, 32 * (later % 2))
-        return tuple(path)
+            if i == 20:
+                jump = jump_at(later >> 1, (later & 1) << 5)
+                for k in range(AHEAD):
+                    ready[k] = costs_at(later >> 1, ((later & 1) << 5) + k)
+        return (*path, jump)
 
     zero = jnp.zeros((8, LANES), jnp.float32)
-    lax.fori_loop(0, blocks // 2, segments, (zero,) * TILES)
+    lax.fori_loop(0, blocks // 2, segments, (zero,) * TILES + (jump_at(0, 0),))
     states[...] = jnp.concatenate([starts[:, s, :] for s in range(8)], 0).T
     for z in range(16):
         block = 2 * z + numbers_ref[8] if two else z
@@ -147,13 +152,13 @@
         out_ref[z, 1:2, :] = jnp.concatenate([end, rear], 1)
 
 
-def path_states(blocks, first, two, numbers, *sources):
+def path_states(blocks, first, two, numbers, pick, *sources):
     smem = pl.BlockSpec(memory_space=pltpu.SMEM)
     vmem = pl.BlockSpec(memory_space=pltpu.VMEM)
     return pl.pallas_call(
         partial(path_kernel, blocks, first, two),
         out_shape=jax.ShapeDtypeStruct((16, 2, 384), jnp.float32),
-        in_specs=[smem] + [vmem] * len(sources),
+        in_specs=[smem] + [vmem] * (1 + len(sources)),
         out_specs=vmem,
         scratch_shapes=[
             pltpu.VMEM((blocks, 16, 256), jnp.bfloat16),
@@ -161,8 +166,7 @@
             pltpu.VMEM((blocks // 4, LANES), jnp.float32),
             pltpu.VMEM((blocks // 4, LANES), jnp.float32),
             pltpu.VMEM((blocks // 4, 256, LANES), jnp.bfloat16),
-            pltpu.VMEM((64, LANES, LANES), jnp.bfloat16),
-            pltpu.VMEM((TILES, 8, LANES), jnp.float32),
+            pltpu.VMEM((AHEAD, TILES, 8, LANES), jnp.float32),
             pltpu.VMEM((TILES, 8, LANES), jnp.float32),
             pltpu.VMEM((LANES, 256), jnp.float32),
         ],
@@ -171,39 +175,49 @@
             flops=blocks * 16 * 256 * 128 * 8, bytes_accessed=blocks * 24 * 1024, transcendentals=0
         ),
         name="line_paths",
-    )(numbers, *sources)
+    )(numbers, pick, *sources)
 
 
 def replay_kernel(first, across, numbers_ref, entry_ref, cost_ref, *refs):
-    *so_far, out_ref = refs
+    *so_far, out_ref, line, total, jumps = refs
     lane = lax.broadcasted_iota(jnp.int32, (16, 256), 1)
     shift = (LANES - 16 * numbers_ref[9 if across else 10]) % LANES
-    paths = [entry_ref[:, i, 0:256] for i in range(2)]
-    jumps = [pltpu.roll(entry_ref[:, i, 256:], shift, 1) for i in range(2)]
+    cost = cost_ref[...].astype(jnp.float32)
+    line[...] = jnp.swapaxes(cost, 0, 1) if across else cost
+    total[...] = jnp.zeros_like(total)
+    for i in range(2):
+        penalty_two = pltpu.roll(entry_ref[:, i, 256:], shift, 1)
+        for at in range(16):
+            jumps[i, at] = jnp.broadcast_to(penalty_two[:, at : at + 1], (16, LANES))
     small = [numbers_ref[first + i].astype(jnp.float32) for i in range(2)]
-    lowest = [jnp.min(path, axis=1, keepdims=True) for path in paths]
-    for j in range(16):
+
+    def lowest_of(x):
+        return jnp.broadcast_to(jnp.min(x, axis=1, keepdims=True), (16, LANES))
+
+    def wide(x):
+        return jnp.concatenate([x, x], 1)
+
+    def step(j, carried):
+        after = []
         for i, at in enumerate((j, 15 - j)):
-            path = paths[i]
-            cost = (cost_ref[:, at, :] if across else cost_ref[at]).astype(jnp.float32)
+            path, lowest = carried[i]
+            cost = line[at]
             below = jnp.where(lane == 0, FAR, pltpu.roll(path, 1, 1))
             above = jnp.where(lane == 255, FAR, pltpu.roll(path, 255, 1))
             near = jnp.minimum(path, jnp.minimum(below, above) + small[i]) + cost
-            highest = lowest[i] + jumps[i][:, at : at + 1]
-            path = jnp.minimum(near, highest + cost)
-            value = path - lowest[i]
-            lowest[i] = jnp.minimum(
-                jnp.min(near, axis=1, keepdims=True),
-                highest + jnp.min(cost, axis=1, keepdims=True),
-            )
-            paths[i] = path
-            here = (slice(None), at) if across else (at,)
-            seen = j >= 8
-            if seen:
-                value = value + out_ref[here]
-            elif across:
-                value = value + so_far[0][here]
-            out_ref[here] = value * OUT_SCALE if across and seen else value
+            highest = lowest + jumps[i, at]
+            path = jnp.minimum(near, wide(highest) + cost)
+            total[at] += path - wide(lowest)
+            lowest = jnp.minimum(lowest_of(near), highest + lowest_of(cost))
+            after.append((path, lowest))
+        return tuple(after)
+
+    paths = [entry_ref[:, i, 0:256] for i in range(2)]
+    lax.fori_loop(0, 16, step, tuple((path, lowest_of(path)) for path in paths), unroll=UNROLL)
+    if across:
+        out_ref[...] = (jnp.swapaxes(total[...], 0, 1) + so_far[0][...]) * OUT_SCALE
+    else:
+        out_ref[...] = total[...]
 
 
 def replay(first, across, numbers, entry, cost, *so_far):
@@ -214,6 +228,11 @@
         out_shape=jax.ShapeDtypeStruct((16, 16, 256), jnp.float32),
         in_specs=[smem] + [vmem] * (2 + len(so_far)),
         out_specs=vmem,
+        scratch_shapes=[
+            pltpu.VMEM((16, 16, 256), jnp.float32),
+            pltpu.VMEM((16, 16, 256), jnp.float32),
+            pltpu.VMEM((2, 16, 16, LANES), jnp.float32),
+        ],
         cost_estimate=pl.CostEstimate(
             flops=2 * 65536 * 100, bytes_accessed=2**20, transcendentals=0
         ),
@@ -249,6 +268,8 @@
     index_x, index_y = lax.axis_index("gx"), lax.axis_index("gy")
     here = jnp.stack([index_x % 2, index_x % 4, index_y % 4]).astype(jnp.int32)
     numbers = jnp.concatenate([p_small, p_large, here])
+    step, pixel, path = (lax.broadcasted_iota(jnp.int32, (64, LANES, LANES), i) for i in range(3))
+    pick = (pixel == jnp.where(path < 64, step, LANES - 1 - step)).astype(jnp.bfloat16)
     chips = [[2 * z + c for z in range(16)] for c in range(2)]
     swap = [(i, i ^ 1) for i in range(32)]
 
@@ -257,12 +278,12 @@
     columns = lax.all_to_all(columns, "gy", 0, 0)
     lines = after(lines, columns)
     lines = lax.all_to_all(lines, "gx", 0, 0, axis_index_groups=chips)
-    entry_y = path_states(16, 2, False, numbers, columns)
+    entry_y = path_states(16, 2, False, numbers, pick, columns)
     lines = after(lines, entry_y)
     others = lax.ppermute(lines, "gx", swap)
 
     entry_y = lax.all_to_all(entry_y, "gy", 0, 0)
-    entry_x = path_states(32, 0, True, numbers, lines, others)
+    entry_x = path_states(32, 0, True, numbers, pick, lines, others)
     entry_x = lax.all_to_all(entry_x, "gx", 0, 0, axis_index_groups=chips)
 
     total = replay(2, False, numbers, entry_y, cost_volume)

time: 107 us -> 104 us (0.972)
  Pallas kernels: 43.7 us -> 38.2 us
  waiting for transfers between devices: 22.5 us -> 24.8 us
    pallas_call x2, Pallas kernels: 34.7 us -> 30.4 us  [path_states(): pl.pallas_call(partial(path_kernel, blocks, first, two), out_shape=jax.Sh...]
    all_to_all x1, waiting for transfers between devices: 6.42 us -> 8.14 us  [on_device(): lines = lax.all_to_all(lines, 'gx', 0, 0, axis_index_groups=chips)]
    pallas_call x2, Pallas kernels: 7.42 us -> 6.2 us  [replay(): pl.pallas_call(partial(replay_kernel, first, across), out_shape=jax.Shape...]
  transfers between devices with their start and end apart: 5 -> 5, of which waited for: 3 -> 3; matrix products, arithmetic and copies ran while one was open for 0% -> 1% of each run, Pallas kernels for 36% -> 32%
where the time goes in v5:
time: 104 us
  Pallas kernels  38.2 us (37%)
  starting transfers between devices  36.8 us (35%)
  waiting for transfers between devices  24.8 us (24%)
  other arithmetic  2.52 us (2%)
  local copies, waits for them, and re-layouts  1.34 us (1%)
    pallas_call x2, Pallas kernels, path_states(): pl.pallas_call(partial(path_kernel, blocks, first, two), out_shape=jax.Sh...  30.4 us
    all_to_all x1, starting transfers between devices, on_device(): lines = lax.all_to_all(lines, 'gx', 0, 0, axis_index_groups=chips)  13.7 us
    all_to_all x1, waiting for transfers between devices, on_device(): entry_x = lax.all_to_all(entry_x, 'gx', 0, 0, axis_index_groups=chips)  9.94 us
    all_to_all x1, starting transfers between devices, on_device(): columns = lax.all_to_all(columns, 'gy', 0, 0)  9.39 us
    all_to_all x1, waiting for transfers between devices, on_device(): lines = lax.all_to_all(lines, 'gx', 0, 0, axis_index_groups=chips)  8.14 us
    all_to_all x1, waiting for transfers between devices, on_device(): columns = lax.all_to_all(columns, 'gy', 0, 0)  6.73 us
    pallas_call x2, Pallas kernels, replay(): pl.pallas_call(partial(replay_kernel, first, across), out_shape=jax.Shape...  6.2 us
    all_to_all x1, starting transfers between devices, on_device(): entry_x = lax.all_to_all(entry_x, 'gx', 0, 0, axis_index_groups=chips)  6.09 us
  transfers between devices with their start and end apart: 5, of which 3 were waited for; matrix products, arithmetic and copies ran while one was open for 1% of the time, Pallas kernels for 32%

profile of v5, /device:TPU:2, one launch (start us, length us, event | category | flops | bytes accessed | tf_op | source)
XLA Modules:
  0.0 103.8 jit_solution(8001794879299654518)
XLA Ops:
  0.0 0.0 copy-start.1
  0.0 0.8 copy.7
  0.8 0.1 tile.19
  0.9 1.1 %fusion.1 = (f32[16,16,256]{2,1,0:T(8,128)S(1)}, f32[16,16,256]{2,0,1:T(8,128)S(1)}) fusion(s32[16,16,256]{2,1,0:T(8,128)} %cost_ref.3), kind=kLoop, calls=%fused_computation.7 | loop fusion | flops 65536 | bytes 786432 | tf_op jit(solution)/shard_map/convert_element_type | solution.py:247
  2.1 0.1 pad.7.clone
  2.2 0.8 maximum_maximum_fusion.1
  3.0 0.0 copy-start.2
  3.0 0.0 copy-start.3
  3.0 9.4 %all-to-all-start = ((f32[16,40,128]{2,1,0:T(8,128)}), f32[16,40,128]{2,1,0:T(8,128)S(1)}, u32[]{:S(2)}, u32[]{:S(2)}) async-start(f32[16,40,128]{2,1,0:T(8,128)} %maximum_maximum_fusion.1), calls=%async_computation | async-start | bytes 655360 | tf_op jit(solution)/shard_map/all_to_all | solution.py:278
  12.4 0.0 copy-done.1
  12.4 0.1 tile.17
  12.5 0.1 maximum_maximum_fusion
  12.6 0.1 copy.8.value_ref
  12.7 6.7 %all-to-all-done.earlier_ref.refs_0_ = f32[16,40,128]{2,1,0:T(8,128)S(1)} async-done(((f32[16,40,128]{2,1,0:T(8,128)}), f32[16,40,128]{2,1,0:T(8,128)S(1)}, u32[]{:S(2)}, u32[]{:S(2)}) %all-to-all-start) | async-done | bytes 327712 | tf_op jit(solution)/shard_map/all_to_all | solution.py:278
  19.5 0.7 after.2
  20.2 13.7 %all-to-all-start.1 = ((f32[16,40,128]{2,1,0:T(8,128)}), f32[16,40,128]{2,1,0:T(8,128)S(1)}, u32[]{:S(2)}, u32[]{:S(2)}) async-start(f32[16,40,128]{2,1,0:T(8,128)} %after.2), calls=%async_computation.1 | async-start | bytes 655360 | tf_op jit(solution)/shard_map/all_to_all | solution.py:280
  33.9 0.0 copy-done.2
  33.9 0.0 copy-done.3
  33.9 0.1 concatenate.9.numbers_ref
  34.0 0.5 fusion.pick
  34.5 10.7 %line_paths.2.earlier_ref = f32[16,2,384]{2,1,0:T(2,128)} custom-call(s32[11]{0:T(128)S(1)} %concatenate.9.numbers_ref, bf16[64,128,128]{2,1,0:T(8,128)(2,1)S(1)} %fusion.pick, f32[16,40,128]{2,1,0:T(8,128)S(1)} %all-to-all-done.earlier_ref.refs_0_), custom_call_target="tpu_custom_call" | custom-call | flops 67108864 | bytes 393216 | tf_op jit(solution)/shard_map/line_paths/pallas_call | solution.py:158
  45.3 0.0 copy-start
  45.3 8.1 %all-to-all-done.1.value_ref = f32[16,40,128]{2,1,0:T(8,128)S(1)} async-done(((f32[16,40,128]{2,1,0:T(8,128)}), f32[16,40,128]{2,1,0:T(8,128)S(1)}, u32[]{:S(2)}, u32[]{:S(2)}) %all-to-all-start.1) | async-done | bytes 327712 | tf_op jit(solution)/shard_map/all_to_all | solution.py:280
  53.4 0.8 after.3.refs_0_
  54.2 1.9 %collective-permute-start = (f32[16,40,128]{2,1,0:T(8,128)S(1)}, f32[16,40,128]{2,1,0:T(8,128)S(1)}, u32[]{:S(2)}, u32[]{:S(2)}) collective-permute-start(f32[16,40,128]{2,1,0:T(8,128)S(1)} %after.3.refs_0_), channel_id=1, source_target_pairs={{0,1},{1,0},{2,3},{3,2},{4,5},{5,4},{6,7},{7,6},{8,9},{9,8},{10,11... | collective-permute-start | bytes 983048 | tf_op jit(solution)/shard_map/ppermute | solution.py:283
  56.1 5.7 %all-to-all-start.3 = ((f32[16,2,384]{2,1,0:T(2,128)}), f32[16,2,384]{2,1,0:T(2,128)S(1)}, u32[]{:S(2)}, u32[]{:S(2)}) async-start(f32[16,2,384]{2,1,0:T(2,128)} %line_paths.2.earlier_ref), calls=%async_computation.3 | async-start | bytes 98304 | tf_op jit(solution)/shard_map/all_to_all | solution.py:285
  61.8 0.0 collective-permute-done.refs_1_
  61.8 19.7 %line_paths.3 = f32[16,2,384]{2,1,0:T(2,128)} custom-call(s32[11]{0:T(128)S(1)} %concatenate.9.numbers_ref, bf16[64,128,128]{2,1,0:T(8,128)(2,1)S(1)} %fusion.pick, f32[16,40,128]{2,1,0:T(8,128)S(1)} %after.3.refs_0_, f32[16,40,128]{2,1,0:T(8,128)S(1)} %collective-permute-done.refs_1_), custom_call_target="tpu_custom_call" | custom-call | flops 134217728 | bytes 786432 | tf_op jit(solution)/shard_map/line_paths/pallas_call | solution.py:158
  81.5 0.0 all-to-all-done.3.entry_ref
  81.5 6.1 %all-to-all-start.2 = ((f32[16,2,384]{2,1,0:T(2,128)}), f32[16,2,384]{2,1,0:T(2,128)S(1)}, u32[]{:S(2)}, u32[]{:S(2)}) async-start(f32[16,2,384]{2,1,0:T(2,128)} %line_paths.3), calls=%async_computation.2 | async-start | bytes 98304 | tf_op jit(solution)/shard_map/all_to_all | solution.py:287
  87.6 0.0 copy-done
  87.6 2.7 %block_paths.2.refs_0_ = f32[16,16,256]{2,1,0:T(8,128)S(1)} custom-call(s32[11]{0:T(128)S(1)} %concatenate.9.numbers_ref, f32[16,2,384]{2,1,0:T(2,128)S(1)} %all-to-all-done.3.entry_ref, s32[16,16,256]{2,1,0:T(8,128)S(1)} %copy-done), custom_call_target="tpu_custom_call" | custom-call | flops 13107200 | bytes 1048576 | tf_op jit(solution)/shard_map/block_paths/pallas_call | solution.py:226
  90.3 9.9 %all-to-all-done.2.entry_ref = f32[16,2,384]{2,1,0:T(2,128)S(1)} async-done(((f32[16,2,384]{2,1,0:T(2,128)}), f32[16,2,384]{2,1,0:T(2,128)S(1)}, u32[]{:S(2)}, u32[]{:S(2)}) %all-to-all-start.2) | async-done | bytes 49184 | tf_op jit(solution)/shard_map/all_to_all | solution.py:287
  100.3 3.5 %block_paths.3 = f32[16,16,256]{2,1,0:T(8,128)} custom-call(s32[11]{0:T(128)S(1)} %concatenate.9.numbers_ref, f32[16,2,384]{2,1,0:T(2,128)S(1)} %all-to-all-done.2.entry_ref, s32[16,16,256]{2,1,0:T(8,128)S(1)} %copy-done, f32[16,16,256]{2,1,0:T(8,128)S(1)} %block_paths.2.refs_0_), custom_call_target="tpu_custom_call" | custom-call | flops 13107200 | bytes 1048576 | tf_op jit(solution)/shard_map/block_paths/pallas_call | solution.py:226
  (7 shorter events, 0.1 us)
Async XLA Ops:
  0.0 12.4 %copy-start.1 = (f32[16,16]{1,0:T(8,128)S(1)}, f32[16,16]{1,0:T(8,128)}, u32[]{:S(2)}) copy-start(f32[16,16]{1,0:T(8,128)} %param.5) | copy-start | bytes 3076
  3.0 31.0 %copy-start.2 = (s32[4]{0:T(128)S(1)}, s32[4]{0:T(128)}, u32[]{:S(2)}) copy-start(s32[4]{0:T(128)} %param.6) | copy-start | bytes 52
  3.0 31.0 %copy-start.3 = (s32[4]{0:T(128)S(1)}, s32[4]{0:T(128)}, u32[]{:S(2)}) copy-start(s32[4]{0:T(128)} %param.7) | copy-start | bytes 52
  3.0 16.5 %all-to-all-start = ((f32[16,40,128]{2,1,0:T(8,128)}), f32[16,40,128]{2,1,0:T(8,128)S(1)}, u32[]{:S(2)}, u32[]{:S(2)}) async-start(f32[16,40,128]{2,1,0:T(8,128)} %maximum_maximum_fusion.1), calls=%async_computation | async-start | bytes 655360 | tf_op jit(solution)/shard_map/all_to_all | solution.py:278
  20.2 33.2 %all-to-all-start.1 = ((f32[16,40,128]{2,1,0:T(8,128)}), f32[16,40,128]{2,1,0:T(8,128)S(1)}, u32[]{:S(2)}, u32[]{:S(2)}) async-start(f32[16,40,128]{2,1,0:T(8,128)} %after.2), calls=%async_computation.1 | async-start | bytes 655360 | tf_op jit(solution)/shard_map/all_to_all | solution.py:280
  45.3 42.4 %copy-start = (s32[16,16,256]{2,1,0:T(8,128)S(1)}, s32[16,16,256]{2,1,0:T(8,128)}, u32[]{:S(2)}) copy-start(s32[16,16,256]{2,1,0:T(8,128)} %cost_ref.3) | copy-start | bytes 786436
  54.2 7.6 %collective-permute-start = (f32[16,40,128]{2,1,0:T(8,128)S(1)}, f32[16,40,128]{2,1,0:T(8,128)S(1)}, u32[]{:S(2)}, u32[]{:S(2)}) collective-permute-start(f32[16,40,128]{2,1,0:T(8,128)S(1)} %after.3.refs_0_), channel_id=1, source_target_pairs={{0,1},{1,0},{2,3},{3,2},{4,5},{5,4},{6,7},{7,6},{8,9},{9,8},{10,11... | collective-permute-start | bytes 983048 | tf_op jit(solution)/shard_map/ppermute | solution.py:283
  56.1 25.4 %all-to-all-start.3 = ((f32[16,2,384]{2,1,0:T(2,128)}), f32[16,2,384]{2,1,0:T(2,128)S(1)}, u32[]{:S(2)}, u32[]{:S(2)}) async-start(f32[16,2,384]{2,1,0:T(2,128)} %line_paths.2.earlier_ref), calls=%async_computation.3 | async-start | bytes 98304 | tf_op jit(solution)/shard_map/all_to_all | solution.py:285
  81.5 18.7 %all-to-all-start.2 = ((f32[16,2,384]{2,1,0:T(2,128)}), f32[16,2,384]{2,1,0:T(2,128)S(1)}, u32[]{:S(2)}, u32[]{:S(2)}) async-start(f32[16,2,384]{2,1,0:T(2,128)} %line_paths.3), calls=%async_computation.2 | async-start | bytes 98304 | tf_op jit(solution)/shard_map/all_to_all | solution.py:287

commit v6 on v5

--- a/solution.py
+++ b/solution.py
@@ -241,6 +241,31 @@
     )(numbers, entry, cost, *so_far)
 
 
+def column_message_kernel(cost_ref, image_ref, out_ref):
+    crossed = jnp.swapaxes(cost_ref[...].astype(jnp.float32), 0, 1)
+    out_ref[:, 0:16, :] = crossed[:, :, 0:LANES]
+    out_ref[:, 16:32, :] = crossed[:, :, LANES:]
+    row = lax.broadcasted_iota(jnp.int32, (16, LANES), 0)
+    lane = lax.broadcasted_iota(jnp.int32, (16, LANES), 1)
+    image = image_ref[...]
+    for c in range(16):
+        column = jnp.where(lane % 16 == row, image[:, c : c + 1], 0.0)
+        line = jnp.sum(column, axis=0, keepdims=True)
+        out_ref[c, 32:40, :] = jnp.broadcast_to(line, (8, LANES))
+
+
+def column_message(cost, image):
+    vmem = pl.BlockSpec(memory_space=pltpu.VMEM)
+    return pl.pallas_call(
+        column_message_kernel,
+        out_shape=jax.ShapeDtypeStruct((16, ROWS, LANES), jnp.float32),
+        in_specs=[vmem] * 2,
+        out_specs=vmem,
+        compiler_params=pltpu.CompilerParams(vmem_limit_bytes=3 * 2**20),
+        name="column_message",
+    )(cost, image)
+
+
 def message(cost, image):
     wide = jnp.tile(image, (1, LANES // 16))[:, None, :]
     empty = jnp.zeros((16, ROWS - 33, LANES), jnp.float32)
@@ -252,12 +277,12 @@
     out_ref[...] = value_ref[...]
 
 
-def after(value, earlier):
+def after(value, earlier, space):
     vmem = pl.BlockSpec(memory_space=pltpu.VMEM)
     return pl.pallas_call(
         after_kernel,
         out_shape=jax.ShapeDtypeStruct(value.shape, value.dtype),
-        in_specs=[vmem] * 2,
+        in_specs=[vmem, pl.BlockSpec(memory_space=space)],
         out_specs=vmem,
         compiler_params=pltpu.CompilerParams(vmem_limit_bytes=2 * 2**20),
         name="after",
@@ -273,13 +298,13 @@
     chips = [[2 * z + c for z in range(16)] for c in range(2)]
     swap = [(i, i ^ 1) for i in range(32)]
 
-    columns = message(jnp.transpose(cost_volume, (1, 0, 2)), left_image.T)
+    columns = column_message(cost_volume, left_image)
     lines = message(cost_volume, left_image)
     columns = lax.all_to_all(columns, "gy", 0, 0)
-    lines = after(lines, columns)
+    lines = after(lines, columns, pltpu.VMEM)
     lines = lax.all_to_all(lines, "gx", 0, 0, axis_index_groups=chips)
     entry_y = path_states(16, 2, False, numbers, pick, columns)
-    lines = after(lines, entry_y)
+    lines = after(lines, entry_y, pl.ANY)
     others = lax.ppermute(lines, "gx", swap)
 
     entry_y = lax.all_to_all(entry_y, "gy", 0, 0)

time: 104 us -> 103 us (level)
    unnamed x8 -> x12, local copies, waits for them, and re-layouts: 0.01 us -> 1.66 us
  transfers between devices with their start and end apart: 5 -> 5, of which waited for: 3 -> 3; matrix products, arithmetic and copies ran while one was open for 1% -> 2% of each run, Pallas kernels for 32% -> 32%
where the time goes in v6:
time: 103 us
  Pallas kernels  38.3 us (37%)
  starting transfers between devices  36.8 us (36%)
  waiting for transfers between devices  23.8 us (23%)
  local copies, waits for them, and re-layouts  1.94 us (2%)
  other arithmetic  1.56 us (2%)
    pallas_call x2, Pallas kernels, path_states(): pl.pallas_call(partial(path_kernel, blocks, first, two), out_shape=jax.Sh...  30.5 us
    all_to_all x1, starting transfers between devices, on_device(): lines = lax.all_to_all(lines, 'gx', 0, 0, axis_index_groups=chips)  13.7 us
    all_to_all x1, waiting for transfers between devices, on_device(): entry_x = lax.all_to_all(entry_x, 'gx', 0, 0, axis_index_groups=chips)  9.94 us
    all_to_all x1, starting transfers between devices, on_device(): columns = lax.all_to_all(columns, 'gy', 0, 0)  9.39 us
    all_to_all x1, waiting for transfers between devices, on_device(): lines = lax.all_to_all(lines, 'gx', 0, 0, axis_index_groups=chips)  8.11 us
    pallas_call x2, Pallas kernels, replay(): pl.pallas_call(partial(replay_kernel, first, across), out_shape=jax.Shape...  6.2 us
    all_to_all x1, starting transfers between devices, on_device(): entry_x = lax.all_to_all(entry_x, 'gx', 0, 0, axis_index_groups=chips)  6.1 us
    all_to_all x1, waiting for transfers between devices, on_device(): columns = lax.all_to_all(columns, 'gy', 0, 0)  5.79 us
  transfers between devices with their start and end apart: 5, of which 3 were waited for; matrix products, arithmetic and copies ran while one was open for 2% of the time, Pallas kernels for 32%

profile of v6, /device:TPU:2, one launch (start us, length us, event | category | flops | bytes accessed | tf_op | source)
XLA Modules:
  0.0 102.5 jit_solution(12137959409763881920)
XLA Ops:
  0.0 0.0 copy-start
  0.0 0.9 copy-done
  1.0 0.0 copy-start.2
  1.0 0.7 copy-done.2
  1.6 0.0 copy-start.3
  1.7 0.9 column_message.1
  2.5 0.0 copy-start.4
  2.5 0.0 copy-start.5
  2.5 9.4 %all-to-all-start = ((f32[16,40,128]{2,1,0:T(8,128)}), f32[16,40,128]{2,1,0:T(8,128)S(1)}, u32[]{:S(2)}, u32[]{:S(2)}) async-start(f32[16,40,128]{2,1,0:T(8,128)} %column_message.1), calls=%async_computation | async-start | bytes 655360 | tf_op jit(solution)/shard_map/all_to_all | solution.py:303
  11.9 1.0 convert_element_type.9
  12.9 0.0 copy-done.3
  12.9 0.1 tile.9
  13.0 0.1 pad.3.clone
  13.1 0.1 maximum_maximum_fusion.value_ref
  13.2 5.8 %all-to-all-done.earlier_ref.refs_0_ = f32[16,40,128]{2,1,0:T(8,128)S(1)} async-done(((f32[16,40,128]{2,1,0:T(8,128)}), f32[16,40,128]{2,1,0:T(8,128)S(1)}, u32[]{:S(2)}, u32[]{:S(2)}) %all-to-all-start) | async-done | bytes 327712 | tf_op jit(solution)/shard_map/all_to_all | solution.py:303
  19.0 0.7 after.2
  19.7 13.7 %all-to-all-start.1 = ((f32[16,40,128]{2,1,0:T(8,128)}), f32[16,40,128]{2,1,0:T(8,128)S(1)}, u32[]{:S(2)}, u32[]{:S(2)}) async-start(f32[16,40,128]{2,1,0:T(8,128)} %after.2), calls=%async_computation.1 | async-start | bytes 655360 | tf_op jit(solution)/shard_map/all_to_all | solution.py:305
  33.5 0.0 copy-done.4
  33.5 0.0 copy-done.5
  33.5 0.1 concatenate.6.numbers_ref
  33.6 0.5 fusion.pick
  34.1 10.7 %line_paths.2.earlier_ref = f32[16,2,384]{2,1,0:T(2,128)} custom-call(s32[11]{0:T(128)S(1)} %concatenate.6.numbers_ref, bf16[64,128,128]{2,1,0:T(8,128)(2,1)S(1)} %fusion.pick, f32[16,40,128]{2,1,0:T(8,128)S(1)} %all-to-all-done.earlier_ref.refs_0_), custom_call_target="tpu_custom_call" | custom-call | flops 67108864 | bytes 393216 | tf_op jit(solution)/shard_map/line_paths/pallas_call | solution.py:158
  44.8 0.0 copy-start.1
  44.8 8.1 %all-to-all-done.1.value_ref = f32[16,40,128]{2,1,0:T(8,128)S(1)} async-done(((f32[16,40,128]{2,1,0:T(8,128)}), f32[16,40,128]{2,1,0:T(8,128)S(1)}, u32[]{:S(2)}, u32[]{:S(2)}) %all-to-all-start.1) | async-done | bytes 327712 | tf_op jit(solution)/shard_map/all_to_all | solution.py:305
  52.9 1.9 %collective-permute-start = (f32[16,40,128]{2,1,0:T(8,128)S(1)}, f32[16,40,128]{2,1,0:T(8,128)S(1)}, u32[]{:S(2)}, u32[]{:S(2)}) collective-permute-start(f32[16,40,128]{2,1,0:T(8,128)S(1)} %after.3.refs_0_), channel_id=1, source_target_pairs={{0,1},{1,0},{2,3},{3,2},{4,5},{5,4},{6,7},{7,6},{8,9},{9,8},{10,11... | collective-permute-start | bytes 983048 | tf_op jit(solution)/shard_map/ppermute | solution.py:308
  54.9 5.7 %all-to-all-start.3 = ((f32[16,2,384]{2,1,0:T(2,128)}), f32[16,2,384]{2,1,0:T(2,128)S(1)}, u32[]{:S(2)}, u32[]{:S(2)}) async-start(f32[16,2,384]{2,1,0:T(2,128)} %line_paths.2.earlier_ref), calls=%async_computation.3 | async-start | bytes 98304 | tf_op jit(solution)/shard_map/all_to_all | solution.py:310
  60.5 0.0 collective-permute-done.refs_1_
  60.5 19.7 %line_paths.3 = f32[16,2,384]{2,1,0:T(2,128)} custom-call(s32[11]{0:T(128)S(1)} %concatenate.6.numbers_ref, bf16[64,128,128]{2,1,0:T(8,128)(2,1)S(1)} %fusion.pick, f32[16,40,128]{2,1,0:T(8,128)S(1)} %after.3.refs_0_, f32[16,40,128]{2,1,0:T(8,128)S(1)} %collective-permute-done.refs_1_), custom_call_target="tpu_custom_call" | custom-call | flops 134217728 | bytes 786432 | tf_op jit(solution)/shard_map/line_paths/pallas_call | solution.py:158
  80.3 0.0 all-to-all-done.3.entry_ref
  80.3 6.1 %all-to-all-start.2 = ((f32[16,2,384]{2,1,0:T(2,128)}), f32[16,2,384]{2,1,0:T(2,128)S(1)}, u32[]{:S(2)}, u32[]{:S(2)}) async-start(f32[16,2,384]{2,1,0:T(2,128)} %line_paths.3), calls=%async_computation.2 | async-start | bytes 98304 | tf_op jit(solution)/shard_map/all_to_all | solution.py:312
  86.4 0.0 copy-done.1
  86.4 2.7 %block_paths.2.refs_0_ = f32[16,16,256]{2,1,0:T(8,128)S(1)} custom-call(s32[11]{0:T(128)S(1)} %concatenate.6.numbers_ref, f32[16,2,384]{2,1,0:T(2,128)S(1)} %all-to-all-done.3.entry_ref, s32[16,16,256]{2,1,0:T(8,128)S(1)} %copy-done.1), custom_call_target="tpu_custom_call" | custom-call | flops 13107200 | bytes 1048576 | tf_op jit(solution)/shard_map/block_paths/pallas_call | solution.py:226
  89.1 9.9 %all-to-all-done.2.entry_ref = f32[16,2,384]{2,1,0:T(2,128)S(1)} async-done(((f32[16,2,384]{2,1,0:T(2,128)}), f32[16,2,384]{2,1,0:T(2,128)S(1)}, u32[]{:S(2)}, u32[]{:S(2)}) %all-to-all-start.2) | async-done | bytes 49184 | tf_op jit(solution)/shard_map/all_to_all | solution.py:312
  99.0 3.5 %block_paths.3 = f32[16,16,256]{2,1,0:T(8,128)} custom-call(s32[11]{0:T(128)S(1)} %concatenate.6.numbers_ref, f32[16,2,384]{2,1,0:T(2,128)S(1)} %all-to-all-done.2.entry_ref, s32[16,16,256]{2,1,0:T(8,128)S(1)} %copy-done.1, f32[16,16,256]{2,1,0:T(8,128)S(1)} %block_paths.2.refs_0_), custom_call_target="tpu_custom_call" | custom-call | flops 13107200 | bytes 1048576 | tf_op jit(solution)/shard_map/block_paths/pallas_call | solution.py:226
  (6 shorter events, 0.1 us)
Async XLA Ops:
  0.0 0.9 copy-start
  1.0 0.7 copy-start.2
  1.6 11.2 %copy-start.3 = (f32[16,16]{1,0:T(8,128)S(1)}, f32[16,16]{1,0:T(8,128)}, u32[]{:S(2)}) copy-start(f32[16,16]{1,0:T(8,128)} %image_ref.1) | copy-start | bytes 3076
  2.5 31.0 %copy-start.4 = (s32[4]{0:T(128)S(1)}, s32[4]{0:T(128)}, u32[]{:S(2)}) copy-start(s32[4]{0:T(128)} %param.6) | copy-start | bytes 52
  2.5 31.0 %copy-start.5 = (s32[4]{0:T(128)S(1)}, s32[4]{0:T(128)}, u32[]{:S(2)}) copy-start(s32[4]{0:T(128)} %param.7) | copy-start | bytes 52
  2.5 16.5 %all-to-all-start = ((f32[16,40,128]{2,1,0:T(8,128)}), f32[16,40,128]{2,1,0:T(8,128)S(1)}, u32[]{:S(2)}, u32[]{:S(2)}) async-start(f32[16,40,128]{2,1,0:T(8,128)} %column_message.1), calls=%async_computation | async-start | bytes 655360 | tf_op jit(solution)/shard_map/all_to_all | solution.py:303
  19.7 33.2 %all-to-all-start.1 = ((f32[16,40,128]{2,1,0:T(8,128)}), f32[16,40,128]{2,1,0:T(8,128)S(1)}, u32[]{:S(2)}, u32[]{:S(2)}) async-start(f32[16,40,128]{2,1,0:T(8,128)} %after.2), calls=%async_computation.1 | async-start | bytes 655360 | tf_op jit(solution)/shard_map/all_to_all | solution.py:305
  44.8 41.6 %copy-start.1 = (s32[16,16,256]{2,1,0:T(8,128)S(1)}, s32[16,16,256]{2,1,0:T(8,128)}, u32[]{:S(2)}) copy-start(s32[16,16,256]{2,1,0:T(8,128)} %cost_ref.5) | copy-start | bytes 786436
  52.9 7.6 %collective-permute-start = (f32[16,40,128]{2,1,0:T(8,128)S(1)}, f32[16,40,128]{2,1,0:T(8,128)S(1)}, u32[]{:S(2)}, u32[]{:S(2)}) collective-permute-start(f32[16,40,128]{2,1,0:T(8,128)S(1)} %after.3.refs_0_), channel_id=1, source_target_pairs={{0,1},{1,0},{2,3},{3,2},{4,5},{5,4},{6,7},{7,6},{8,9},{9,8},{10,11... | collective-permute-start | bytes 983048 | tf_op jit(solution)/shard_map/ppermute | solution.py:308
  54.9 25.4 %all-to-all-start.3 = ((f32[16,2,384]{2,1,0:T(2,128)}), f32[16,2,384]{2,1,0:T(2,128)S(1)}, u32[]{:S(2)}, u32[]{:S(2)}) async-start(f32[16,2,384]{2,1,0:T(2,128)} %line_paths.2.earlier_ref), calls=%async_computation.3 | async-start | bytes 98304 | tf_op jit(solution)/shard_map/all_to_all | solution.py:310
  80.3 18.7 %all-to-all-start.2 = ((f32[16,2,384]{2,1,0:T(2,128)}), f32[16,2,384]{2,1,0:T(2,128)S(1)}, u32[]{:S(2)}, u32[]{:S(2)}) async-start(f32[16,2,384]{2,1,0:T(2,128)} %line_paths.3), calls=%async_computation.2 | async-start | bytes 98304 | tf_op jit(solution)/shard_map/all_to_all | solution.py:312

commit v7 on v6

--- a/solution.py
+++ b/solution.py
@@ -19,6 +19,10 @@
 
 def adaptive(penalty_one, penalty_two, step_diff):
     return penalty_one + (penalty_two - penalty_one) / (1.0 + GRADIENT_GAIN * jnp.abs(step_diff))
+
+
+def taken(values, lanes):
+    return jnp.take_along_axis(values, lanes, axis=1, mode="promise_in_bounds")
 
 
 def gather_costs(blocks, two, core, sources, scr, img):
@@ -103,7 +107,7 @@
         )
 
     def jump_at(g, i):
-        return jnp.take_along_axis(penalties(g), mirror ^ i, axis=1)
+        return taken(penalties(g), mirror ^ i)
 
     for i in range(AHEAD):
         ready[i] = costs_at(0, i)
@@ -178,18 +182,13 @@
     )(numbers, pick, *sources)
 
 
-def replay_kernel(first, across, numbers_ref, entry_ref, cost_ref, *refs):
-    *so_far, out_ref, line, total, jumps = refs
+def replay_steps(first, place, rows_ref, entry_ref, line, total, jumps):
     lane = lax.broadcasted_iota(jnp.int32, (16, 256), 1)
-    shift = (LANES - 16 * numbers_ref[9 if across else 10]) % LANES
-    cost = cost_ref[...].astype(jnp.float32)
-    line[...] = jnp.swapaxes(cost, 0, 1) if across else cost
-    total[...] = jnp.zeros_like(total)
+    offset = 16 * rows_ref[place : place + 1, :]
     for i in range(2):
-        penalty_two = pltpu.roll(entry_ref[:, i, 256:], shift, 1)
         for at in range(16):
-            jumps[i, at] = jnp.broadcast_to(penalty_two[:, at : at + 1], (16, LANES))
-    small = [numbers_ref[first + i].astype(jnp.float32) for i in range(2)]
+            source = jnp.broadcast_to(offset + at, (16, LANES))
+            jumps[i, at] = taken(entry_ref[:, i, 256:], source)
 
     def lowest_of(x):
         return jnp.broadcast_to(jnp.min(x, axis=1, keepdims=True), (16, LANES))
@@ -197,8 +196,10 @@
     def wide(x):
         return jnp.concatenate([x, x], 1)
 
+    small = [wide(rows_ref[first + i : first + i + 1, :].astype(jnp.float32)) for i in range(2)]
+
     def step(j, carried):
-        after = []
+        done = []
         for i, at in enumerate((j, 15 - j)):
             path, lowest = carried[i]
             cost = line[at]
@@ -209,39 +210,53 @@
             path = jnp.minimum(near, wide(highest) + cost)
             total[at] += path - wide(lowest)
             lowest = jnp.minimum(lowest_of(near), highest + lowest_of(cost))
-            after.append((path, lowest))
-        return tuple(after)
+            done.append((path, lowest))
+        return tuple(done)
 
     paths = [entry_ref[:, i, 0:256] for i in range(2)]
     lax.fori_loop(0, 16, step, tuple((path, lowest_of(path)) for path in paths), unroll=UNROLL)
-    if across:
-        out_ref[...] = (jnp.swapaxes(total[...], 0, 1) + so_far[0][...]) * OUT_SCALE
-    else:
-        out_ref[...] = total[...]
-
-
-def replay(first, across, numbers, entry, cost, *so_far):
-    smem = pl.BlockSpec(memory_space=pltpu.SMEM)
+
+
+def columns_replay_kernel(rows_ref, entry_ref, cost_ref, sum_ref, line_ref, line, total, jumps):
+    cost = cost_ref[...].astype(jnp.float32)
+    line[...] = cost
+    total[...] = jnp.zeros_like(total)
+    replay_steps(2, 10, rows_ref, entry_ref, line, total, jumps)
+    sum_ref[...] = jnp.swapaxes(total[...], 0, 1)
+    line_ref[...] = jnp.swapaxes(cost, 0, 1)
+
+
+def lines_replay_kernel(rows_ref, entry_ref, sum_ref, line_ref, out_ref, total, jumps):
+    total[...] = sum_ref[...]
+    replay_steps(0, 9, rows_ref, entry_ref, line_ref, total, jumps)
+    out_ref[...] = jnp.swapaxes(total[...], 0, 1) * OUT_SCALE
+
+
+def replay(kernel, outs, *operands):
+    block = jax.ShapeDtypeStruct((16, 16, 256), jnp.float32)
     vmem = pl.BlockSpec(memory_space=pltpu.VMEM)
     return pl.pallas_call(
-        partial(replay_kernel, first, across),
-        out_shape=jax.ShapeDtypeStruct((16, 16, 256), jnp.float32),
-        in_specs=[smem] + [vmem] * (2 + len(so_far)),
-        out_specs=vmem,
-        scratch_shapes=[
-            pltpu.VMEM((16, 16, 256), jnp.float32),
-            pltpu.VMEM((16, 16, 256), jnp.float32),
-            pltpu.VMEM((2, 16, 16, LANES), jnp.float32),
-        ],
+        kernel,
+        out_shape=[block] * outs,
+        in_specs=[vmem] * len(operands),
+        out_specs=[vmem] * outs,
+        scratch_shapes=[pltpu.VMEM(block.shape, block.dtype)] * outs
+        + [pltpu.VMEM((2, 16, 16, LANES), jnp.float32)],
         cost_estimate=pl.CostEstimate(
             flops=2 * 65536 * 100, bytes_accessed=2**20, transcendentals=0
         ),
-        compiler_params=pltpu.CompilerParams(vmem_limit_bytes=3 * 2**20),
+        compiler_params=pltpu.CompilerParams(vmem_limit_bytes=4 * 2**20),
         name="block_paths",
-    )(numbers, entry, cost, *so_far)
-
-
-def column_message_kernel(cost_ref, image_ref, out_ref):
+    )(*operands)
+
+
+def column_message_kernel(cost_hbm, image_hbm, out_ref, cost_ref, image_ref, cost_sem, image_sem):
+    cost_copy = pltpu.make_async_copy(cost_hbm, cost_ref, cost_sem)
+    image_copy = pltpu.make_async_copy(image_hbm, image_ref, image_sem)
+    cost_copy.start()
+    image_copy.start()
+    cost_copy.wait()
+    image_copy.wait()
     crossed = jnp.swapaxes(cost_ref[...].astype(jnp.float32), 0, 1)
     out_ref[:, 0:16, :] = crossed[:, :, 0:LANES]
     out_ref[:, 16:32, :] = crossed[:, :, LANES:]
@@ -255,13 +270,18 @@
 
 
 def column_message(cost, image):
-    vmem = pl.BlockSpec(memory_space=pltpu.VMEM)
     return pl.pallas_call(
         column_message_kernel,
         out_shape=jax.ShapeDtypeStruct((16, ROWS, LANES), jnp.float32),
-        in_specs=[vmem] * 2,
-        out_specs=vmem,
-        compiler_params=pltpu.CompilerParams(vmem_limit_bytes=3 * 2**20),
+        in_specs=[pl.BlockSpec(memory_space=pltpu.HBM)] * 2,
+        out_specs=pl.BlockSpec(memory_space=pltpu.VMEM),
+        scratch_shapes=[
+            pltpu.VMEM((16, 16, 256), jnp.int32),
+            pltpu.VMEM((16, 16), jnp.float32),
+            pltpu.SemaphoreType.DMA,
+            pltpu.SemaphoreType.DMA,
+        ],
+        compiler_params=pltpu.CompilerParams(vmem_limit_bytes=56 * 2**20),
         name="column_message",
     )(cost, image)
 
@@ -277,12 +297,28 @@
     out_ref[...] = value_ref[...]
 
 
-def after(value, earlier, space):
+def pass_kernel(value_ref, earlier_ref, out_ref):
+    pass
+
+
+def passed_after(value, earlier):
+    return pl.pallas_call(
+        pass_kernel,
+        out_shape=jax.ShapeDtypeStruct(value.shape, value.dtype),
+        in_specs=[pl.BlockSpec(memory_space=pl.ANY), pl.BlockSpec(memory_space=pltpu.VMEM)],
+        out_specs=pl.BlockSpec(memory_space=pl.ANY),
+        input_output_aliases={0: 0},
+        compiler_params=pltpu.CompilerParams(vmem_limit_bytes=2 * 2**20),
+        name="passed_after",
+    )(value, earlier)
+
+
+def after(value, earlier):
     vmem = pl.BlockSpec(memory_space=pltpu.VMEM)
     return pl.pallas_call(
         after_kernel,
         out_shape=jax.ShapeDtypeStruct(value.shape, value.dtype),
-        in_specs=[vmem, pl.BlockSpec(memory_space=space)],
+        in_specs=[vmem, pl.BlockSpec(memory_space=pl.ANY)],
         out_specs=vmem,
         compiler_params=pltpu.CompilerParams(vmem_limit_bytes=2 * 2**20),
         name="after",
@@ -293,6 +329,7 @@
     index_x, index_y = lax.axis_index("gx"), lax.axis_index("gy")
     here = jnp.stack([index_x % 2, index_x % 4, index_y % 4]).astype(jnp.int32)
     numbers = jnp.concatenate([p_small, p_large, here])
+    rows = jnp.broadcast_to(jnp.pad(numbers, (0, 5))[:, None], (16, LANES))
     step, pixel, path = (lax.broadcasted_iota(jnp.int32, (64, LANES, LANES), i) for i in range(3))
     pick = (pixel == jnp.where(path < 64, step, LANES - 1 - step)).astype(jnp.bfloat16)
     chips = [[2 * z + c for z in range(16)] for c in range(2)]
@@ -301,18 +338,18 @@
     columns = column_message(cost_volume, left_image)
     lines = message(cost_volume, left_image)
     columns = lax.all_to_all(columns, "gy", 0, 0)
-    lines = after(lines, columns, pltpu.VMEM)
+    lines = passed_after(lines, columns)
     lines = lax.all_to_all(lines, "gx", 0, 0, axis_index_groups=chips)
     entry_y = path_states(16, 2, False, numbers, pick, columns)
-    lines = after(lines, entry_y, pl.ANY)
+    lines = after(lines, entry_y)
     others = lax.ppermute(lines, "gx", swap)
 
     entry_y = lax.all_to_all(entry_y, "gy", 0, 0)
     entry_x = path_states(32, 0, True, numbers, pick, lines, others)
     entry_x = lax.all_to_all(entry_x, "gx", 0, 0, axis_index_groups=chips)
 
-    total = replay(2, False, numbers, entry_y, cost_volume)
-    return replay(0, True, numbers, entry_x, cost_volume, total)
+    total, line = replay(columns_replay_kernel, 2, rows, entry_y, cost_volume)
+    return replay(lines_replay_kernel, 1, rows, entry_x, total, line)[0]
 
 
 def solution(mesh):

time: 103 us -> 101 us (0.981)
  local copies, waits for them, and re-layouts: 1.94 us -> 0.37 us
    unnamed x12 -> x8, local copies, waits for them, and re-layouts: 1.66 us -> 0.02 us
    pallas_call x2 -> x3, Pallas kernels: 6.2 us -> 5.08 us  [the longest x2 5.08 us: replay(): pl.pallas_call(kernel, out_shape=[block] * outs, in_specs=[vmem] * len(op...]
  transfers between devices with their start and end apart: 5 -> 5, of which waited for: 3 -> 3; matrix products, arithmetic and copies ran while one was open for 2% -> 3% of each run, Pallas kernels for 32% -> 33%
where the time goes in v7:
time: 101 us
  Pallas kernels  37.8 us (37%)
  starting transfers between devices  36.7 us (36%)
  waiting for transfers between devices  23.4 us (23%)
  other arithmetic  2.28 us (2%)
    pallas_call x2, Pallas kernels, path_states(): pl.pallas_call(partial(path_kernel, blocks, first, two), out_shape=jax.Sh...  30.8 us
    all_to_all x1, starting transfers between devices, on_device(): lines = lax.all_to_all(lines, 'gx', 0, 0, axis_index_groups=chips)  13.7 us
    all_to_all x1, waiting for transfers between devices, on_device(): entry_x = lax.all_to_all(entry_x, 'gx', 0, 0, axis_index_groups=chips)  10.3 us
    all_to_all x1, starting transfers between devices, on_device(): columns = lax.all_to_all(columns, 'gy', 0, 0)  9.27 us
    all_to_all x1, waiting for transfers between devices, on_device(): lines = lax.all_to_all(lines, 'gx', 0, 0, axis_index_groups=chips)  8 us
    all_to_all x1, starting transfers between devices, on_device(): entry_x = lax.all_to_all(entry_x, 'gx', 0, 0, axis_index_groups=chips)  6.1 us
    all_to_all x1, starting transfers between devices, on_device(): entry_y = lax.all_to_all(entry_y, 'gy', 0, 0)  5.67 us
    pallas_call x2, Pallas kernels, replay(): pl.pallas_call(kernel, out_shape=[block] * outs, in_specs=[vmem] * len(op...  5.08 us
  transfers between devices with their start and end apart: 5, of which 3 were waited for; matrix products, arithmetic and copies ran while one was open for 3% of the time, Pallas kernels for 33%

profile of v7, /device:TPU:2, one launch (start us, length us, event | category | flops | bytes accessed | tf_op | source)
XLA Modules:
  0.0 100.7 jit_solution(8519887212871386100)
XLA Ops:
  0.0 0.0 copy-start.1
  0.0 1.8 %column_message.1 = f32[16,40,128]{2,1,0:T(8,128)} custom-call(s32[16,16,256]{2,1,0:T(8,128)} %cost_ref.1, f32[16,16]{1,0:T(8,128)} %image_hbm.1), custom_call_target="tpu_custom_call" | custom-call | tf_op jit(solution)/shard_map/column_message/pallas_call | solution.py:273
  1.8 0.0 copy-start.2
  1.9 0.0 copy-start.3
  1.9 9.3 %all-to-all-start = ((f32[16,40,128]{2,1,0:T(8,128)}), f32[16,40,128]{2,1,0:T(8,128)S(1)}, u32[]{:S(2)}, u32[]{:S(2)}) async-start(f32[16,40,128]{2,1,0:T(8,128)} %column_message.1), calls=%async_computation | async-start | bytes 655360 | tf_op jit(solution)/shard_map/all_to_all | solution.py:340
  11.1 1.0 convert_element_type.9
  12.1 0.0 copy-done.1
  12.2 0.1 tile.9
  12.3 0.1 pad.8.clone
  12.3 0.8 maximum_maximum_fusion.value_ref
  13.2 5.1 %all-to-all-done.earlier_ref.refs_0_ = f32[16,40,128]{2,1,0:T(8,128)S(1)} async-done(((f32[16,40,128]{2,1,0:T(8,128)}), f32[16,40,128]{2,1,0:T(8,128)S(1)}, u32[]{:S(2)}, u32[]{:S(2)}) %all-to-all-start) | async-done | bytes 327712 | tf_op jit(solution)/shard_map/all_to_all | solution.py:340
  18.2 13.7 %all-to-all-start.1 = ((f32[16,40,128]{2,1,0:T(8,128)}), f32[16,40,128]{2,1,0:T(8,128)S(1)}, u32[]{:S(2)}, u32[]{:S(2)}) async-start(f32[16,40,128]{2,1,0:T(8,128)} %passed_after.1), calls=%async_computation.1 | async-start | bytes 655360 | tf_op jit(solution)/shard_map/all_to_all | solution.py:342
  32.0 0.0 copy-done.2
  32.0 0.0 copy-done.3
  32.0 0.1 concatenate.6.numbers_ref
  32.1 0.5 fusion.pick
  32.6 10.9 %line_paths.2.earlier_ref = f32[16,2,384]{2,1,0:T(2,128)} custom-call(s32[11]{0:T(128)S(1)} %concatenate.6.numbers_ref, bf16[64,128,128]{2,1,0:T(8,128)(2,1)S(1)} %fusion.pick, f32[16,40,128]{2,1,0:T(8,128)S(1)} %all-to-all-done.earlier_ref.refs_0_), custom_call_target="tpu_custom_call" | custom-call | flops 67108864 | bytes 393216 | tf_op jit(solution)/shard_map/line_paths/pallas_call | solution.py:162
  43.4 0.0 copy-start
  43.4 8.0 %all-to-all-done.1.value_ref = f32[16,40,128]{2,1,0:T(8,128)S(1)} async-done(((f32[16,40,128]{2,1,0:T(8,128)}), f32[16,40,128]{2,1,0:T(8,128)S(1)}, u32[]{:S(2)}, u32[]{:S(2)}) %all-to-all-start.1) | async-done | bytes 327712 | tf_op jit(solution)/shard_map/all_to_all | solution.py:342
  51.4 1.9 %collective-permute-start = (f32[16,40,128]{2,1,0:T(8,128)S(1)}, f32[16,40,128]{2,1,0:T(8,128)S(1)}, u32[]{:S(2)}, u32[]{:S(2)}) collective-permute-start(f32[16,40,128]{2,1,0:T(8,128)S(1)} %after.1.refs_0_), channel_id=1, source_target_pairs={{0,1},{1,0},{2,3},{3,2},{4,5},{5,4},{6,7},{7,6},{8,9},{9,8},{10,11... | collective-permute-start | bytes 983048 | tf_op jit(solution)/shard_map/ppermute | solution.py:345
  53.4 5.7 %all-to-all-start.3 = ((f32[16,2,384]{2,1,0:T(2,128)}), f32[16,2,384]{2,1,0:T(2,128)S(1)}, u32[]{:S(2)}, u32[]{:S(2)}) async-start(f32[16,2,384]{2,1,0:T(2,128)} %line_paths.2.earlier_ref), calls=%async_computation.3 | async-start | bytes 98304 | tf_op jit(solution)/shard_map/all_to_all | solution.py:347
  59.0 0.0 collective-permute-done.refs_1_
  59.1 20.0 %line_paths.3 = f32[16,2,384]{2,1,0:T(2,128)} custom-call(s32[11]{0:T(128)S(1)} %concatenate.6.numbers_ref, bf16[64,128,128]{2,1,0:T(8,128)(2,1)S(1)} %fusion.pick, f32[16,40,128]{2,1,0:T(8,128)S(1)} %after.1.refs_0_, f32[16,40,128]{2,1,0:T(8,128)S(1)} %collective-permute-done.refs_1_), custom_call_target="tpu_custom_call" | custom-call | flops 134217728 | bytes 786432 | tf_op jit(solution)/shard_map/line_paths/pallas_call | solution.py:162
  79.0 0.0 all-to-all-done.3.entry_ref
  79.0 6.1 %all-to-all-start.2 = ((f32[16,2,384]{2,1,0:T(2,128)}), f32[16,2,384]{2,1,0:T(2,128)S(1)}, u32[]{:S(2)}, u32[]{:S(2)}) async-start(f32[16,2,384]{2,1,0:T(2,128)} %line_paths.3), calls=%async_computation.2 | async-start | bytes 98304 | tf_op jit(solution)/shard_map/all_to_all | solution.py:349
  85.2 0.1 broadcast_in_dim.4.rows_ref
  85.2 0.0 copy-done
  85.2 2.2 %block_paths.2 = (f32[16,16,256]{2,1,0:T(8,128)S(1)}, f32[16,16,256]{2,1,0:T(8,128)S(1)}) custom-call(s32[16,128]{1,0:T(8,128)S(1)} %broadcast_in_dim.4.rows_ref, f32[16,2,384]{2,1,0:T(2,128)S(1)} %all-to-all-done.3.entry_ref, s32[16,16,256]{2,1,0:T(8,128)S(1)} %copy-done), custom_call_target="tpu_custom_call" | custom-call | flops 13107200 | bytes 1048576 | tf_op jit(solution)/shard_map/block_paths/pallas_call | solution.py:238
  87.4 10.3 %all-to-all-done.2.entry_ref = f32[16,2,384]{2,1,0:T(2,128)S(1)} async-done(((f32[16,2,384]{2,1,0:T(2,128)}), f32[16,2,384]{2,1,0:T(2,128)S(1)}, u32[]{:S(2)}, u32[]{:S(2)}) %all-to-all-start.2) | async-done | bytes 49184 | tf_op jit(solution)/shard_map/all_to_all | solution.py:349
  97.8 2.9 %block_paths.3 = f32[16,16,256]{2,1,0:T(8,128)} custom-call(s32[16,128]{1,0:T(8,128)S(1)} %broadcast_in_dim.4.rows_ref, f32[16,2,384]{2,1,0:T(2,128)S(1)} %all-to-all-done.2.entry_ref, f32[16,16,256]{2,1,0:T(8,128)S(1)} %get-tuple-element.7.sum_ref, f32[16,16,256]{2,1,0:T(8,128)S(1)} %get-tuple-element.8.line_ref), custom_call_target="tpu_custom_call" | custom-call | flops 13107200 | bytes 1048576 | tf_op jit(solution)/shard_map/block_paths/pallas_call | solution.py:238
  (8 shorter events, 0.1 us)
Async XLA Ops:
  0.0 12.1 %copy-start.1 = (f32[16,16]{1,0:T(8,128)S(1)}, f32[16,16]{1,0:T(8,128)}, u32[]{:S(2)}) copy-start(f32[16,16]{1,0:T(8,128)} %image_hbm.1) | copy-start | bytes 3076
  1.8 30.1 %copy-start.2 = (s32[4]{0:T(128)S(1)}, s32[4]{0:T(128)}, u32[]{:S(2)}) copy-start(s32[4]{0:T(128)} %param.6) | copy-start | bytes 52
  1.9 30.1 %copy-start.3 = (s32[4]{0:T(128)S(1)}, s32[4]{0:T(128)}, u32[]{:S(2)}) copy-start(s32[4]{0:T(128)} %param.7) | copy-start | bytes 52
  1.9 16.4 %all-to-all-start = ((f32[16,40,128]{2,1,0:T(8,128)}), f32[16,40,128]{2,1,0:T(8,128)S(1)}, u32[]{:S(2)}, u32[]{:S(2)}) async-start(f32[16,40,128]{2,1,0:T(8,128)} %column_message.1), calls=%async_computation | async-start | bytes 655360 | tf_op jit(solution)/shard_map/all_to_all | solution.py:340
  18.2 33.2 %all-to-all-start.1 = ((f32[16,40,128]{2,1,0:T(8,128)}), f32[16,40,128]{2,1,0:T(8,128)S(1)}, u32[]{:S(2)}, u32[]{:S(2)}) async-start(f32[16,40,128]{2,1,0:T(8,128)} %passed_after.1), calls=%async_computation.1 | async-start | bytes 655360 | tf_op jit(solution)/shard_map/all_to_all | solution.py:342
  43.4 41.8 %copy-start = (s32[16,16,256]{2,1,0:T(8,128)S(1)}, s32[16,16,256]{2,1,0:T(8,128)}, u32[]{:S(2)}) copy-start(s32[16,16,256]{2,1,0:T(8,128)} %cost_ref.1) | copy-start | bytes 786436
  51.4 7.6 %collective-permute-start = (f32[16,40,128]{2,1,0:T(8,128)S(1)}, f32[16,40,128]{2,1,0:T(8,128)S(1)}, u32[]{:S(2)}, u32[]{:S(2)}) collective-permute-start(f32[16,40,128]{2,1,0:T(8,128)S(1)} %after.1.refs_0_), channel_id=1, source_target_pairs={{0,1},{1,0},{2,3},{3,2},{4,5},{5,4},{6,7},{7,6},{8,9},{9,8},{10,11... | collective-permute-start | bytes 983048 | tf_op jit(solution)/shard_map/ppermute | solution.py:345
  53.4 25.7 %all-to-all-start.3 = ((f32[16,2,384]{2,1,0:T(2,128)}), f32[16,2,384]{2,1,0:T(2,128)S(1)}, u32[]{:S(2)}, u32[]{:S(2)}) async-start(f32[16,2,384]{2,1,0:T(2,128)} %line_paths.2.earlier_ref), calls=%async_computation.3 | async-start | bytes 98304 | tf_op jit(solution)/shard_map/all_to_all | solution.py:347
  79.0 18.8 %all-to-all-start.2 = ((f32[16,2,384]{2,1,0:T(2,128)}), f32[16,2,384]{2,1,0:T(2,128)S(1)}, u32[]{:S(2)}, u32[]{:S(2)}) async-start(f32[16,2,384]{2,1,0:T(2,128)} %line_paths.3), calls=%async_computation.2 | async-start | bytes 98304 | tf_op jit(solution)/shard_map/all_to_all | solution.py:349

commit v8 on v7

--- a/solution.py
+++ b/solution.py
@@ -13,7 +13,7 @@
 LANES = 128
 TILES = 32
 UNROLL = 4
-AHEAD = 3
+AHEAD = 4
 ROWS = 40
 
 
@@ -40,12 +40,13 @@
     lax.fori_loop(0, 16, fetch, 0, unroll=4)
 
 
-def path_kernel(blocks, first, two, numbers_ref, pick, *refs):
+def path_kernel(blocks, first, two, rows_ref, pick, *refs):
     sources, (out_ref, scr, img, ahead, back, costs, ready, starts, states) = refs[:-9], refs[-9:]
     groups = blocks // 4
     lane = lax.broadcasted_iota(jnp.int32, (8, LANES), 1)
     sub = lax.broadcasted_iota(jnp.int32, (8, LANES), 0)
-    gather_costs(blocks, two, numbers_ref[8], sources, scr, img)
+    core = lax.axis_index("gx") % 2 if two else 0
+    gather_costs(blocks, two, core, sources, scr, img)
 
     place, row = lane[:groups] % 64, sub[:groups]
     line = img[pl.ds(0, groups, stride=4), :]
@@ -57,8 +58,10 @@
     after = pltpu.roll(line, LANES - 1, 1)
     wrapped = jnp.concatenate([after[1:], after[:1]], 0)
     after = jnp.where(place == 63, jnp.where(row == groups - 1, 0.0, wrapped), after)
-    small = [numbers_ref[first + i].astype(jnp.float32) for i in range(2)]
-    large = [numbers_ref[4 + first + i].astype(jnp.float32) for i in range(2)]
+    small, large = (
+        [rows_ref[at + i : at + i + 1, :].astype(jnp.float32) for i in range(2)]
+        for at in (first, 4 + first)
+    )
     ahead[...] = adaptive(small[0], large[0], line - before)
     back[...] = adaptive(small[1], large[1], line - after)
     forward = lane < 64
@@ -95,9 +98,9 @@
             level = halved(level)
         return across_sublanes(level[0])
 
-    def costs_at(g, i):
-        cost = jnp.dot(costs[g], pick[i], preferred_element_type=jnp.float32)
-        return cost.reshape(TILES, 8, LANES)
+    def costs_at(g, pair):
+        both = jnp.dot(costs[g], pick[pair], preferred_element_type=jnp.float32)
+        return [both[:, at : at + LANES].reshape(TILES, 8, LANES) for at in (0, LANES)]
 
     def penalties(g):
         return jnp.where(
@@ -109,26 +112,25 @@
     def jump_at(g, i):
         return taken(penalties(g), mirror ^ i)
 
-    for i in range(AHEAD):
-        ready[i] = costs_at(0, i)
-
-    def segments(t, carried):
+    for i in range(0, AHEAD, 2):
+        ready[i], ready[i + 1] = costs_at(0, i // 2)
+
+    def group(g, carried):
         *path, jump = carried
-        g = t >> 1
-        base = (t & 1) << 5
-        later = jnp.minimum(t + 1, blocks // 2 - 1)
+        later = jnp.minimum(g + 1, groups - 1)
         lowest = lowest_of(path)
-        ordered = penalty_one
-        for i in range(32):
+        for i in range(64):
             if i % 16 == 0:
                 path = [x - lowest for x in path]
                 lowest = jnp.zeros_like(lowest)
-                here = (lane & 63) == 2 * t + i // 16
+                here = (lane & 63) == 4 * g + i // 16
                 for v in range(TILES):
                     starts[v] = jnp.where(here, path[v], starts[v])
-            highest = lowest + (jump if i == 0 else jump_at(g, base + i))
-            cost = ready[i] if i < AHEAD else costs_at(g, base + i)
-            raised = [x + ordered for x in path]
+            highest = lowest + (jump if i == 0 else jump_at(g, i))
+            if i >= AHEAD and i % 2 == 0:
+                pair = costs_at(g, i // 2)
+            cost = ready[i] if i < AHEAD else pair[i % 2]
+            raised = [x + penalty_one for x in path]
             below = jnp.where(sub == 0, FAR, pltpu.roll(raised[-1], 1, 0))
             above = jnp.where(sub == 7, FAR, pltpu.roll(raised[0], 7, 0))
             padded = [below, *raised, above]
@@ -136,33 +138,30 @@
                 jnp.minimum(path[v], jnp.minimum(padded[v], padded[v + 2])) for v in range(TILES)
             ]
             path = [jnp.minimum(near[v], highest) + cost[v] for v in range(TILES)]
-            pairs = halved(path)
-            ordered = jnp.maximum(penalty_one, jnp.minimum(pairs[-1], -FAR))
-            lowest = lowest_of(pairs)
-            if i == 20:
-                jump = jump_at(later >> 1, (later & 1) << 5)
-                for k in range(AHEAD):
-                    ready[k] = costs_at(later >> 1, ((later & 1) << 5) + k)
+            lowest = lowest_of(path)
+            if i == 58:
+                jump = jump_at(later, 0)
+                for k in range(0, AHEAD, 2):
+                    ready[k], ready[k + 1] = costs_at(later, k // 2)
         return (*path, jump)
 
     zero = jnp.zeros((8, LANES), jnp.float32)
-    lax.fori_loop(0, blocks // 2, segments, (zero,) * TILES + (jump_at(0, 0),))
+    lax.fori_loop(0, groups, group, (zero,) * TILES + (jump_at(0, 0),))
     states[...] = jnp.concatenate([starts[:, s, :] for s in range(8)], 0).T
     for z in range(16):
-        block = 2 * z + numbers_ref[8] if two else z
+        block = 2 * z + core if two else z
         fore, rear = ahead[pl.ds(block // 4, 1), :], back[pl.ds(block // 4, 1), :]
         start, end = states[pl.ds(block, 1), :], states[pl.ds(64 + blocks - 1 - block, 1), :]
         out_ref[z, 0:1, :] = jnp.concatenate([start, fore], 1)
         out_ref[z, 1:2, :] = jnp.concatenate([end, rear], 1)
 
 
-def path_states(blocks, first, two, numbers, pick, *sources):
-    smem = pl.BlockSpec(memory_space=pltpu.SMEM)
+def path_states(blocks, first, two, rows, pick, *sources):
     vmem = pl.BlockSpec(memory_space=pltpu.VMEM)
     return pl.pallas_call(
         partial(path_kernel, blocks, first, two),
         out_shape=jax.ShapeDtypeStruct((16, 2, 384), jnp.float32),
-        in_specs=[smem] + [vmem] * (1 + len(sources)),
+        in_specs=[vmem] * (2 + len(sources)),
         out_specs=vmem,
         scratch_shapes=[
             pltpu.VMEM((blocks, 16, 256), jnp.bfloat16),
@@ -179,7 +178,7 @@
             flops=blocks * 16 * 256 * 128 * 8, bytes_accessed=blocks * 24 * 1024, transcendentals=0
         ),
         name="line_paths",
-    )(numbers, pick, *sources)
+    )(rows, pick, *sources)
 
 
 def replay_steps(first, place, rows_ref, entry_ref, line, total, jumps):
@@ -221,14 +220,14 @@
     cost = cost_ref[...].astype(jnp.float32)
     line[...] = cost
     total[...] = jnp.zeros_like(total)
-    replay_steps(2, 10, rows_ref, entry_ref, line, total, jumps)
+    replay_steps(2, 9, rows_ref, entry_ref, line, total, jumps)
     sum_ref[...] = jnp.swapaxes(total[...], 0, 1)
     line_ref[...] = jnp.swapaxes(cost, 0, 1)
 
 
 def lines_replay_kernel(rows_ref, entry_ref, sum_ref, line_ref, out_ref, total, jumps):
     total[...] = sum_ref[...]
-    replay_steps(0, 9, rows_ref, entry_ref, line_ref, total, jumps)
+    replay_steps(0, 8, rows_ref, entry_ref, line_ref, total, jumps)
     out_ref[...] = jnp.swapaxes(total[...], 0, 1) * OUT_SCALE
 
 
@@ -327,11 +326,14 @@
 
 def on_device(cost_volume, left_image, p_small, p_large):
     index_x, index_y = lax.axis_index("gx"), lax.axis_index("gy")
-    here = jnp.stack([index_x % 2, index_x % 4, index_y % 4]).astype(jnp.int32)
+    here = jnp.stack([index_x % 4, index_y % 4]).astype(jnp.int32)
     numbers = jnp.concatenate([p_small, p_large, here])
-    rows = jnp.broadcast_to(jnp.pad(numbers, (0, 5))[:, None], (16, LANES))
-    step, pixel, path = (lax.broadcasted_iota(jnp.int32, (64, LANES, LANES), i) for i in range(3))
-    pick = (pixel == jnp.where(path < 64, step, LANES - 1 - step)).astype(jnp.bfloat16)
+    rows = jnp.broadcast_to(jnp.pad(numbers, (0, 6))[:, None], (16, LANES))
+    pair, pixel, path = (
+        lax.broadcasted_iota(jnp.int32, (32, LANES, 2 * LANES), i) for i in range(3)
+    )
+    step = 2 * pair + path // LANES
+    pick = (pixel == jnp.where(path % LANES < 64, step, LANES - 1 - step)).astype(jnp.bfloat16)
     chips = [[2 * z + c for z in range(16)] for c in range(2)]
     swap = [(i, i ^ 1) for i in range(32)]
 
@@ -340,12 +342,12 @@
     columns = lax.all_to_all(columns, "gy", 0, 0)
     lines = passed_after(lines, columns)
     lines = lax.all_to_all(lines, "gx", 0, 0, axis_index_groups=chips)
-    entry_y = path_states(16, 2, False, numbers, pick, columns)
+    entry_y = path_states(16, 2, False, rows, pick, columns)
     lines = after(lines, entry_y)
     others = lax.ppermute(lines, "gx", swap)
 
     entry_y = lax.all_to_all(entry_y, "gy", 0, 0)
-    entry_x = path_states(32, 0, True, numbers, pick, lines, others)
+    entry_x = path_states(32, 0, True, rows, pick, lines, others)
     entry_x = lax.all_to_all(entry_x, "gx", 0, 0, axis_index_groups=chips)
 
     total, line = replay(columns_replay_kernel, 2, rows, entry_y, cost_volume)

time: 101 us -> 100 us (0.990)
  Pallas kernels: 37.8 us -> 36.1 us
    pallas_call x2, Pallas kernels: 30.8 us -> 29.2 us  [path_states(): pl.pallas_call(partial(path_kernel, blocks, first, two), out_shape=jax.Sh...]
  transfers between devices with their start and end apart: 5 -> 5, of which waited for: 3 -> 3; matrix products, arithmetic and copies ran while one was open for 3% -> 3% of each run, Pallas kernels for 33% -> 31%
where the time goes in v8:
time: 100 us; the launch traced here: 99.8 us
  starting transfers between devices  36.6 us (37%)
  Pallas kernels  36.1 us (36%)
  waiting for transfers between devices  24.2 us (24%)
  other arithmetic  2.31 us (2%)
    pallas_call x2, Pallas kernels, path_states(): pl.pallas_call(partial(path_kernel, blocks, first, two), out_shape=jax.Sh...  29.2 us
    all_to_all x1, starting transfers between devices, on_device(): lines = lax.all_to_all(lines, 'gx', 0, 0, axis_index_groups=chips)  13.7 us
    all_to_all x1, waiting for transfers between devices, on_device(): entry_x = lax.all_to_all(entry_x, 'gx', 0, 0, axis_index_groups=chips)  10.4 us
    all_to_all x1, starting transfers between devices, on_device(): columns = lax.all_to_all(columns, 'gy', 0, 0)  9.27 us
    all_to_all x1, waiting for transfers between devices, on_device(): lines = lax.all_to_all(lines, 'gx', 0, 0, axis_index_groups=chips)  8.74 us
    all_to_all x1, starting transfers between devices, on_device(): entry_x = lax.all_to_all(entry_x, 'gx', 0, 0, axis_index_groups=chips)  6.09 us
    all_to_all x1, starting transfers between devices, on_device(): entry_y = lax.all_to_all(entry_y, 'gy', 0, 0)  5.67 us
    all_to_all x1, waiting for transfers between devices, on_device(): columns = lax.all_to_all(columns, 'gy', 0, 0)  5.08 us
  transfers between devices with their start and end apart: 5, of which 3 were waited for; matrix products, arithmetic and copies ran while one was open for 3% of the time, Pallas kernels for 31%

profile of v8, /device:TPU:2, one launch (start us, length us, event | category | flops | bytes accessed | tf_op | source)
XLA Modules:
  0.0 99.8 jit_solution(6269642436661667386)
XLA Ops:
  0.0 0.0 copy-start.1
  0.0 1.8 %column_message.1 = f32[16,40,128]{2,1,0:T(8,128)} custom-call(s32[16,16,256]{2,1,0:T(8,128)} %cost_ref.1, f32[16,16]{1,0:T(8,128)} %image_hbm.1), custom_call_target="tpu_custom_call" | custom-call | tf_op jit(solution)/shard_map/column_message/pallas_call | solution.py:272
  1.8 0.0 copy-start.2
  1.8 0.0 copy-start.3
  1.9 9.3 %all-to-all-start = ((f32[16,40,128]{2,1,0:T(8,128)}), f32[16,40,128]{2,1,0:T(8,128)S(1)}, u32[]{:S(2)}, u32[]{:S(2)}) async-start(f32[16,40,128]{2,1,0:T(8,128)} %column_message.1), calls=%async_computation | async-start | bytes 655360 | tf_op jit(solution)/shard_map/all_to_all | solution.py:342
  11.1 1.0 convert_element_type.9
  12.1 0.0 copy-done.1
  12.2 0.1 tile.9
  12.3 0.1 pad.8.clone
  12.3 0.8 maximum_maximum_fusion.value_ref
  13.1 5.1 %all-to-all-done.earlier_ref.refs_0_ = f32[16,40,128]{2,1,0:T(8,128)S(1)} async-done(((f32[16,40,128]{2,1,0:T(8,128)}), f32[16,40,128]{2,1,0:T(8,128)S(1)}, u32[]{:S(2)}, u32[]{:S(2)}) %all-to-all-start) | async-done | bytes 327712 | tf_op jit(solution)/shard_map/all_to_all | solution.py:342
  18.2 13.7 %all-to-all-start.1 = ((f32[16,40,128]{2,1,0:T(8,128)}), f32[16,40,128]{2,1,0:T(8,128)S(1)}, u32[]{:S(2)}, u32[]{:S(2)}) async-start(f32[16,40,128]{2,1,0:T(8,128)} %passed_after.1), calls=%async_computation.1 | async-start | bytes 655360 | tf_op jit(solution)/shard_map/all_to_all | solution.py:344
  31.9 0.0 copy-done.2
  32.0 0.0 copy-done.3
  32.0 0.1 pad_add_fusion
  32.1 0.4 fusion.1.pick
  32.5 0.1 broadcast_in_dim.4.rows_ref
  32.6 10.1 %line_paths.2.earlier_ref = f32[16,2,384]{2,1,0:T(2,128)} custom-call(s32[16,128]{1,0:T(8,128)S(1)} %broadcast_in_dim.4.rows_ref, bf16[32,128,256]{2,1,0:T(8,128)(2,1)S(1)} %fusion.1.pick, f32[16,40,128]{2,1,0:T(8,128)S(1)} %all-to-all-done.earlier_ref.refs_0_), custom_call_target="tpu_custom_call" | custom-call | flops 67108864 | bytes 393216 | tf_op jit(solution)/shard_map/line_paths/pallas_call | solution.py:161
  42.7 0.0 copy-start
  42.7 8.7 %all-to-all-done.1.value_ref = f32[16,40,128]{2,1,0:T(8,128)S(1)} async-done(((f32[16,40,128]{2,1,0:T(8,128)}), f32[16,40,128]{2,1,0:T(8,128)S(1)}, u32[]{:S(2)}, u32[]{:S(2)}) %all-to-all-start.1) | async-done | bytes 327712 | tf_op jit(solution)/shard_map/all_to_all | solution.py:344
  51.4 1.9 %collective-permute-start = (f32[16,40,128]{2,1,0:T(8,128)S(1)}, f32[16,40,128]{2,1,0:T(8,128)S(1)}, u32[]{:S(2)}, u32[]{:S(2)}) collective-permute-start(f32[16,40,128]{2,1,0:T(8,128)S(1)} %after.1.refs_0_), channel_id=1, source_target_pairs={{0,1},{1,0},{2,3},{3,2},{4,5},{5,4},{6,7},{7,6},{8,9},{9,8},{10,11... | collective-permute-start | bytes 983048 | tf_op jit(solution)/shard_map/ppermute | solution.py:347
  53.4 5.7 %all-to-all-start.3 = ((f32[16,2,384]{2,1,0:T(2,128)}), f32[16,2,384]{2,1,0:T(2,128)S(1)}, u32[]{:S(2)}, u32[]{:S(2)}) async-start(f32[16,2,384]{2,1,0:T(2,128)} %line_paths.2.earlier_ref), calls=%async_computation.3 | async-start | bytes 98304 | tf_op jit(solution)/shard_map/all_to_all | solution.py:349
  59.0 0.0 collective-permute-done.refs_1_
  59.0 19.1 %line_paths.3 = f32[16,2,384]{2,1,0:T(2,128)} custom-call(s32[16,128]{1,0:T(8,128)S(1)} %broadcast_in_dim.4.rows_ref, bf16[32,128,256]{2,1,0:T(8,128)(2,1)S(1)} %fusion.1.pick, f32[16,40,128]{2,1,0:T(8,128)S(1)} %after.1.refs_0_, f32[16,40,128]{2,1,0:T(8,128)S(1)} %collective-permute-done.refs_1_), custom_call_target="tpu_custom_call" | custom-call | flops 134217728 | bytes 786432 | tf_op jit(solution)/shard_map/line_paths/pallas_call | solution.py:161
  78.2 0.0 all-to-all-done.3.entry_ref
  78.2 6.1 %all-to-all-start.2 = ((f32[16,2,384]{2,1,0:T(2,128)}), f32[16,2,384]{2,1,0:T(2,128)S(1)}, u32[]{:S(2)}, u32[]{:S(2)}) async-start(f32[16,2,384]{2,1,0:T(2,128)} %line_paths.3), calls=%async_computation.2 | async-start | bytes 98304 | tf_op jit(solution)/shard_map/all_to_all | solution.py:351
  84.3 0.0 copy-done
  84.3 2.2 %block_paths.2 = (f32[16,16,256]{2,1,0:T(8,128)S(1)}, f32[16,16,256]{2,1,0:T(8,128)S(1)}) custom-call(s32[16,128]{1,0:T(8,128)S(1)} %broadcast_in_dim.4.rows_ref, f32[16,2,384]{2,1,0:T(2,128)S(1)} %all-to-all-done.3.entry_ref, s32[16,16,256]{2,1,0:T(8,128)S(1)} %copy-done), custom_call_target="tpu_custom_call" | custom-call | flops 13107200 | bytes 1048576 | tf_op jit(solution)/shard_map/block_paths/pallas_call | solution.py:237
  86.5 10.4 %all-to-all-done.2.entry_ref = f32[16,2,384]{2,1,0:T(2,128)S(1)} async-done(((f32[16,2,384]{2,1,0:T(2,128)}), f32[16,2,384]{2,1,0:T(2,128)S(1)}, u32[]{:S(2)}, u32[]{:S(2)}) %all-to-all-start.2) | async-done | bytes 49184 | tf_op jit(solution)/shard_map/all_to_all | solution.py:351
  96.9 2.9 %block_paths.3 = f32[16,16,256]{2,1,0:T(8,128)} custom-call(s32[16,128]{1,0:T(8,128)S(1)} %broadcast_in_dim.4.rows_ref, f32[16,2,384]{2,1,0:T(2,128)S(1)} %all-to-all-done.2.entry_ref, f32[16,16,256]{2,1,0:T(8,128)S(1)} %get-tuple-element.7.sum_ref, f32[16,16,256]{2,1,0:T(8,128)S(1)} %get-tuple-element.8.line_ref), custom_call_target="tpu_custom_call" | custom-call | flops 13107200 | bytes 1048576 | tf_op jit(solution)/shard_map/block_paths/pallas_call | solution.py:237
  (10 shorter events, 0.1 us)
Async XLA Ops:
  0.0 12.1 %copy-start.1 = (f32[16,16]{1,0:T(8,128)S(1)}, f32[16,16]{1,0:T(8,128)}, u32[]{:S(2)}) copy-start(f32[16,16]{1,0:T(8,128)} %image_hbm.1) | copy-start | bytes 3076
  1.8 30.1 %copy-start.2 = (s32[4]{0:T(128)S(1)}, s32[4]{0:T(128)}, u32[]{:S(2)}) copy-start(s32[4]{0:T(128)} %param.7) | copy-start | bytes 52
  1.8 30.1 %copy-start.3 = (s32[4]{0:T(128)S(1)}, s32[4]{0:T(128)}, u32[]{:S(2)}) copy-start(s32[4]{0:T(128)} %param.6) | copy-start | bytes 52
  1.9 16.4 %all-to-all-start = ((f32[16,40,128]{2,1,0:T(8,128)}), f32[16,40,128]{2,1,0:T(8,128)S(1)}, u32[]{:S(2)}, u32[]{:S(2)}) async-start(f32[16,40,128]{2,1,0:T(8,128)} %column_message.1), calls=%async_computation | async-start | bytes 655360 | tf_op jit(solution)/shard_map/all_to_all | solution.py:342
  18.2 33.2 %all-to-all-start.1 = ((f32[16,40,128]{2,1,0:T(8,128)}), f32[16,40,128]{2,1,0:T(8,128)S(1)}, u32[]{:S(2)}, u32[]{:S(2)}) async-start(f32[16,40,128]{2,1,0:T(8,128)} %passed_after.1), calls=%async_computation.1 | async-start | bytes 655360 | tf_op jit(solution)/shard_map/all_to_all | solution.py:344
  42.7 41.6 %copy-start = (s32[16,16,256]{2,1,0:T(8,128)S(1)}, s32[16,16,256]{2,1,0:T(8,128)}, u32[]{:S(2)}) copy-start(s32[16,16,256]{2,1,0:T(8,128)} %cost_ref.1) | copy-start | bytes 786436
  51.4 7.6 %collective-permute-start = (f32[16,40,128]{2,1,0:T(8,128)S(1)}, f32[16,40,128]{2,1,0:T(8,128)S(1)}, u32[]{:S(2)}, u32[]{:S(2)}) collective-permute-start(f32[16,40,128]{2,1,0:T(8,128)S(1)} %after.1.refs_0_), channel_id=1, source_target_pairs={{0,1},{1,0},{2,3},{3,2},{4,5},{5,4},{6,7},{7,6},{8,9},{9,8},{10,11... | collective-permute-start | bytes 983048 | tf_op jit(solution)/shard_map/ppermute | solution.py:347
  53.4 24.8 %all-to-all-start.3 = ((f32[16,2,384]{2,1,0:T(2,128)}), f32[16,2,384]{2,1,0:T(2,128)S(1)}, u32[]{:S(2)}, u32[]{:S(2)}) async-start(f32[16,2,384]{2,1,0:T(2,128)} %line_paths.2.earlier_ref), calls=%async_computation.3 | async-start | bytes 98304 | tf_op jit(solution)/shard_map/all_to_all | solution.py:349
  78.2 18.7 %all-to-all-start.2 = ((f32[16,2,384]{2,1,0:T(2,128)}), f32[16,2,384]{2,1,0:T(2,128)S(1)}, u32[]{:S(2)}, u32[]{:S(2)}) async-start(f32[16,2,384]{2,1,0:T(2,128)} %line_paths.3), calls=%async_computation.2 | async-start | bytes 98304 | tf_op jit(solution)/shard_map/all_to_all | solution.py:351

commit v9 on v8

--- a/solution.py
+++ b/solution.py
@@ -165,7 +165,7 @@
         out_specs=vmem,
         scratch_shapes=[
             pltpu.VMEM((blocks, 16, 256), jnp.bfloat16),
-            pltpu.VMEM((blocks, LANES), jnp.float32),
+            pltpu.VMEM((32, LANES), jnp.float32),
             pltpu.VMEM((blocks // 4, LANES), jnp.float32),
             pltpu.VMEM((blocks // 4, LANES), jnp.float32),
             pltpu.VMEM((blocks // 4, 256, LANES), jnp.bfloat16),

time: 100 us -> 100 us (level)
  no operation moved by 1% of the time
where the time goes in v9:
time: 100 us; the launch traced here: 99.8 us
  starting transfers between devices  36.6 us (37%)
  Pallas kernels  36.1 us (36%)
  waiting for transfers between devices  24.3 us (24%)
  other arithmetic  2.31 us (2%)
    pallas_call x2, Pallas kernels, path_states(): pl.pallas_call(partial(path_kernel, blocks, first, two), out_shape=jax.Sh...  29.2 us
    all_to_all x1, starting transfers between devices, on_device(): lines = lax.all_to_all(lines, 'gx', 0, 0, axis_index_groups=chips)  13.7 us
    all_to_all x1, waiting for transfers between devices, on_device(): entry_x = lax.all_to_all(entry_x, 'gx', 0, 0, axis_index_groups=chips)  10.4 us
    all_to_all x1, starting transfers between devices, on_device(): columns = lax.all_to_all(columns, 'gy', 0, 0)  9.27 us
    all_to_all x1, waiting for transfers between devices, on_device(): lines = lax.all_to_all(lines, 'gx', 0, 0, axis_index_groups=chips)  8.75 us
    all_to_all x1, starting transfers between devices, on_device(): entry_x = lax.all_to_all(entry_x, 'gx', 0, 0, axis_index_groups=chips)  6.09 us
    all_to_all x1, starting transfers between devices, on_device(): entry_y = lax.all_to_all(entry_y, 'gy', 0, 0)  5.67 us
    all_to_all x1, waiting for transfers between devices, on_device(): columns = lax.all_to_all(columns, 'gy', 0, 0)  5.08 us
  transfers between devices with their start and end apart: 5, of which 3 were waited for; matrix products, arithmetic and copies ran while one was open for 3% of the time, Pallas kernels for 31%

profile of v9, /device:TPU:2, one launch (start us, length us, event | category | flops | bytes accessed | tf_op | source)
XLA Modules:
  0.0 99.8 jit_solution(14818016094619465914)
XLA Ops:
  0.0 0.0 copy-start.1
  0.0 1.8 %column_message.1 = f32[16,40,128]{2,1,0:T(8,128)} custom-call(s32[16,16,256]{2,1,0:T(8,128)} %cost_ref.1, f32[16,16]{1,0:T(8,128)} %image_hbm.1), custom_call_target="tpu_custom_call" | custom-call | tf_op jit(solution)/shard_map/column_message/pallas_call | solution.py:272
  1.8 0.0 copy-start.2
  1.8 0.0 copy-start.3
  1.9 9.3 %all-to-all-start = ((f32[16,40,128]{2,1,0:T(8,128)}), f32[16,40,128]{2,1,0:T(8,128)S(1)}, u32[]{:S(2)}, u32[]{:S(2)}) async-start(f32[16,40,128]{2,1,0:T(8,128)} %column_message.1), calls=%async_computation | async-start | bytes 655360 | tf_op jit(solution)/shard_map/all_to_all | solution.py:342
  11.1 1.0 convert_element_type.9
  12.1 0.0 copy-done.1
  12.2 0.1 tile.9
  12.3 0.1 pad.8.clone
  12.3 0.8 maximum_maximum_fusion.value_ref
  13.1 5.1 %all-to-all-done.earlier_ref.refs_0_ = f32[16,40,128]{2,1,0:T(8,128)S(1)} async-done(((f32[16,40,128]{2,1,0:T(8,128)}), f32[16,40,128]{2,1,0:T(8,128)S(1)}, u32[]{:S(2)}, u32[]{:S(2)}) %all-to-all-start) | async-done | bytes 327712 | tf_op jit(solution)/shard_map/all_to_all | solution.py:342
  18.2 13.7 %all-to-all-start.1 = ((f32[16,40,128]{2,1,0:T(8,128)}), f32[16,40,128]{2,1,0:T(8,128)S(1)}, u32[]{:S(2)}, u32[]{:S(2)}) async-start(f32[16,40,128]{2,1,0:T(8,128)} %passed_after.1), calls=%async_computation.1 | async-start | bytes 655360 | tf_op jit(solution)/shard_map/all_to_all | solution.py:344
  31.9 0.0 copy-done.2
  32.0 0.0 copy-done.3
  32.0 0.1 pad_add_fusion
  32.1 0.4 fusion.1.pick
  32.5 0.1 broadcast_in_dim.4.rows_ref
  32.6 10.1 %line_paths.2.earlier_ref = f32[16,2,384]{2,1,0:T(2,128)} custom-call(s32[16,128]{1,0:T(8,128)S(1)} %broadcast_in_dim.4.rows_ref, bf16[32,128,256]{2,1,0:T(8,128)(2,1)S(1)} %fusion.1.pick, f32[16,40,128]{2,1,0:T(8,128)S(1)} %all-to-all-done.earlier_ref.refs_0_), custom_call_target="tpu_custom_call" | custom-call | flops 67108864 | bytes 393216 | tf_op jit(solution)/shard_map/line_paths/pallas_call | solution.py:161
  42.7 0.0 copy-start
  42.7 8.7 %all-to-all-done.1.value_ref = f32[16,40,128]{2,1,0:T(8,128)S(1)} async-done(((f32[16,40,128]{2,1,0:T(8,128)}), f32[16,40,128]{2,1,0:T(8,128)S(1)}, u32[]{:S(2)}, u32[]{:S(2)}) %all-to-all-start.1) | async-done | bytes 327712 | tf_op jit(solution)/shard_map/all_to_all | solution.py:344
  51.4 1.9 %collective-permute-start = (f32[16,40,128]{2,1,0:T(8,128)S(1)}, f32[16,40,128]{2,1,0:T(8,128)S(1)}, u32[]{:S(2)}, u32[]{:S(2)}) collective-permute-start(f32[16,40,128]{2,1,0:T(8,128)S(1)} %after.1.refs_0_), channel_id=1, source_target_pairs={{0,1},{1,0},{2,3},{3,2},{4,5},{5,4},{6,7},{7,6},{8,9},{9,8},{10,11... | collective-permute-start | bytes 983048 | tf_op jit(solution)/shard_map/ppermute | solution.py:347
  53.4 5.7 %all-to-all-start.3 = ((f32[16,2,384]{2,1,0:T(2,128)}), f32[16,2,384]{2,1,0:T(2,128)S(1)}, u32[]{:S(2)}, u32[]{:S(2)}) async-start(f32[16,2,384]{2,1,0:T(2,128)} %line_paths.2.earlier_ref), calls=%async_computation.3 | async-start | bytes 98304 | tf_op jit(solution)/shard_map/all_to_all | solution.py:349
  59.0 0.0 collective-permute-done.refs_1_
  59.0 19.1 %line_paths.3 = f32[16,2,384]{2,1,0:T(2,128)} custom-call(s32[16,128]{1,0:T(8,128)S(1)} %broadcast_in_dim.4.rows_ref, bf16[32,128,256]{2,1,0:T(8,128)(2,1)S(1)} %fusion.1.pick, f32[16,40,128]{2,1,0:T(8,128)S(1)} %after.1.refs_0_, f32[16,40,128]{2,1,0:T(8,128)S(1)} %collective-permute-done.refs_1_), custom_call_target="tpu_custom_call" | custom-call | flops 134217728 | bytes 786432 | tf_op jit(solution)/shard_map/line_paths/pallas_call | solution.py:161
  78.2 0.0 all-to-all-done.3.entry_ref
  78.2 6.1 %all-to-all-start.2 = ((f32[16,2,384]{2,1,0:T(2,128)}), f32[16,2,384]{2,1,0:T(2,128)S(1)}, u32[]{:S(2)}, u32[]{:S(2)}) async-start(f32[16,2,384]{2,1,0:T(2,128)} %line_paths.3), calls=%async_computation.2 | async-start | bytes 98304 | tf_op jit(solution)/shard_map/all_to_all | solution.py:351
  84.3 0.0 copy-done
  84.3 2.2 %block_paths.2 = (f32[16,16,256]{2,1,0:T(8,128)S(1)}, f32[16,16,256]{2,1,0:T(8,128)S(1)}) custom-call(s32[16,128]{1,0:T(8,128)S(1)} %broadcast_in_dim.4.rows_ref, f32[16,2,384]{2,1,0:T(2,128)S(1)} %all-to-all-done.3.entry_ref, s32[16,16,256]{2,1,0:T(8,128)S(1)} %copy-done), custom_call_target="tpu_custom_call" | custom-call | flops 13107200 | bytes 1048576 | tf_op jit(solution)/shard_map/block_paths/pallas_call | solution.py:237
  86.5 10.4 %all-to-all-done.2.entry_ref = f32[16,2,384]{2,1,0:T(2,128)S(1)} async-done(((f32[16,2,384]{2,1,0:T(2,128)}), f32[16,2,384]{2,1,0:T(2,128)S(1)}, u32[]{:S(2)}, u32[]{:S(2)}) %all-to-all-start.2) | async-done | bytes 49184 | tf_op jit(solution)/shard_map/all_to_all | solution.py:351
  96.9 2.9 %block_paths.3 = f32[16,16,256]{2,1,0:T(8,128)} custom-call(s32[16,128]{1,0:T(8,128)S(1)} %broadcast_in_dim.4.rows_ref, f32[16,2,384]{2,1,0:T(2,128)S(1)} %all-to-all-done.2.entry_ref, f32[16,16,256]{2,1,0:T(8,128)S(1)} %get-tuple-element.7.sum_ref, f32[16,16,256]{2,1,0:T(8,128)S(1)} %get-tuple-element.8.line_ref), custom_call_target="tpu_custom_call" | custom-call | flops 13107200 | bytes 1048576 | tf_op jit(solution)/shard_map/block_paths/pallas_call | solution.py:237
  (10 shorter events, 0.1 us)
Async XLA Ops:
  0.0 12.1 %copy-start.1 = (f32[16,16]{1,0:T(8,128)S(1)}, f32[16,16]{1,0:T(8,128)}, u32[]{:S(2)}) copy-start(f32[16,16]{1,0:T(8,128)} %image_hbm.1) | copy-start | bytes 3076
  1.8 30.1 %copy-start.2 = (s32[4]{0:T(128)S(1)}, s32[4]{0:T(128)}, u32[]{:S(2)}) copy-start(s32[4]{0:T(128)} %param.7) | copy-start | bytes 52
  1.8 30.1 %copy-start.3 = (s32[4]{0:T(128)S(1)}, s32[4]{0:T(128)}, u32[]{:S(2)}) copy-start(s32[4]{0:T(128)} %param.6) | copy-start | bytes 52
  1.9 16.4 %all-to-all-start = ((f32[16,40,128]{2,1,0:T(8,128)}), f32[16,40,128]{2,1,0:T(8,128)S(1)}, u32[]{:S(2)}, u32[]{:S(2)}) async-start(f32[16,40,128]{2,1,0:T(8,128)} %column_message.1), calls=%async_computation | async-start | bytes 655360 | tf_op jit(solution)/shard_map/all_to_all | solution.py:342
  18.2 33.2 %all-to-all-start.1 = ((f32[16,40,128]{2,1,0:T(8,128)}), f32[16,40,128]{2,1,0:T(8,128)S(1)}, u32[]{:S(2)}, u32[]{:S(2)}) async-start(f32[16,40,128]{2,1,0:T(8,128)} %passed_after.1), calls=%async_computation.1 | async-start | bytes 655360 | tf_op jit(solution)/shard_map/all_to_all | solution.py:344
  42.7 41.6 %copy-start = (s32[16,16,256]{2,1,0:T(8,128)S(1)}, s32[16,16,256]{2,1,0:T(8,128)}, u32[]{:S(2)}) copy-start(s32[16,16,256]{2,1,0:T(8,128)} %cost_ref.1) | copy-start | bytes 786436
  51.4 7.6 %collective-permute-start = (f32[16,40,128]{2,1,0:T(8,128)S(1)}, f32[16,40,128]{2,1,0:T(8,128)S(1)}, u32[]{:S(2)}, u32[]{:S(2)}) collective-permute-start(f32[16,40,128]{2,1,0:T(8,128)S(1)} %after.1.refs_0_), channel_id=1, source_target_pairs={{0,1},{1,0},{2,3},{3,2},{4,5},{5,4},{6,7},{7,6},{8,9},{9,8},{10,11... | collective-permute-start | bytes 983048 | tf_op jit(solution)/shard_map/ppermute | solution.py:347
  53.4 24.8 %all-to-all-start.3 = ((f32[16,2,384]{2,1,0:T(2,128)}), f32[16,2,384]{2,1,0:T(2,128)S(1)}, u32[]{:S(2)}, u32[]{:S(2)}) async-start(f32[16,2,384]{2,1,0:T(2,128)} %line_paths.2.earlier_ref), calls=%async_computation.3 | async-start | bytes 98304 | tf_op jit(solution)/shard_map/all_to_all | solution.py:349
  78.2 18.7 %all-to-all-start.2 = ((f32[16,2,384]{2,1,0:T(2,128)}), f32[16,2,384]{2,1,0:T(2,128)S(1)}, u32[]{:S(2)}, u32[]{:S(2)}) async-start(f32[16,2,384]{2,1,0:T(2,128)} %line_paths.3), calls=%async_computation.2 | async-start | bytes 98304 | tf_op jit(solution)/shard_map/all_to_all | solution.py:351

commit v10 on v9

--- a/solution.py
+++ b/solution.py
@@ -70,11 +70,11 @@
     to = lax.broadcasted_iota(jnp.int32, (256, 256), 0)
     of = lax.broadcasted_iota(jnp.int32, (256, 256), 1)
     order = (of == (to % 8) * TILES + to // 8).astype(jnp.bfloat16)
-    for g in range(groups):
+    def turn(g, nothing):
         pixels = jnp.concatenate(
             [
-                scr[4 * g : 4 * g + 4].reshape(64, 256),
-                scr[blocks - 4 * g - 4 : blocks - 4 * g].reshape(64, 256),
+                scr[pl.ds(4 * g, 4)].reshape(64, 256),
+                scr[pl.ds(blocks - 4 - 4 * g, 4)].reshape(64, 256),
             ],
             0,
         )
@@ -82,6 +82,9 @@
             order, pixels, (((1,), (1,)), ((), ())), preferred_element_type=jnp.float32
         )
         costs[g] = turned.astype(jnp.bfloat16)
+        return nothing
+
+    lax.fori_loop(0, groups, turn, 0, unroll=4)
 
     mirror = jnp.where(lane < 64, 0, LANES - 1)
 
@@ -148,12 +151,15 @@
     zero = jnp.zeros((8, LANES), jnp.float32)
     lax.fori_loop(0, groups, group, (zero,) * TILES + (jump_at(0, 0),))
     states[...] = jnp.concatenate([starts[:, s, :] for s in range(8)], 0).T
-    for z in range(16):
+    def send(z, nothing):
         block = 2 * z + core if two else z
-        fore, rear = ahead[pl.ds(block // 4, 1), :], back[pl.ds(block // 4, 1), :]
+        fore, rear = ahead[pl.ds(block >> 2, 1), :], back[pl.ds(block >> 2, 1), :]
         start, end = states[pl.ds(block, 1), :], states[pl.ds(64 + blocks - 1 - block, 1), :]
         out_ref[z, 0:1, :] = jnp.concatenate([start, fore], 1)
         out_ref[z, 1:2, :] = jnp.concatenate([end, rear], 1)
+        return nothing
+
+    lax.fori_loop(0, 16, send, 0, unroll=4)
 
 
 def path_states(blocks, first, two, rows, pick, *sources):

time: 100 us -> 101 us (1.010)
  transfers between devices with their start and end apart: 5 -> 5, of which waited for: 3 -> 3; matrix products, arithmetic and copies ran while one was open for 3% -> 3% of each run, Pallas kernels for 31% -> 32%
where the time goes in v10:
time: 101 us; the launch traced here: 100 us
  Pallas kernels  36.7 us (36%)
  starting transfers between devices  36.6 us (36%)
  waiting for transfers between devices  24.2 us (24%)
  other arithmetic  2.31 us (2%)
    pallas_call x2, Pallas kernels, path_states(): pl.pallas_call(partial(path_kernel, blocks, first, two), out_shape=jax.Sh...  29.8 us
    all_to_all x1, starting transfers between devices, on_device(): lines = lax.all_to_all(lines, 'gx', 0, 0, axis_index_groups=chips)  13.7 us
    all_to_all x1, waiting for transfers between devices, on_device(): entry_x = lax.all_to_all(entry_x, 'gx', 0, 0, axis_index_groups=chips)  10.4 us
    all_to_all x1, starting transfers between devices, on_device(): columns = lax.all_to_all(columns, 'gy', 0, 0)  9.27 us
    all_to_all x1, waiting for transfers between devices, on_device(): lines = lax.all_to_all(lines, 'gx', 0, 0, axis_index_groups=chips)  8.67 us
    all_to_all x1, starting transfers between devices, on_device(): entry_x = lax.all_to_all(entry_x, 'gx', 0, 0, axis_index_groups=chips)  6.09 us
    all_to_all x1, starting transfers between devices, on_device(): entry_y = lax.all_to_all(entry_y, 'gy', 0, 0)  5.67 us
    all_to_all x1, waiting for transfers between devices, on_device(): columns = lax.all_to_all(columns, 'gy', 0, 0)  5.08 us
  transfers between devices with their start and end apart: 5, of which 3 were waited for; matrix products, arithmetic and copies ran while one was open for 3% of the time, Pallas kernels for 32%

profile of v10, /device:TPU:2, one launch (start us, length us, event | category | flops | bytes accessed | tf_op | source)
XLA Modules:
  0.0 100.3 jit_solution(13588428107313726215)
XLA Ops:
  0.0 0.0 copy-start.1
  0.0 1.8 %column_message.1 = f32[16,40,128]{2,1,0:T(8,128)} custom-call(s32[16,16,256]{2,1,0:T(8,128)} %cost_ref.1, f32[16,16]{1,0:T(8,128)} %image_hbm.1), custom_call_target="tpu_custom_call" | custom-call | tf_op jit(solution)/shard_map/column_message/pallas_call | solution.py:278
  1.8 0.0 copy-start.2
  1.8 0.0 copy-start.3
  1.9 9.3 %all-to-all-start = ((f32[16,40,128]{2,1,0:T(8,128)}), f32[16,40,128]{2,1,0:T(8,128)S(1)}, u32[]{:S(2)}, u32[]{:S(2)}) async-start(f32[16,40,128]{2,1,0:T(8,128)} %column_message.1), calls=%async_computation | async-start | bytes 655360 | tf_op jit(solution)/shard_map/all_to_all | solution.py:348
  11.1 1.0 convert_element_type.9
  12.1 0.0 copy-done.1
  12.2 0.1 tile.9
  12.3 0.1 pad.8.clone
  12.3 0.8 maximum_maximum_fusion.value_ref
  13.1 5.1 %all-to-all-done.earlier_ref.refs_0_ = f32[16,40,128]{2,1,0:T(8,128)S(1)} async-done(((f32[16,40,128]{2,1,0:T(8,128)}), f32[16,40,128]{2,1,0:T(8,128)S(1)}, u32[]{:S(2)}, u32[]{:S(2)}) %all-to-all-start) | async-done | bytes 327712 | tf_op jit(solution)/shard_map/all_to_all | solution.py:348
  18.2 13.7 %all-to-all-start.1 = ((f32[16,40,128]{2,1,0:T(8,128)}), f32[16,40,128]{2,1,0:T(8,128)S(1)}, u32[]{:S(2)}, u32[]{:S(2)}) async-start(f32[16,40,128]{2,1,0:T(8,128)} %passed_after.1), calls=%async_computation.1 | async-start | bytes 655360 | tf_op jit(solution)/shard_map/all_to_all | solution.py:350
  31.9 0.0 copy-done.2
  32.0 0.0 copy-done.3
  32.0 0.1 pad_add_fusion
  32.1 0.4 fusion.1.pick
  32.5 0.1 broadcast_in_dim.4.rows_ref
  32.6 10.1 %line_paths.2.earlier_ref = f32[16,2,384]{2,1,0:T(2,128)} custom-call(s32[16,128]{1,0:T(8,128)S(1)} %broadcast_in_dim.4.rows_ref, bf16[32,128,256]{2,1,0:T(8,128)(2,1)S(1)} %fusion.1.pick, f32[16,40,128]{2,1,0:T(8,128)S(1)} %all-to-all-done.earlier_ref.refs_0_), custom_call_target="tpu_custom_call" | custom-call | flops 67108864 | bytes 393216 | tf_op jit(solution)/shard_map/line_paths/pallas_call | solution.py:167
  42.7 0.0 copy-start
  42.7 8.7 %all-to-all-done.1.value_ref = f32[16,40,128]{2,1,0:T(8,128)S(1)} async-done(((f32[16,40,128]{2,1,0:T(8,128)}), f32[16,40,128]{2,1,0:T(8,128)S(1)}, u32[]{:S(2)}, u32[]{:S(2)}) %all-to-all-start.1) | async-done | bytes 327712 | tf_op jit(solution)/shard_map/all_to_all | solution.py:350
  51.4 1.9 %collective-permute-start = (f32[16,40,128]{2,1,0:T(8,128)S(1)}, f32[16,40,128]{2,1,0:T(8,128)S(1)}, u32[]{:S(2)}, u32[]{:S(2)}) collective-permute-start(f32[16,40,128]{2,1,0:T(8,128)S(1)} %after.1.refs_0_), channel_id=1, source_target_pairs={{0,1},{1,0},{2,3},{3,2},{4,5},{5,4},{6,7},{7,6},{8,9},{9,8},{10,11... | collective-permute-start | bytes 983048 | tf_op jit(solution)/shard_map/ppermute | solution.py:353
  53.4 5.7 %all-to-all-start.3 = ((f32[16,2,384]{2,1,0:T(2,128)}), f32[16,2,384]{2,1,0:T(2,128)S(1)}, u32[]{:S(2)}, u32[]{:S(2)}) async-start(f32[16,2,384]{2,1,0:T(2,128)} %line_paths.2.earlier_ref), calls=%async_computation.3 | async-start | bytes 98304 | tf_op jit(solution)/shard_map/all_to_all | solution.py:355
  59.0 0.0 collective-permute-done.refs_1_
  59.0 19.7 %line_paths.3 = f32[16,2,384]{2,1,0:T(2,128)} custom-call(s32[16,128]{1,0:T(8,128)S(1)} %broadcast_in_dim.4.rows_ref, bf16[32,128,256]{2,1,0:T(8,128)(2,1)S(1)} %fusion.1.pick, f32[16,40,128]{2,1,0:T(8,128)S(1)} %after.1.refs_0_, f32[16,40,128]{2,1,0:T(8,128)S(1)} %collective-permute-done.refs_1_), custom_call_target="tpu_custom_call" | custom-call | flops 134217728 | bytes 786432 | tf_op jit(solution)/shard_map/line_paths/pallas_call | solution.py:167
  78.7 0.0 all-to-all-done.3.entry_ref
  78.7 6.1 %all-to-all-start.2 = ((f32[16,2,384]{2,1,0:T(2,128)}), f32[16,2,384]{2,1,0:T(2,128)S(1)}, u32[]{:S(2)}, u32[]{:S(2)}) async-start(f32[16,2,384]{2,1,0:T(2,128)} %line_paths.3), calls=%async_computation.2 | async-start | bytes 98304 | tf_op jit(solution)/shard_map/all_to_all | solution.py:357
  84.8 0.0 copy-done
  84.8 2.2 %block_paths.2 = (f32[16,16,256]{2,1,0:T(8,128)S(1)}, f32[16,16,256]{2,1,0:T(8,128)S(1)}) custom-call(s32[16,128]{1,0:T(8,128)S(1)} %broadcast_in_dim.4.rows_ref, f32[16,2,384]{2,1,0:T(2,128)S(1)} %all-to-all-done.3.entry_ref, s32[16,16,256]{2,1,0:T(8,128)S(1)} %copy-done), custom_call_target="tpu_custom_call" | custom-call | flops 13107200 | bytes 1048576 | tf_op jit(solution)/shard_map/block_paths/pallas_call | solution.py:243
  87.0 10.4 %all-to-all-done.2.entry_ref = f32[16,2,384]{2,1,0:T(2,128)S(1)} async-done(((f32[16,2,384]{2,1,0:T(2,128)}), f32[16,2,384]{2,1,0:T(2,128)S(1)}, u32[]{:S(2)}, u32[]{:S(2)}) %all-to-all-start.2) | async-done | bytes 49184 | tf_op jit(solution)/shard_map/all_to_all | solution.py:357
  97.5 2.9 %block_paths.3 = f32[16,16,256]{2,1,0:T(8,128)} custom-call(s32[16,128]{1,0:T(8,128)S(1)} %broadcast_in_dim.4.rows_ref, f32[16,2,384]{2,1,0:T(2,128)S(1)} %all-to-all-done.2.entry_ref, f32[16,16,256]{2,1,0:T(8,128)S(1)} %get-tuple-element.7.sum_ref, f32[16,16,256]{2,1,0:T(8,128)S(1)} %get-tuple-element.8.line_ref), custom_call_target="tpu_custom_call" | custom-call | flops 13107200 | bytes 1048576 | tf_op jit(solution)/shard_map/block_paths/pallas_call | solution.py:243
  (10 shorter events, 0.1 us)
Async XLA Ops:
  0.0 12.1 %copy-start.1 = (f32[16,16]{1,0:T(8,128)S(1)}, f32[16,16]{1,0:T(8,128)}, u32[]{:S(2)}) copy-start(f32[16,16]{1,0:T(8,128)} %image_hbm.1) | copy-start | bytes 3076
  1.8 30.1 %copy-start.2 = (s32[4]{0:T(128)S(1)}, s32[4]{0:T(128)}, u32[]{:S(2)}) copy-start(s32[4]{0:T(128)} %param.7) | copy-start | bytes 52
  1.8 30.1 %copy-start.3 = (s32[4]{0:T(128)S(1)}, s32[4]{0:T(128)}, u32[]{:S(2)}) copy-start(s32[4]{0:T(128)} %param.6) | copy-start | bytes 52
  1.9 16.4 %all-to-all-start = ((f32[16,40,128]{2,1,0:T(8,128)}), f32[16,40,128]{2,1,0:T(8,128)S(1)}, u32[]{:S(2)}, u32[]{:S(2)}) async-start(f32[16,40,128]{2,1,0:T(8,128)} %column_message.1), calls=%async_computation | async-start | bytes 655360 | tf_op jit(solution)/shard_map/all_to_all | solution.py:348
  18.2 33.2 %all-to-all-start.1 = ((f32[16,40,128]{2,1,0:T(8,128)}), f32[16,40,128]{2,1,0:T(8,128)S(1)}, u32[]{:S(2)}, u32[]{:S(2)}) async-start(f32[16,40,128]{2,1,0:T(8,128)} %passed_after.1), calls=%async_computation.1 | async-start | bytes 655360 | tf_op jit(solution)/shard_map/all_to_all | solution.py:350
  42.7 42.1 %copy-start = (s32[16,16,256]{2,1,0:T(8,128)S(1)}, s32[16,16,256]{2,1,0:T(8,128)}, u32[]{:S(2)}) copy-start(s32[16,16,256]{2,1,0:T(8,128)} %cost_ref.1) | copy-start | bytes 786436
  51.4 7.6 %collective-permute-start = (f32[16,40,128]{2,1,0:T(8,128)S(1)}, f32[16,40,128]{2,1,0:T(8,128)S(1)}, u32[]{:S(2)}, u32[]{:S(2)}) collective-permute-start(f32[16,40,128]{2,1,0:T(8,128)S(1)} %after.1.refs_0_), channel_id=1, source_target_pairs={{0,1},{1,0},{2,3},{3,2},{4,5},{5,4},{6,7},{7,6},{8,9},{9,8},{10,11... | collective-permute-start | bytes 983048 | tf_op jit(solution)/shard_map/ppermute | solution.py:353
  53.4 25.4 %all-to-all-start.3 = ((f32[16,2,384]{2,1,0:T(2,128)}), f32[16,2,384]{2,1,0:T(2,128)S(1)}, u32[]{:S(2)}, u32[]{:S(2)}) async-start(f32[16,2,384]{2,1,0:T(2,128)} %line_paths.2.earlier_ref), calls=%async_computation.3 | async-start | bytes 98304 | tf_op jit(solution)/shard_map/all_to_all | solution.py:355
  78.7 18.7 %all-to-all-start.2 = ((f32[16,2,384]{2,1,0:T(2,128)}), f32[16,2,384]{2,1,0:T(2,128)S(1)}, u32[]{:S(2)}, u32[]{:S(2)}) async-start(f32[16,2,384]{2,1,0:T(2,128)} %line_paths.3), calls=%async_computation.2 | async-start | bytes 98304 | tf_op jit(solution)/shard_map/all_to_all | solution.py:357
